TPU v7x, 32 devices: a whole 2x2x4 slice. The times are simulated.
32 devices in a mesh: prow: 4 (over y, x), pcol: 8 (over z, core).
Axes of the slice: x: 2, y: 2, z: 4, core: 2. Of those that a mesh axis runs over, the one named last changes fastest.
Arguments:
- adjoint_trail: float32 [8, 4, 256, 4, 8, 256], P(None, 'prow', None, None, 'pcol'), as said below
- factor_low: float32 [8, 4, 8, 32, 4, 256], P(None, 'prow', 'pcol'), may hold values from -0.0625 to 0.0625
- adjoint_low: float32 [8, 4, 8, 32, 4, 256], P(None, 'prow', 'pcol'), may hold values from -6 to 6
- factor_top: float32 [10, 256, 256], P(None, 'pcol'), as said below
- adjoint_top: float32 [10, 256, 256], P(None, 'pcol'), may hold values from -6 to 6
- diag_inverse: float32 [4, 256, 256], P(None, 'pcol'), as said below
Outputs:
- grad_low: float32 [8, 4, 8, 32, 4, 256], P(None, 'prow', 'pcol')
- grad_top: float32 [10, 256, 256], P(None, 'pcol')
Inputs may be any that keep to these rules, and one draw needn't show every extreme that they name: adjoint_trail reshaped row-major to 8192 x 8192 is symmetric. The diagonal blocks factor_top[j (j + 1) / 2 + j] are lower triangular with a positive diagonal. diag_inverse[j] is the inverse of factor_top[j (j + 1) / 2 + j].
All inputs are finite; a program needn't handle non-finite values.
Results may differ from a plain program's by a relative error of at most 0.00024.
Values sent between devices are 32-bit elements; how exact they have to be, the bound alone decides.
No kernel may reach another device: no remote copies, remote signals or barrier semaphores. Data moves between devices by JAX's collectives and lax.ppermute only.
A program may use at most 128 MiB of HBM per device.

v0:
```python
import jax
import jax.numpy as jnp
from jax import lax
from jax.sharding import PartitionSpec as P

NB = 256
K = 4


HIGHEST = lax.Precision.HIGHEST


def from_root(array, axis, root):
    mine = lax.axis_index(axis) == root
    return lax.psum(jnp.where(mine, array, jnp.zeros_like(array)), axis)


def matmul(left, right):
    return jnp.dot(left, right, precision=HIGHEST, preferred_element_type=jnp.float32)


def inner_product(left, right):
    return lax.dot_general(
        left, right, (((0,), (0,)), ((), ())), precision=HIGHEST, preferred_element_type=jnp.float32
    )


def block_slot(row_block, col_block):
    return row_block * (row_block + 1) // 2 + col_block


def half_lower(square):
    size = square.shape[0]
    row_ids = lax.broadcasted_iota(jnp.int32, (size, size), 0)
    col_ids = lax.broadcasted_iota(jnp.int32, (size, size), 1)
    return jnp.where(row_ids > col_ids, square, jnp.where(row_ids == col_ids, 0.5 * square, 0.0))


def diagonal_adjoint(diagonal, inverse, lower_adj):
    inner = half_lower(inner_product(jnp.tril(diagonal), lower_adj))
    spread = inner_product(inverse, matmul(inner, inverse))
    return 0.5 * (spread + spread.T)


def rows_one(piece):
    return lax.all_gather(piece, "pcol", axis=1, tiled=True)


def owner_one(piece, root):
    return from_root(piece, "prow", root)


def reduce_one(term, count):
    return lax.psum_scatter(
        term(jnp.int32(0), lax.axis_size("pcol") * count), "pcol", scatter_dimension=0, tiled=True
    )


def trailing_product(trail, panels, gather_rows, send_owner, reduce_rows):
    prow_count = lax.axis_size("prow")
    pcol_count = lax.axis_size("pcol")
    cycles, sub_rows, width = panels.shape
    block = sub_rows * pcol_count
    gathered = gather_rows(panels[:, None]).reshape(cycles, block, width)
    column = lax.axis_index("pcol")
    col_cycles = trail.shape[3]
    owned = []
    for cycle in range(col_cycles):
        global_block = cycle * pcol_count + column
        share = lax.dynamic_index_in_dim(gathered, global_block // prow_count, 0, keepdims=False)
        owned.append(send_owner(share, global_block % prow_count))
    stacked = jnp.stack(owned)
    view = trail.reshape(cycles, pcol_count, sub_rows, col_cycles, block)
    unit = cycles * sub_rows

    def term(start, count):
        product = jnp.einsum(
            "iaekb,kbn->aien", view, stacked, precision=HIGHEST, preferred_element_type=jnp.float32
        )
        return product.reshape(count, width)

    return reduce_rows(term, unit).reshape(cycles, sub_rows, width)


def per_device(adjoint_trail, factor_low, adjoint_low, factor_top, adjoint_top, diag_inverse):
    cycles = factor_low.shape[0]
    sub_rows = factor_low.shape[3]
    local_rows = cycles * sub_rows
    low_factor = factor_low.reshape(cycles, sub_rows, K * NB)
    low_adjoint = adjoint_low.reshape(local_rows, K, NB)
    columns = low_factor.reshape(local_rows, K, NB)
    top_factor, top_adjoint, inverses = (
        lax.all_gather(factor_top, "pcol", axis=1, tiled=True),
        lax.all_gather(adjoint_top, "pcol", axis=1, tiled=True),
        lax.all_gather(diag_inverse, "pcol", axis=1, tiled=True),
    )
    lower_grads = [None] * K
    diag_grads = [None] * K
    upper_grads = {}
    grams = {}

    def lower_step(panel):
        single = low_factor[:, :, panel * NB : (panel + 1) * NB]
        image = trailing_product(adjoint_trail, single, rows_one, owner_one, reduce_one).reshape(
            local_rows, NB
        )
        residual = low_adjoint[:, panel] - 2.0 * image
        for later in range(panel + 1, K):
            residual = residual - matmul(lower_grads[later], top_factor[block_slot(later, panel)])
        lower_grads[panel] = matmul(residual, inverses[panel])

    def top_step(panel):
        for row_block in range(panel + 1, K):
            top_residual = top_adjoint[block_slot(row_block, panel)] - grams[row_block, panel]
            top_residual = top_residual - 2.0 * matmul(
                diag_grads[row_block], top_factor[block_slot(row_block, panel)]
            )
            for middle in range(panel + 1, row_block):
                top_residual = top_residual - matmul(
                    upper_grads[middle, row_block], top_factor[block_slot(middle, panel)]
                )
            for beyond in range(row_block + 1, K):
                top_residual = top_residual - inner_product(
                    upper_grads[row_block, beyond], top_factor[block_slot(beyond, panel)]
                )
            upper_grads[panel, row_block] = matmul(top_residual, inverses[panel])
        lower_adj = top_adjoint[block_slot(panel, panel)] - grams[panel, panel]
        for row_block in range(panel + 1, K):
            lower_adj = lower_adj - inner_product(
                upper_grads[panel, row_block], top_factor[block_slot(row_block, panel)]
            )
        diag_grads[panel] = diagonal_adjoint(
            top_factor[block_slot(panel, panel)], inverses[panel], jnp.tril(lower_adj)
        )

    for panel in reversed(range(K)):
        lower_step(panel)
        local_gram = jnp.stack(
            [inner_product(lower_grads[panel], columns[:, earlier]) for earlier in range(panel + 1)]
        )
        summed = lax.psum(local_gram, ("prow", "pcol"))
        for earlier in range(panel + 1):
            grams[panel, earlier] = summed[earlier]
        top_step(panel)
    grad_low = jnp.stack(lower_grads, 1).reshape(factor_low.shape)
    blocks = []
    for row_block in range(K):
        for col_block in range(row_block + 1):
            if row_block == col_block:
                blocks.append(diag_grads[col_block])
            else:
                blocks.append(upper_grads[col_block, row_block])
    full_top = jnp.stack(blocks)
    share_rows = factor_top.shape[1]
    grad_top = lax.dynamic_slice_in_dim(
        full_top, lax.axis_index("pcol") * share_rows, share_rows, 1
    )
    return (grad_low, grad_top)


def solution(mesh):
    in_specs = (
        P(None, "prow", None, None, "pcol", None),
        P(None, "prow", "pcol", None, None, None),
        P(None, "prow", "pcol", None, None, None),
        P(None, "pcol", None),
        P(None, "pcol", None),
        P(None, "pcol", None),
    )
    out_specs = (P(None, "prow", "pcol", None, None, None), P(None, "pcol", None))
    return jax.shard_map(
        per_device, mesh=mesh, in_specs=in_specs, out_specs=out_specs, check_vma=False
    )
```

profile of v0, /device:TPU:0, one launch (start us, length us, event | category | flops | bytes accessed | tf_op | source)
XLA Modules:
  0.0 678.1 jit_solution(14019835247173433526)
XLA Ops:
  7.2 1.8 reshape.122
  12.2 29.8 %all-gather.24.cloned.1.call-done = f32[8,256,256]{2,1,0:T(8,128)} async-done(((f32[8,32,256]{2,1,0:T(8,128)}), f32[8,256,256]{2,1,0:T(8,128)}) %all-gather.24.cloned.1.call-update) | async-done | bytes 2097168 | tf_op jit(solution)/shard_map/all_gather | solution.py:46
  42.0 2.2 dynamic-slice_select_fusion
  44.2 28.1 %all-gather.22.cloned.1.call-done = f32[8,256,256]{2,1,0:T(8,128)} async-done(((f32[8,32,256]{2,1,0:T(8,128)}), f32[8,256,256]{2,1,0:T(8,128)}) %all-gather.22.cloned.1.call-update) | async-done | bytes 2097168 | tf_op jit(solution)/shard_map/all_gather | solution.py:46
  72.2 2.2 dynamic-slice_select_fusion.1
  74.5 28.0 %all-gather.20.cloned.1.call-done = f32[8,256,256]{2,1,0:T(8,128)} async-done(((f32[8,32,256]{2,1,0:T(8,128)}), f32[8,256,256]{2,1,0:T(8,128)}) %all-gather.20.cloned.1.call-update) | async-done | bytes 2097168 | tf_op jit(solution)/shard_map/all_gather | solution.py:46
  102.5 2.2 dynamic-slice_select_fusion.2
  104.7 28.4 %all-gather.18.cloned.1.call-done = f32[8,256,256]{2,1,0:T(8,128)} async-done(((f32[8,32,256]{2,1,0:T(8,128)}), f32[8,256,256]{2,1,0:T(8,128)}) %all-gather.18.cloned.1.call-update) | async-done | bytes 2097168 | tf_op jit(solution)/shard_map/all_gather | solution.py:46
  133.1 2.2 dynamic-slice_select_fusion.3
  136.0 8.9 %copy.33 = f32[8,1,256,4,1,256]{5,3,4,2,1,0:T(4,128)} copy(f32[8,1,256,4,1,256]{5,4,3,2,1,0:T(1,128)} %param.6) | data formatting | bytes 16777216
  144.9 103.6 %all-reduce.7.cloned.1.call-done = (f32[1,256,256]{2,1,0:T(8,128)}, f32[1,256,256]{2,1,0:T(8,128)}, f32[1,256,256]{2,1,0:T(8,128)}, f32[1,256,256]{2,1,0:T(8,128...) async-done(((f32[1,256,256]{2,1,0:T(8,128)}, ...) | async-done | bytes 4194320 | tf_op jit(solution)/shard_map/psum | solution.py:15
  248.5 11.0 %fusion.17 = f32[8,8,32,256]{3,2,0,1:T(8,128)S(1)} fusion(f32[8,8,32,4,256]{4,3,2,1,0:T(4,128)} %bitcast.335, f32[1,256,256]{2,1,0:T(8,128)} %get-tuple-element.6, f32[1,256,256]{2,1,0:T(8,128)} %get-tuple-element.7, f32[1,256,256]{2,1,0:T(8,128)} %get-tuple-element.8, f32[1,256,256]{2,1,0:T(8,128)} %get-tuple-element.9), kind=kOutput, calls=%fused_computation.11 | convolution fusion | flops 6443237376 | bytes 11534336 | tf_op jit(solution)/shard_map/iaekb,kbn->aien/dot_general | solution.py:77
  262.2 10.9 %fusion.14 = f32[8,8,32,256]{3,2,0,1:T(8,128)S(1)} fusion(f32[8,8,32,4,256]{4,3,2,1,0:T(4,128)} %bitcast.336, f32[1,256,256]{2,1,0:T(8,128)S(1)} %copy-done.45, f32[1,256,256]{2,1,0:T(8,128)S(1)} %copy-done.46, f32[1,256,256]{2,1,0:T(8,128)S(1)} %copy-done.47, f32[1,256,256]{2,1,0:T(8,128)S(1)} %copy-done.48), kind=kOutput, calls=%fused_computation.10 | convolution fusion | flops 6443237376 | bytes 11534336 | tf_op jit(solution)/shard_map/iaekb,kbn->aien/dot_general | solution.py:77
  274.7 10.8 %fusion.11 = f32[8,8,32,256]{3,2,0,1:T(8,128)S(1)} fusion(f32[8,8,32,4,256]{4,3,2,1,0:T(4,128)} %bitcast.337, f32[1,256,256]{2,1,0:T(8,128)S(1)} %copy-done.41, f32[1,256,256]{2,1,0:T(8,128)S(1)} %copy-done.42, f32[1,256,256]{2,1,0:T(8,128)S(1)} %copy-done.43, f32[1,256,256]{2,1,0:T(8,128)S(1)} %copy-done.44), kind=kOutput, calls=%fused_computation.9 | convolution fusion | flops 6443237376 | bytes 11534336 | tf_op jit(solution)/shard_map/iaekb,kbn->aien/dot_general | solution.py:77
  287.2 10.9 %fusion.8 = f32[8,8,32,256]{3,2,0,1:T(8,128)S(1)} fusion(f32[8,8,32,4,256]{4,3,2,1,0:T(4,128)} %bitcast.338, f32[1,256,256]{2,1,0:T(8,128)S(1)} %copy-done.37, f32[1,256,256]{2,1,0:T(8,128)S(1)} %copy-done.38, f32[1,256,256]{2,1,0:T(8,128)S(1)} %copy-done.39, f32[1,256,256]{2,1,0:T(8,128)S(1)} %copy-done.40), kind=kOutput, calls=%fused_computation.8 | convolution fusion | flops 6443237376 | bytes 11534336 | tf_op jit(solution)/shard_map/iaekb,kbn->aien/dot_general | solution.py:77
  302.6 7.5 %reduce-scatter.11.cloned.1.call-done = f32[256,256]{1,0:T(8,128)} async-done(((f32[2048,256]{1,0:T(8,128)}), f32[256,256]{1,0:T(8,128)}) %reduce-scatter.11.cloned.1.call-update) | async-done | bytes 262160 | tf_op jit(solution)/shard_map/reduce_scatter | solution.py:54
  311.5 32.7 %all-gather.14.cloned.1.call-done = f32[10,256,256]{2,1,0:T(8,128)} async-done(((f32[10,32,256]{2,1,0:T(8,128)}), f32[10,256,256]{2,1,0:T(8,128)}) %all-gather.14.cloned.1.call-update) | async-done | bytes 2621456 | tf_op jit(solution)/shard_map/all_gather | solution.py:93
  344.3 37.3 %reduce-scatter.9.cloned.1.call-done = f32[256,256]{1,0:T(8,128)} async-done(((f32[2048,256]{1,0:T(8,128)}), f32[256,256]{1,0:T(8,128)}) %reduce-scatter.9.cloned.1.call-update) | async-done | bytes 262160 | tf_op jit(solution)/shard_map/reduce_scatter | solution.py:54
  384.4 33.7 %reduce-scatter.7.cloned.1.call-done = f32[256,256]{1,0:T(8,128)} async-done(((f32[2048,256]{1,0:T(8,128)}), f32[256,256]{1,0:T(8,128)}) %reduce-scatter.7.cloned.1.call-update) | async-done | bytes 262160 | tf_op jit(solution)/shard_map/reduce_scatter | solution.py:54
  434.7 20.5 %reduce-scatter.5.cloned.1.call-done = f32[256,256]{1,0:T(8,128)} async-done(((f32[2048,256]{1,0:T(8,128)}), f32[256,256]{1,0:T(8,128)}) %reduce-scatter.5.cloned.1.call-update) | async-done | bytes 262160 | tf_op jit(solution)/shard_map/reduce_scatter | solution.py:54
  465.1 2.0 pad_maximum_fusion
  467.1 22.1 %all-gather.16.cloned.1.call-done = f32[10,256,256]{2,1,0:T(8,128)} async-done(((f32[10,32,256]{2,1,0:T(8,128)}), f32[10,256,256]{2,1,0:T(8,128)}) %all-gather.16.cloned.1.call-update) | async-done | bytes 2621456 | tf_op jit(solution)/shard_map/all_gather | solution.py:94
  489.3 142.7 %all-reduce.5.cloned.1.call-done = (f32[2,256,256]{2,1,0:T(8,128)}, f32[3,256,256]{2,1,0:T(8,128)}, f32[4,256,256]{2,1,0:T(8,128)}, f32[1,256,256]{2,1,0:T(8,128)}) async-done(((f32[2,256,256]{2,1,0:T(8,128)}, f32[3,256,256]{2,1,0:T(8,128)}, f32[4,256,256]{2,1,0:T(8,128)}, f32[1,256,256]{2,1,0:T(8,128)}), (f32[2,256,256]{2,1,0:T(8,128)}, f32[3,256,256]{2,1,0:T(8,128)}, f32[4,256,256]{2,1,0:T(8,128)}, ...) | async-done | bytes 2621456 | tf_op jit(solution)/shard_map/psum | solution.py:141
  652.9 1.8 copy.23
  (212 shorter events, 81.3 us)
Async XLA Ops:
  7.2 34.8 %all-gather.24.cloned.1.call-start = ((), (), s32[]{:S(2)}) async-start(), calls=%async_computation.14 | async-start | bytes 2359296 | tf_op jit(solution)/shard_map/all_gather | solution.py:46
  10.0 62.2 %all-gather.22.cloned.1.call-start = ((), (), s32[]{:S(2)}) async-start(), calls=%async_computation.13 | async-start | bytes 2359296 | tf_op jit(solution)/shard_map/all_gather | solution.py:46
  10.8 91.7 %all-gather.20.cloned.1.call-start = ((), (), s32[]{:S(2)}) async-start(), calls=%async_computation.12 | async-start | bytes 2359296 | tf_op jit(solution)/shard_map/all_gather | solution.py:46
  11.5 121.6 %all-gather.18.cloned.1.call-start = ((), (), s32[]{:S(2)}) async-start(), calls=%async_computation.11 | async-start | bytes 2359296 | tf_op jit(solution)/shard_map/all_gather | solution.py:46
  12.1 236.4 %all-reduce.7.cloned.1.call-start = ((), (), s32[]{:S(2)}) async-start(), calls=%async_computation.16 | async-start | bytes 8388608 | tf_op jit(solution)/shard_map/psum | solution.py:15
  135.4 167.2 %all-gather.12.cloned.1.call-start = ((), (), s32[]{:S(2)}) async-start(), calls=%async_computation.8 | async-start | bytes 1179648 | tf_op jit(solution)/shard_map/all_gather | solution.py:95
  135.9 174.2 %reduce-scatter.11.cloned.1.call-start = ((), (), s32[]{:S(2)}) async-start(), calls=%async_computation.7 | async-start | bytes 2359296 | tf_op jit(solution)/shard_map/reduce_scatter | solution.py:54
  261.2 83.1 %all-gather.14.cloned.1.call-start = ((), (), s32[]{:S(2)}) async-start(), calls=%async_computation.9 | async-start | bytes 2949120 | tf_op jit(solution)/shard_map/all_gather | solution.py:93
  261.9 119.7 %reduce-scatter.9.cloned.1.call-start = ((), (), s32[]{:S(2)}) async-start(), calls=%async_computation.6 | async-start | bytes 2359296 | tf_op jit(solution)/shard_map/reduce_scatter | solution.py:54
  274.6 143.5 %reduce-scatter.7.cloned.1.call-start = ((), (), s32[]{:S(2)}) async-start(), calls=%async_computation.5 | async-start | bytes 2359296 | tf_op jit(solution)/shard_map/reduce_scatter | solution.py:54
  287.1 168.1 %reduce-scatter.5.cloned.1.call-start = ((), (), s32[]{:S(2)}) async-start(), calls=%async_computation.4 | async-start | bytes 2359296 | tf_op jit(solution)/shard_map/reduce_scatter | solution.py:54
  299.6 189.7 %all-gather.16.cloned.1.call-start = ((), (), s32[]{:S(2)}) async-start(), calls=%async_computation.10 | async-start | bytes 2949120 | tf_op jit(solution)/shard_map/all_gather | solution.py:94
  300.2 331.8 %all-reduce.5.cloned.1.call-start = ((), (), s32[]{:S(2)}) async-start(), calls=%async_computation.15 | async-start | bytes 5242880 | tf_op jit(solution)/shard_map/psum | solution.py:141
  300.9 10.7 %copy-start.12 = (f32[8,1,1,32,4,256]{5,3,0,4,2,1:T(8,128)}, f32[8,1,1,32,4,256]{5,3,0,4,2,1:T(8,128)S(1)}, u32[]{:S(2)}) copy-start(f32[8,1,1,32,4,256]{5,3,0,4,2,1:T(8,128)S(1)} %copy.8) | copy-start | bytes 3145732
  344.3 75.4 %copy-start = (f32[10,256,256]{2,1,0:T(8,128)S(1)}, f32[10,256,256]{2,1,0:T(8,128)}, u32[]{:S(2)}) copy-start(f32[10,256,256]{2,1,0:T(8,128)} %all-gather.14.cloned.1.call-done) | copy-start | bytes 7864324
  418.1 7.3 %copy-start.15 = (f32[256,1,256]{2,1,0:T(1,128)S(1)}, f32[256,1,256]{2,1,0:T(1,128)}, u32[]{:S(2)}) copy-start(f32[256,1,256]{2,1,0:T(1,128)} %get-tuple-element.40) | copy-start | bytes 786436
  419.7 7.1 %copy-start.7 = (f32[256,1,256]{2,1,0:T(1,128)S(1)}, f32[256,1,256]{2,1,0:T(1,128)}, u32[]{:S(2)}) copy-start(f32[256,1,256]{2,1,0:T(1,128)} %get-tuple-element.41) | copy-start | bytes 786436
  420.1 8.0 %copy-start.24 = (f32[256,1,256]{2,1,0:T(1,128)S(1)}, f32[256,1,256]{2,1,0:T(1,128)}, u32[]{:S(2)}) copy-start(f32[256,1,256]{2,1,0:T(1,128)} %get-tuple-element.39) | copy-start | bytes 786436
  425.4 8.0 %copy-start.29 = (f32[256,1,256]{2,1,0:T(1,128)S(1)}, f32[256,1,256]{2,1,0:T(1,128)}, u32[]{:S(2)}) copy-start(f32[256,1,256]{2,1,0:T(1,128)} %get-tuple-element.38) | copy-start | bytes 786436
  455.2 5.7 copy-start.26
  455.2 5.7 copy-start.27
  455.2 5.7 copy-start.28
  456.7 5.1 copy-start.30
  654.7 5.4 copy-start.10
  (38 other events, 111.3 us)
Sparse Core Ops, SparseCore 0:
  10.2 31.7 all-gather.23
  43.6 28.5 all-gather.21
  73.9 28.5 all-gather.19
  104.5 28.5 all-gather.17
  139.3 109.1 all-reduce.6
  250.1 22.0 all-gather.11
  274.6 35.4 reduce-scatter.10
  311.8 32.4 all-gather.13
  346.7 34.8 reduce-scatter.8
  383.8 34.2 reduce-scatter.6
  420.5 34.5 reduce-scatter.4
  456.7 32.5 all-gather.15
  496.1 135.8 all-reduce.4
where the time goes:
time: 685 us; the launch traced here: 678 us
  waiting for transfers between devices  518 us (76%)
  matrix products  101 us (15%)
  local copies, waits for them, and re-layouts  27.4 us (4%)
  between operations  15.4 us (2%)
  other arithmetic  14.8 us (2%)
    psum x1, waiting for transfers between devices, per_device(): summed = lax.psum(local_gram, ('prow', 'pcol'))  143 us
    all_gather x4, waiting for transfers between devices, rows_one(): return lax.all_gather(piece, 'pcol', axis=1, tiled=True)  114 us
    psum x1, waiting for transfers between devices, from_root(): return lax.psum(jnp.where(mine, array, jnp.zeros_like(array)), axis)  104 us
    reduce_scatter x4, waiting for transfers between devices, reduce_one(): lax.psum_scatter(term(jnp.int32(0), lax.axis_size('pcol') * count), 'pcol...  99 us
    dot_general x4, matrix products, term(): jnp.einsum('iaekb,kbn->aien', view, stacked, precision=HIGHEST, preferred...  43.6 us
    all_gather x1, waiting for transfers between devices, per_device(): lax.all_gather(factor_top, 'pcol', axis=1, tiled=True)  32.7 us
    dot_general x28, matrix products, inner_product(): lax.dot_general(left, right, (((0,), (0,)), ((), ())), precision=HIGHEST,...  29.9 us
    dot_general x30, matrix products, matmul(): jnp.dot(left, right, precision=HIGHEST, preferred_element_type=jnp.float32)  27.6 us
  transfers between devices with their start and end apart: 13, of which 12 were waited for; matrix products, arithmetic and copies ran while one was open for 15% of the time, Pallas kernels for 0%

commit v1 on v0

--- a/solution.py
+++ b/solution.py
@@ -1,6 +1,8 @@
 import jax
 import jax.numpy as jnp
 from jax import lax
+from jax.experimental import pallas as pl
+from jax.experimental.pallas import tpu as pltpu
 from jax.sharding import PartitionSpec as P
 
 NB = 256
@@ -82,7 +84,7 @@
     return reduce_rows(term, unit).reshape(cycles, sub_rows, width)
 
 
-def per_device(adjoint_trail, factor_low, adjoint_low, factor_top, adjoint_top, diag_inverse):
+def per_device_any(adjoint_trail, factor_low, adjoint_low, factor_top, adjoint_top, diag_inverse):
     cycles = factor_low.shape[0]
     sub_rows = factor_low.shape[3]
     local_rows = cycles * sub_rows
@@ -158,6 +160,440 @@
     return (grad_low, grad_top)
 
 
+AXES = ("prow", "pcol")
+NZ = 4
+LANES = 128
+VMEM = 48 * 1024 * 1024
+GROUPS = ((3, 2), (1, 0))
+HOLDS = ((0, 2, 1, 3), (1, 3, 0, 2), (2, 0, 3, 1), (3, 1, 2, 0))
+
+
+def route(place):
+    pairs = []
+    for prow in range(4):
+        for pcol in range(8):
+            goal = place(prow, pcol // 2, pcol % 2)
+            if goal is not None:
+                pairs.append((prow * 8 + pcol, goal[0] * 8 + goal[1] * 2 + goal[2]))
+    return pairs
+
+
+CORE = route(lambda p, z, c: (p, z, 1 - c))
+UP = route(lambda p, z, c: (p, z + 1, c) if z + 1 < NZ else None)
+DOWN = route(lambda p, z, c: (p, z - 1, c) if z > 0 else None)
+PLANE = {d: route(lambda p, z, c, d=d: (p ^ d, z, c)) for d in (1, 2, 3)}
+LINE = {d: route(lambda p, z, c, d=d: (p, z ^ d, c)) for d in (1, 2, 3)}
+HOME = {
+    s: route(lambda p, z, c, s=s: ((z % 2) * 2 + c, HOLDS[p][z], (z // 2) ^ s)) for s in (0, 1)
+}
+
+
+def move(array, pairs):
+    return lax.ppermute(array, AXES, pairs)
+
+
+def pick(array, index, axis):
+    return lax.dynamic_index_in_dim(array, index, axis, keepdims=False)
+
+
+def call(body, out, cost, **more):
+    flops, bytes_accessed = cost
+    return pl.pallas_call(
+        body,
+        out_shape=out,
+        compiler_params=pltpu.CompilerParams(vmem_limit_bytes=VMEM),
+        cost_estimate=pl.CostEstimate(
+            flops=flops, bytes_accessed=bytes_accessed, transcendentals=0
+        ),
+        **more,
+    )
+
+
+def struct(*shape, dtype=jnp.float32):
+    return jax.ShapeDtypeStruct(shape, dtype)
+
+
+def split(value):
+    high = value.astype(jnp.bfloat16)
+    return high, (value - high.astype(jnp.float32)).astype(jnp.bfloat16)
+
+
+def dot(left, right):
+    return jnp.dot(left, right, preferred_element_type=jnp.float32)
+
+
+def dot3(left, right):
+    return dot(left[0], right[0]) + (dot(left[0], right[1]) + dot(left[1], right[0]))
+
+
+def panel_of(view, panel):
+    rows = view.shape[0] // 8
+    halves = [view[pl.ds(4 * half + panel, rows, stride=8), :] for half in range(2)]
+    return jnp.concatenate(halves, 1)
+
+
+def eighths(array):
+    rows = array.size // (K * NB)
+    return array.reshape(rows, K, 2, LANES).transpose(0, 2, 1, 3).reshape(rows * 8, LANES)
+
+
+def take_body(panels, view, extra, out):
+    rows = view.shape[0] // 8
+    for at, panel in enumerate(panels):
+        out[:rows, at * NB : (at + 1) * NB] = panel_of(view, panel)
+    if extra is not None:
+        out[rows:, :] = extra[...]
+
+
+def take(panels, view, extra):
+    rows = view.shape[0] // 8
+    width = len(panels) * NB
+    if extra is None:
+        return call(
+            lambda v, o: take_body(panels, v, None, o), struct(rows, width), (0, 2 * view.size)
+        )(view)
+    return call(
+        lambda v, e, o: take_body(panels, v, e, o),
+        struct(rows + extra.shape[0], width),
+        (0, 2 * view.size),
+    )(view, extra)
+
+
+def turn_body(order, block, high, low):
+    rows = block.shape[0] * block.shape[2] // 8
+    flat = block.reshape(rows * 8, LANES)
+    for part in range(8):
+        value = flat[pl.ds(part, rows, stride=8), :].T
+        top, rest = split(value)
+        high[part * LANES : (part + 1) * LANES, :] = top
+        low[part * LANES : (part + 1) * LANES, :] = rest
+
+
+def turn(trail, order):
+    cycles, slots, rows, _ = trail.shape
+    unit = cycles * rows // 8
+    spec = pl.BlockSpec((8 * LANES, unit), lambda i, order: (0, i))
+    shape = struct(8 * LANES, slots * unit, dtype=jnp.bfloat16)
+    return call(
+        turn_body,
+        (shape, shape),
+        (0, 2 * trail.size * 4),
+        grid_spec=pltpu.PrefetchScalarGridSpec(
+            num_scalar_prefetch=1,
+            grid=(slots,),
+            in_specs=[
+                pl.BlockSpec((cycles, 1, rows, LANES), lambda i, order: (0, order[i], 0, 0))
+            ],
+            out_specs=[spec, spec],
+        ),
+    )(order, trail)
+
+
+def product_body(order, high, low, own, others, own_x, others_x, *rest):
+    outs, (c_high, c_low, total) = rest[:4], rest[4:]
+    unit = high.shape[1] // 8
+
+    @pl.when(pl.program_id(0) == 0)
+    def _():
+        for half, (first, later) in enumerate(((own, others), (own_x, others_x))):
+            for slot in range(NZ):
+                value = first[:unit, :] if slot == 0 else later[slot - 1, :unit, :]
+                at = pl.ds((half * NZ + slot) * unit, unit)
+                c_high[at, :], c_low[at, :] = split(value)
+
+    total[...] = dot3((high[...], low[...]), (c_high[...], c_low[...]))
+    span = total.shape[0] // NZ
+    for d in range(4):
+        outs[d][0] = total[pl.ds(pl.multiple_of(order[d] * span, span), span), :]
+
+
+def product(turned, order, own, others, own_x, others_x):
+    high, low = turned
+    rows, depth = high.shape
+    width = own.shape[1]
+    steps = rows // NB
+    spec = pl.BlockSpec((NB, depth), lambda i, order: (i, 0))
+
+    def whole(array):
+        return pl.BlockSpec(array.shape, lambda i, order: (0,) * array.ndim)
+
+    arrays = (own, others, own_x, others_x)
+    span = NB // NZ
+    return call(
+        product_body,
+        [struct(steps, span, width)] * 4,
+        (6 * rows * depth * width, rows * depth * 4 + depth * width * 4),
+        grid_spec=pltpu.PrefetchScalarGridSpec(
+            num_scalar_prefetch=1,
+            grid=(steps,),
+            in_specs=[spec, spec] + [whole(a) for a in arrays],
+            out_specs=[pl.BlockSpec((1, span, width), lambda i, order: (i, 0, 0))] * 4,
+            scratch_shapes=[
+                pltpu.VMEM((depth, width), jnp.bfloat16),
+                pltpu.VMEM((depth, width), jnp.bfloat16),
+                pltpu.VMEM((NB, width), jnp.float32),
+            ],
+        ),
+    )(order, high, low, *arrays)
+
+
+def smem():
+    return pl.BlockSpec(memory_space=pltpu.SMEM)
+
+
+def vmem():
+    return pl.BlockSpec(memory_space=pltpu.VMEM)
+
+
+def lay_top_body(where, lines, planes, planes_x, own_x, others_x, high, low, scratch):
+    prow, layer, core = where[0], where[1], where[2]
+    blocks = scratch.shape[0]
+    rows = lines.shape[1]
+    skip = own_x.shape[0] - rows
+    share = rows // (blocks // 2)
+    sub = 4 * share
+    for far in range(2):
+        for slot in range(NZ):
+            for d in range(4):
+                column = ((layer + slot) % NZ) * 2 + (core ^ far)
+                at = pl.multiple_of(column * sub + (prow ^ d) * share, share)
+                for block in range(blocks):
+                    start = (block % (blocks // 2)) * share
+                    lanes = slice(block // (blocks // 2) * NB, (block // (blocks // 2) + 1) * NB)
+                    if d > 0:
+                        source = planes_x if far else planes
+                        value = source[d - 1, slot, start : start + share, lanes]
+                    elif not far:
+                        value = lines[slot, start : start + share, lanes]
+                    elif slot == 0:
+                        value = own_x[skip + start : skip + start + share, lanes]
+                    else:
+                        value = others_x[slot - 1, skip + start : skip + start + share, lanes]
+                    scratch[block, pl.ds(at, share), :] = value
+    for block in range(blocks):
+        high[block], low[block] = split(scratch[block])
+
+
+def lay_top(where, blocks, lines, planes, planes_x, own_x, others_x):
+    shape = struct(blocks, NB, NB, dtype=jnp.bfloat16)
+    return call(
+        lay_top_body,
+        (shape, shape),
+        (0, 3 * blocks * NB * NB * 4),
+        in_specs=[smem()] + [vmem()] * 5,
+        out_specs=[vmem()] * 2,
+        scratch_shapes=[pltpu.VMEM((blocks, NB, NB), jnp.float32)],
+    )(where, lines, planes, planes_x, own_x, others_x)
+
+
+def panel_body(panels, done, *refs):
+    where, same, cross, adjoint, factor, top_high, top_low, adjoint_top = refs[:8]
+    refs = refs[8:]
+    lower_in, refs = refs[: len(done)], refs[len(done) :]
+    blocks_in, refs = refs[: bool(done)], refs[bool(done) :]
+    last = 0 in panels
+    if last:
+        grad, keep, send, image, scratch = refs
+        lower_out = blocks_out = None
+    else:
+        lower_out, refs = refs[: len(panels)], refs[len(panels) :]
+        blocks_out, keep, send, image, scratch = refs
+    prow, pcol, core = where[0], where[1], where[2]
+    steps = same.shape[0]
+    sub = same.shape[1]
+    for k in range(steps):
+        image[pl.ds(pl.multiple_of((2 * k + core) * sub, sub), sub), :] = same[k]
+        image[pl.ds(pl.multiple_of((2 * k + 1 - core) * sub, sub), sub), :] = cross[k]
+
+    def block(row, column):
+        slot = block_slot(row, column)
+        return top_high[slot], top_low[slot]
+
+    def block_row(row, columns):
+        parts = [block(row, column) for column in range(columns)]
+        return tuple(jnp.concatenate([part[i] for part in parts], 1) for i in range(2))
+
+    def inverse(panel):
+        slot = block_slot(K, 0) + panel
+        return top_high[slot], top_low[slot]
+
+    lower, parts = {}, {}
+    for at, panel in enumerate(done):
+        lower[panel] = lower_in[at][...]
+        parts[panel] = split(lower[panel])
+    columns = [split(panel_of(factor, panel)) for panel in range(max(panels) + 1)]
+    terms = {}
+    for at, panel in enumerate(panels):
+        residual = panel_of(adjoint, panel) - 2.0 * image[:, at * NB : (at + 1) * NB]
+        for later in range(panel + 1, K):
+            residual = residual - dot3(parts[later], block(later, panel))
+        value = dot3(split(residual), inverse(panel))
+        lower[panel] = value
+        parts[panel] = split(value)
+        turned = split(value.T)
+        for earlier in range(panel + 1):
+            terms[panel, earlier] = -dot3(turned, columns[earlier])
+    if last:
+        for panel in range(K):
+            for half in range(2):
+                grad[pl.ds(4 * half + panel, grad.shape[0] // 8, stride=8), :] = lower[panel][
+                    :, half * LANES : (half + 1) * LANES
+                ]
+    else:
+        for at, panel in enumerate(panels):
+            lower_out[at][...] = lower[panel]
+
+    share = adjoint_top.shape[1]
+    mine = jnp.where(prow == 0, 1.0, 0.0)
+    upper, diag = {}, {}
+    if done:
+        slots = sorted(block_slot(r, c) for r in done for c in range(r + 1))
+        for r in done:
+            for c in range(r):
+                upper[c, r] = blocks_in[0][slots.index(block_slot(r, c))]
+    rows = {}
+    for row in panels:
+        flipped = {b: split(upper[row, b].T) for b in range(row + 1, K)}
+        total = []
+        for column in range(row + 1):
+            scratch[...] = terms[row, column]
+            at = pl.ds(pl.multiple_of(pcol * share, share), share)
+            scratch[at, :] = scratch[at, :] + mine * adjoint_top[block_slot(row, column)]
+            total.append(scratch[...])
+        for b in range(row + 1, K):
+            for column in range(row + 1):
+                total[column] = total[column] - dot3(flipped[b], block(b, column))
+        ids = [lax.broadcasted_iota(jnp.int32, (NB, NB), axis) for axis in range(2)]
+        lower_adj = jnp.where(ids[0] >= ids[1], total[row], 0.0)
+        d_high, d_low = block(row, row)
+        factor_block = d_high.astype(jnp.float32) + d_low.astype(jnp.float32)
+        factor_block = jnp.where(ids[0] >= ids[1], factor_block, 0.0).T
+        inner = dot3(split(factor_block), split(lower_adj))
+        inner = jnp.where(ids[0] > ids[1], inner, jnp.where(ids[0] == ids[1], 0.5 * inner, 0.0))
+        i_high, i_low = inverse(row)
+        turned = (i_high.astype(jnp.float32) + i_low.astype(jnp.float32)).T
+        spread = dot3(split(turned), split(dot3(split(inner), inverse(row))))
+        diag[row] = 0.5 * (spread + spread.T)
+        doubled = split(2.0 * diag[row])
+        for column in range(row):
+            total[column] = total[column] - dot3(doubled, block(row, column))
+        for column in reversed(range(row)):
+            for middle in range(column + 1, row):
+                total[column] = total[column] - dot3(split(upper[middle, row]), block(middle, column))
+            upper[column, row] = dot3(split(total[column]), inverse(column))
+        for column in range(row):
+            rows[row, column] = upper[column, row]
+        rows[row, row] = diag[row]
+    for at, key in enumerate(sorted(rows)):
+        scratch[...] = rows[key]
+        if blocks_out is not None:
+            blocks_out[at] = rows[key]
+        for z in range(NZ):
+            for target, which in ((keep, core), (send, 1 - core)):
+                start = pl.multiple_of(z * 2 * share + which * share, share)
+                target[at, z] = scratch[pl.ds(start, share), :]
+
+
+def panel_group(panels, done, where, same, cross, views, top, adjoint_top, lower, blocks):
+    local_rows = views[0].shape[0] // 8
+    share = adjoint_top.shape[1]
+    count = sum(panel + 1 for panel in panels)
+    scattered = [struct(count, NZ, share, NB)] * 2
+    if 0 in panels:
+        out = [struct(*views[0].shape)] + scattered
+    else:
+        out = [struct(local_rows, NB)] * len(panels) + [struct(count, NB, NB)] + scattered
+    arrays = (where, same, cross, *views, *top, adjoint_top, *lower, *blocks)
+    work = 40 * 6 * NB**3
+    return call(
+        lambda *refs: panel_body(panels, done, *refs),
+        out,
+        (work, 10 * 1024 * 1024),
+        in_specs=[smem()] + [vmem()] * (len(arrays) - 1),
+        out_specs=[vmem()] * len(out),
+        scratch_shapes=[
+            pltpu.VMEM((local_rows, len(panels) * NB), jnp.float32),
+            pltpu.VMEM((NB, NB), jnp.float32),
+        ],
+    )(*arrays)
+
+
+def line_gather(piece):
+    up, down = [piece], [piece]
+    for _ in range(NZ - 1):
+        up.append(move(up[-1], UP))
+        down.append(move(down[-1], DOWN))
+    return jnp.stack([down[t] + up[NZ - t] for t in range(1, NZ)])
+
+
+def per_device(adjoint_trail, factor_low, adjoint_low, factor_top, adjoint_top, diag_inverse):
+    cycles, sub_rows = factor_low.shape[0], factor_low.shape[3]
+    col_cycles = adjoint_trail.shape[3]
+    prow, pcol = lax.axis_index("prow"), lax.axis_index("pcol")
+    layer, core = pcol // 2, pcol % 2
+    holds = jnp.array(HOLDS, jnp.int32)
+    shares = factor_top.shape[1]
+    count = factor_top.shape[0]
+    where = jnp.stack([prow, pcol, core]).astype(jnp.int32)
+    order = jnp.stack([((layer + t) % NZ) * 2 + (core ^ f) for f in range(2) for t in range(NZ)])
+    quarter = jnp.stack([holds[prow ^ d, layer] for d in range(4)])
+
+    views = (eighths(adjoint_low), eighths(factor_low))
+    part = shares // 4
+    top_all = jnp.concatenate([factor_top, diag_inverse])
+    total_blocks = top_all.shape[0]
+    extra = pick(top_all.reshape(total_blocks, 4, part, NB), prow, 1)
+    extra = extra.reshape(2, total_blocks // 2 * part, NB)
+    extra = jnp.concatenate([extra[0], extra[1]], 1)
+
+    pieces = [
+        take(panels, views[1], extra if at == 0 else None) for at, panels in enumerate(GROUPS)
+    ]
+    gathered = [line_gather(piece) for piece in pieces]
+    trail = adjoint_trail.reshape(cycles, 2 * NZ, sub_rows * 8, LANES)
+    turned = turn(trail, order.astype(jnp.int32))
+
+    rows = cycles * sub_rows
+    lower, lower_of, blocks, scattered, low_out = [], [], [], [], None
+    top = None
+    for at, panels in enumerate(GROUPS):
+        own, others = pieces[at], gathered[at]
+        own_x, others_x = move(own, CORE), move(others, CORE)
+        if at == 0:
+            lines = jnp.concatenate([own[None, rows:], others[:, rows:]])
+            planes = jnp.stack([move(lines, PLANE[d]) for d in (1, 2, 3)])
+            planes_x = move(planes, CORE)
+            spot = jnp.stack([prow, layer, core]).astype(jnp.int32)
+            top = lay_top(spot, total_blocks, lines, planes, planes_x, own_x, others_x)
+        outs = product(turned, quarter, own, others, own_x, others_x)
+        total = outs[0] + sum(move(outs[d], PLANE[d]) for d in (1, 2, 3))
+        total = total.reshape(col_cycles, 2, sub_rows, -1)
+        same = move(pick(total, layer // 2, 1), HOME[0])
+        cross = move(pick(total, 1 - layer // 2, 1), HOME[1])
+        results = panel_group(
+            panels, tuple(lower_of), where, same, cross, views, top, adjoint_top, lower, blocks
+        )
+        if 0 in panels:
+            low_out = results[0]
+        else:
+            lower.extend(results[: len(panels)])
+            lower_of.extend(panels)
+            blocks = [results[len(panels)]]
+        keep, send = results[-2:]
+        kept = keep + move(send, CORE)
+        line = pick(kept, layer, 1)
+        for d in (1, 2, 3):
+            line = line + move(pick(kept, layer ^ d, 1), LINE[d])
+        scattered.append(line + sum(move(line, PLANE[d]) for d in (1, 2, 3)))
+    grad_top = jnp.concatenate(scattered[::-1])
+    grad_low = low_out.reshape(rows, 2, K, LANES).transpose(0, 2, 1, 3).reshape(factor_low.shape)
+    return (grad_low, grad_top)
+
+
+def covers(mesh):
+    return mesh.shape["prow"] == 4 and mesh.shape["pcol"] == 8
+
+
 def solution(mesh):
     in_specs = (
         P(None, "prow", None, None, "pcol", None),
@@ -169,5 +605,5 @@
     )
     out_specs = (P(None, "prow", "pcol", None, None, None), P(None, "pcol", None))
     return jax.shard_map(
-        per_device, mesh=mesh, in_specs=in_specs, out_specs=out_specs, check_vma=False
+        per_device if covers(mesh) else per_device_any, mesh=mesh, in_specs=in_specs, out_specs=out_specs, check_vma=False
     )

time: 685 us -> 270 us (0.39)
  waiting for transfers between devices: 518 us -> 114 us
  matrix products: 101 us -> 0 us
  starting transfers between devices: 1.1 us -> 82.3 us
  Pallas kernels: 0 us -> 55.8 us
  local copies, waits for them, and re-layouts: 27.4 us -> 6.16 us
  between operations: 15.4 us -> 1.09 us
    psum x2 -> x0, waiting for transfers between devices: 246 us -> none  [the longest x1 143 us: per_device(): summed = lax.psum(local_gram, ('prow', 'pcol'))]
    all_gather x7 -> x0, waiting for transfers between devices: 169 us -> none  [the longest x4 114 us: rows_one(): return lax.all_gather(piece, 'pcol', axis=1, tiled=True)]
    ppermute x0 -> x44, waiting for transfers between devices: none -> 114 us  [move(): return lax.ppermute(array, AXES, pairs)]
    dot_general x62 -> x0, matrix products: 101 us -> none  [the longest x4 43.6 us: term(): jnp.einsum('iaekb,kbn->aien', view, stacked, precision=HIGHEST, preferred...]
    reduce_scatter x4 -> x0, waiting for transfers between devices: 99 us -> none  [reduce_one(): lax.psum_scatter(term(jnp.int32(0), lax.axis_size('pcol') * count), 'pcol...]
    ppermute x0 -> x44, starting transfers between devices: none -> 82.3 us  [move(): return lax.ppermute(array, AXES, pairs)]
    pallas_call x0 -> x8, Pallas kernels: none -> 55.8 us  [the longest x2 22.5 us: product(): call(product_body, [struct(steps, span, width)] * 4, (6 * rows * depth *...]
    select_n x4 -> x0, other arithmetic: 8.79 us -> none  [from_root(): return lax.psum(jnp.where(mine, array, jnp.zeros_like(array)), axis)]
  transfers between devices with their start and end apart: 13 -> 44, of which waited for: 12 -> 21; matrix products, arithmetic and copies ran while one was open for 15% -> 4% of each run, Pallas kernels for 0% -> 20%
where the time goes in v1:
time: 270 us; the launch traced here: 269 us
  waiting for transfers between devices  114 us (42%)
  starting transfers between devices  82.3 us (30%)
  Pallas kernels  55.8 us (21%)
  other arithmetic  10.2 us (4%)
  local copies, waits for them, and re-layouts  6.16 us (2%)
    ppermute x44, waiting for transfers between devices, move(): return lax.ppermute(array, AXES, pairs)  114 us
    ppermute x44, starting transfers between devices, move(): return lax.ppermute(array, AXES, pairs)  82.3 us
    pallas_call x2, Pallas kernels, product(): call(product_body, [struct(steps, span, width)] * 4, (6 * rows * depth *...  22.5 us
    pallas_call x2, Pallas kernels, panel_group(): call(lambda *refs: panel_body(panels, done, *refs), out, (work, 10 * 1024...  18.9 us
    pallas_call x1, Pallas kernels, turn(): call(turn_body, (shape, shape), (0, 2 * trail.size * 4), grid_spec=pltpu....  9.43 us
  transfers between devices with their start and end apart: 44, of which 21 were waited for; matrix products, arithmetic and copies ran while one was open for 4% of the time, Pallas kernels for 20%

profile of v1, /device:TPU:0, one launch (start us, length us, event | category | flops | bytes accessed | tf_op | source)
XLA Modules:
  0.0 269.1 jit_solution(14872030590076432934)
XLA Ops:
  4.2 5.6 %collective-permute-start.14 = (f32[312,512]{1,0:T(8,128)}, f32[312,512]{1,0:T(8,128)S(1)}, u32[]{:S(2)}, u32[]{:S(2)}) collective-permute-start(f32[312,512]{1,0:T(8,128)} %shard_map.89.own), channel_id=1, source_target_pairs={{0,2},{1,3},{2,4},{3,5},{4,6},{5,7},{8,10},{9,11},{10,12},{11,13},... | collective-permute-start | bytes 1916936 | tf_op jit(solution)/shard_map/ppermute | solution.py:192
  11.3 4.6 %collective-permute-start.1 = (f32[256,512]{1,0:T(8,128)S(1)}, f32[256,512]{1,0:T(8,128)S(1)}, u32[]{:S(2)}, u32[]{:S(2)}) collective-permute-start(f32[256,512]{1,0:T(8,128)S(1)} %shard_map.87.own), channel_id=1, source_target_pairs={{0,2},{1,3},{2,4},{3,5},{4,6},{5,7},{8,10},{9,11},{10,12},{11,13},... | collective-permute-start | bytes 1572872 | tf_op jit(solution)/shard_map/ppermute | solution.py:192
  15.9 7.4 %collective-permute-done.13 = f32[312,512]{1,0:T(8,128)S(1)} collective-permute-done((f32[312,512]{1,0:T(8,128)}, f32[312,512]{1,0:T(8,128)S(1)}, u32[]{:S(2)}, u32[]{:S(2)}) %collective-permute-start.13) | collective-permute-done | bytes 639008 | tf_op jit(solution)/shard_map/ppermute | solution.py:192
  29.2 5.3 %collective-permute-done = f32[256,512]{1,0:T(8,128)S(1)} collective-permute-done((f32[256,512]{1,0:T(8,128)S(1)}, f32[256,512]{1,0:T(8,128)S(1)}, u32[]{:S(2)}, u32[]{:S(2)}) %collective-permute-start) | collective-permute-done | bytes 524320 | tf_op jit(solution)/shard_map/ppermute | solution.py:192
  36.0 4.4 %collective-permute-start.2 = (f32[256,512]{1,0:T(8,128)S(1)}, f32[256,512]{1,0:T(8,128)S(1)}, u32[]{:S(2)}, u32[]{:S(2)}) collective-permute-start(f32[256,512]{1,0:T(8,128)S(1)} %collective-permute-done.1), channel_id=1, source_target_pairs={{0,2},{1,3},{2,4},{3,5},{4,6},{5,7},{8,10},{9,11},{10,12},{11,13},... | collective-permute-start | bytes 1572872 | tf_op jit(solution)/shard_map/ppermute | solution.py:192
  40.4 7.8 %collective-permute-done.17 = f32[312,512]{1,0:T(8,128)S(1)} collective-permute-done((f32[312,512]{1,0:T(8,128)S(1)}, f32[312,512]{1,0:T(8,128)S(1)}, u32[]{:S(2)}, u32[]{:S(2)}) %collective-permute-start.17) | collective-permute-done | bytes 639008 | tf_op jit(solution)/shard_map/ppermute | solution.py:192
  49.7 4.4 %collective-permute-start.16 = (f32[312,512]{1,0:T(8,128)S(1)}, f32[312,512]{1,0:T(8,128)S(1)}, u32[]{:S(2)}, u32[]{:S(2)}) collective-permute-start(f32[312,512]{1,0:T(8,128)S(1)} %collective-permute-done.15), channel_id=1, source_target_pairs={{0,2},{1,3},{2,4},{3,5},{4,6},{5,7},{8,10},{9,11},{10,12},{11,13},... | collective-permute-start | bytes 1916936 | tf_op jit(solution)/shard_map/ppermute | solution.py:192
  61.0 4.4 %collective-permute-start.3 = (f32[256,512]{1,0:T(8,128)S(1)}, f32[256,512]{1,0:T(8,128)S(1)}, u32[]{:S(2)}, u32[]{:S(2)}) collective-permute-start(f32[256,512]{1,0:T(8,128)S(1)} %collective-permute-done.2), channel_id=1, source_target_pairs={{0,2},{1,3},{2,4},{3,5},{4,6},{5,7},{8,10},{9,11},{10,12},{11,13},... | collective-permute-start | bytes 1572872 | tf_op jit(solution)/shard_map/ppermute | solution.py:192
  65.5 7.7 %collective-permute-done.18 = f32[312,512]{1,0:T(8,128)S(1)} collective-permute-done((f32[312,512]{1,0:T(8,128)S(1)}, f32[312,512]{1,0:T(8,128)S(1)}, u32[]{:S(2)}, u32[]{:S(2)}) %collective-permute-start.18) | collective-permute-done | bytes 639008 | tf_op jit(solution)/shard_map/ppermute | solution.py:192
  75.1 8.4 %collective-permute-done.5 = f32[256,512]{1,0:T(8,128)S(1)} collective-permute-done((f32[256,512]{1,0:T(8,128)S(1)}, f32[256,512]{1,0:T(8,128)S(1)}, u32[]{:S(2)}, u32[]{:S(2)}) %collective-permute-start.5) | collective-permute-done | bytes 524320 | tf_op jit(solution)/shard_map/ppermute | solution.py:192
  89.9 7.5 %collective-permute-done.21 = f32[4,56,512]{2,1,0:T(8,128)S(1)} collective-permute-done((f32[4,56,512]{2,1,0:T(8,128)S(1)}, f32[4,56,512]{2,1,0:T(8,128)S(1)}, u32[]{:S(2)}, u32[]{:S(2)}) %collective-permute-start.21) | collective-permute-done | bytes 458784 | tf_op jit(solution)/shard_map/ppermute | solution.py:192
  99.6 9.4 %shard_map.86 = (bf16[1024,2048]{1,0:T(8,128)(2,1)S(1)}, bf16[1024,2048]{1,0:T(8,128)(2,1)}) custom-call(s32[8]{0:T(128)S(1)} %stack.99.order, f32[8,8,256,128]{3,2,1,0:T(8,128)} %bitcast.108), custom_call_target="tpu_custom_call" | custom-call | bytes 16777216 | tf_op jit(solution)/shard_map/pallas_call | solution.py:277
  116.4 11.3 %shard_map.91 = (f32[4,64,512]{2,1,0:T(8,128)S(1)}, f32[4,64,512]{2,1,0:T(8,128)S(1)}, f32[4,64,512]{2,1,0:T(8,128)S(1)}, f32[4,64,512]{2,1,0:T(8,128)S(1)}) custom-call(s32[4]{0:T(128)S(1)} %pad_add_fusion.order, bf16[1024,2048]{1,0:T(8,128)(2,1)} %copy-done.3, bf16[1024,2048]{1,0:T(8,128)(2,1)} %get-tuple-element.23.low, f32[312,512]{1,0:T(8,128)} %shard_map.89.own, ...), custom_call_target="tpu_custom_call" | custom-call | flops 6442450944 | bytes 12582912 | tf_op jit(solution)/shard_map/pallas_call | solution.py:322
  131.2 11.2 %shard_map.88 = (f32[4,64,512]{2,1,0:T(8,128)S(1)}, f32[4,64,512]{2,1,0:T(8,128)S(1)}, f32[4,64,512]{2,1,0:T(8,128)S(1)}, f32[4,64,512]{2,1,0:T(8,128)S(1)}) custom-call(s32[4]{0:T(128)S(1)} %pad_add_fusion.order, bf16[1024,2048]{1,0:T(8,128)(2,1)} %copy-done.3, bf16[1024,2048]{1,0:T(8,128)(2,1)} %get-tuple-element.23.low, f32[256,512]{1,0:T(8,128)S(1)} %copy-done.2, ...), custom_call_target="tpu_custom_call" | custom-call | flops 6442450944 | bytes 12582912 | tf_op jit(solution)/shard_map/pallas_call | solution.py:322
  145.5 9.3 %collective-permute-done.25 = f32[4,64,512]{2,1,0:T(8,128)S(1)} collective-permute-done((f32[4,64,512]{2,1,0:T(8,128)S(1)}, f32[4,64,512]{2,1,0:T(8,128)S(1)}, u32[]{:S(2)}, u32[]{:S(2)}) %collective-permute-start.25) | collective-permute-done | bytes 524320 | tf_op jit(solution)/shard_map/ppermute | solution.py:192
  156.3 12.5 %collective-permute-done.10 = f32[4,64,512]{2,1,0:T(8,128)S(1)} collective-permute-done((f32[4,64,512]{2,1,0:T(8,128)S(1)}, f32[4,64,512]{2,1,0:T(8,128)S(1)}, u32[]{:S(2)}, u32[]{:S(2)}) %collective-permute-start.10) | collective-permute-done | bytes 524320 | tf_op jit(solution)/shard_map/ppermute | solution.py:192
  170.7 11.3 %collective-permute-done.8 = f32[4,64,512]{2,1,0:T(8,128)S(1)} collective-permute-done((f32[4,64,512]{2,1,0:T(8,128)S(1)}, f32[4,64,512]{2,1,0:T(8,128)S(1)}, u32[]{:S(2)}, u32[]{:S(2)}) %collective-permute-start.8) | collective-permute-done | bytes 524320 | tf_op jit(solution)/shard_map/ppermute | solution.py:192
  191.4 10.2 %shard_map.92 = (f32[256,256]{1,0:T(8,128)S(1)}, f32[256,256]{1,0:T(8,128)S(1)}, f32[7,256,256]{2,1,0:T(8,128)}, f32[7,4,32,256]{3,2,1,0:T(8,128)S(1)}, f32[7,4,32,256]{3,2,1,0:T(8,128)S(1)}) custom-call(s32[3]{0:T(128)S(1)} %add_add_fusion.4.refs_0_, f32[4,32,512]{2,1,0:T(8,128)S(1)} %collective-permute-done.28.refs_1_, ...), custom_call_target="tpu_custom_call" | custom-call | flops 4026531840 | bytes 10485760 | tf_op jit(solution)/shard_map/pallas_call | solution.py:508
  204.8 8.7 %shard_map.93 = (f32[2048,128]{1,0:T(8,128)}, f32[3,4,32,256]{3,2,1,0:T(8,128)S(1)}, f32[3,4,32,256]{3,2,1,0:T(8,128)}) custom-call(s32[3]{0:T(128)S(1)} %add_add_fusion.4.refs_0_, f32[4,32,512]{2,1,0:T(8,128)S(1)} %collective-permute-done.11.refs_1_, f32[4,32,512]{2,1,0:T(8,128)S(1)} %collective-permute-done.12.refs_2_, f32[2048,128]{1,0:T(8,128)S(1)} %bitcast.107, ...), custom_call_target="tpu_custom_call" | custom-call | flops 4026531840 | bytes 10485760 | tf_op jit(solution)/shard_map/pallas_call | solution.py:508
  215.6 8.8 %collective-permute-start.33 = (f32[3,32,256]{2,1,0:T(8,128)S(1)}, f32[3,32,256]{2,1,0:T(8,128)S(1)}, u32[]{:S(2)}, u32[]{:S(2)}) collective-permute-start(f32[3,32,256]{2,1,0:T(8,128)S(1)} %get-tuple-element.52), channel_id=1, source_target_pairs={{0,6},{1,7},{2,4},{3,5},{4,2},{5,3},{6,0},{7,1},{8,14},{9,15},{10,... | collective-permute-start | bytes 294920 | tf_op jit(solution)/shard_map/ppermute | solution.py:192
  232.9 10.9 %collective-permute-done.32 = f32[3,32,256]{2,1,0:T(8,128)S(1)} collective-permute-done((f32[3,32,256]{2,1,0:T(8,128)S(1)}, f32[3,32,256]{2,1,0:T(8,128)S(1)}, u32[]{:S(2)}, u32[]{:S(2)}) %collective-permute-start.32) | collective-permute-done | bytes 98336 | tf_op jit(solution)/shard_map/ppermute | solution.py:192
  248.1 5.4 %collective-permute-done.39 = f32[7,32,256]{2,1,0:T(8,128)S(1)} collective-permute-done((f32[7,32,256]{2,1,0:T(8,128)S(1)}, f32[7,32,256]{2,1,0:T(8,128)S(1)}, u32[]{:S(2)}, u32[]{:S(2)}) %collective-permute-start.39) | collective-permute-done | bytes 229408 | tf_op jit(solution)/shard_map/ppermute | solution.py:192
  257.9 5.5 %collective-permute-done.43 = f32[7,32,256]{2,1,0:T(8,128)S(1)} collective-permute-done((f32[7,32,256]{2,1,0:T(8,128)S(1)}, f32[7,32,256]{2,1,0:T(8,128)S(1)}, u32[]{:S(2)}, u32[]{:S(2)}) %collective-permute-start.43) | collective-permute-done | bytes 229408 | tf_op jit(solution)/shard_map/ppermute | solution.py:192
  263.4 4.9 %collective-permute-done.41 = f32[7,32,256]{2,1,0:T(8,128)S(1)} collective-permute-done((f32[7,32,256]{2,1,0:T(8,128)S(1)}, f32[7,32,256]{2,1,0:T(8,128)S(1)}, u32[]{:S(2)}, u32[]{:S(2)}) %collective-permute-start.41) | collective-permute-done | bytes 229408 | tf_op jit(solution)/shard_map/ppermute | solution.py:192
  (125 shorter events, 81.2 us)
Async XLA Ops:
  10.0 24.6 %collective-permute-start = (f32[256,512]{1,0:T(8,128)S(1)}, f32[256,512]{1,0:T(8,128)S(1)}, u32[]{:S(2)}, u32[]{:S(2)}) collective-permute-start(f32[256,512]{1,0:T(8,128)S(1)} %shard_map.87.own), channel_id=1, source_target_pairs={{2,0},{3,1},{4,2},{5,3},{6,4},{7,5},{10,8},{11,9},{12,10},{13,11},... | collective-permute-start | bytes 1572872 | tf_op jit(solution)/shard_map/ppermute | solution.py:192
  11.3 24.8 %collective-permute-start.1 = (f32[256,512]{1,0:T(8,128)S(1)}, f32[256,512]{1,0:T(8,128)S(1)}, u32[]{:S(2)}, u32[]{:S(2)}) collective-permute-start(f32[256,512]{1,0:T(8,128)S(1)} %shard_map.87.own), channel_id=1, source_target_pairs={{0,2},{1,3},{2,4},{3,5},{4,6},{5,7},{8,10},{9,11},{10,12},{11,13},... | collective-permute-start | bytes 1572872 | tf_op jit(solution)/shard_map/ppermute | solution.py:192
  23.3 24.9 %collective-permute-start.17 = (f32[312,512]{1,0:T(8,128)S(1)}, f32[312,512]{1,0:T(8,128)S(1)}, u32[]{:S(2)}, u32[]{:S(2)}) collective-permute-start(f32[312,512]{1,0:T(8,128)S(1)} %collective-permute-done.13), channel_id=1, source_target_pairs={{2,0},{3,1},{4,2},{5,3},{6,4},{7,5},{10,8},{11,9},{12,10},{13,11},... | collective-permute-start | bytes 1916936 | tf_op jit(solution)/shard_map/ppermute | solution.py:192
  24.9 24.8 %collective-permute-start.15 = (f32[312,512]{1,0:T(8,128)S(1)}, f32[312,512]{1,0:T(8,128)S(1)}, u32[]{:S(2)}, u32[]{:S(2)}) collective-permute-start(f32[312,512]{1,0:T(8,128)S(1)} %collective-permute-done.14), channel_id=1, source_target_pairs={{0,2},{1,3},{2,4},{3,5},{4,6},{5,7},{8,10},{9,11},{10,12},{11,13},... | collective-permute-start | bytes 1916936 | tf_op jit(solution)/shard_map/ppermute | solution.py:192
  34.5 24.9 %collective-permute-start.4 = (f32[256,512]{1,0:T(8,128)S(1)}, f32[256,512]{1,0:T(8,128)S(1)}, u32[]{:S(2)}, u32[]{:S(2)}) collective-permute-start(f32[256,512]{1,0:T(8,128)S(1)} %collective-permute-done), channel_id=1, source_target_pairs={{2,0},{3,1},{4,2},{5,3},{6,4},{7,5},{10,8},{11,9},{12,10},{13,11},... | collective-permute-start | bytes 1572872 | tf_op jit(solution)/shard_map/ppermute | solution.py:192
  36.0 24.9 %collective-permute-start.2 = (f32[256,512]{1,0:T(8,128)S(1)}, f32[256,512]{1,0:T(8,128)S(1)}, u32[]{:S(2)}, u32[]{:S(2)}) collective-permute-start(f32[256,512]{1,0:T(8,128)S(1)} %collective-permute-done.1), channel_id=1, source_target_pairs={{0,2},{1,3},{2,4},{3,5},{4,6},{5,7},{8,10},{9,11},{10,12},{11,13},... | collective-permute-start | bytes 1572872 | tf_op jit(solution)/shard_map/ppermute | solution.py:192
  48.2 24.9 %collective-permute-start.18 = (f32[312,512]{1,0:T(8,128)S(1)}, f32[312,512]{1,0:T(8,128)S(1)}, u32[]{:S(2)}, u32[]{:S(2)}) collective-permute-start(f32[312,512]{1,0:T(8,128)S(1)} %collective-permute-done.17), channel_id=1, source_target_pairs={{2,0},{3,1},{4,2},{5,3},{6,4},{7,5},{10,8},{11,9},{12,10},{13,11},... | collective-permute-start | bytes 1916936 | tf_op jit(solution)/shard_map/ppermute | solution.py:192
  49.7 24.9 %collective-permute-start.16 = (f32[312,512]{1,0:T(8,128)S(1)}, f32[312,512]{1,0:T(8,128)S(1)}, u32[]{:S(2)}, u32[]{:S(2)}) collective-permute-start(f32[312,512]{1,0:T(8,128)S(1)} %collective-permute-done.15), channel_id=1, source_target_pairs={{0,2},{1,3},{2,4},{3,5},{4,6},{5,7},{8,10},{9,11},{10,12},{11,13},... | collective-permute-start | bytes 1916936 | tf_op jit(solution)/shard_map/ppermute | solution.py:192
  59.5 24.1 %collective-permute-start.5 = (f32[256,512]{1,0:T(8,128)S(1)}, f32[256,512]{1,0:T(8,128)S(1)}, u32[]{:S(2)}, u32[]{:S(2)}) collective-permute-start(f32[256,512]{1,0:T(8,128)S(1)} %collective-permute-done.4), channel_id=1, source_target_pairs={{2,0},{3,1},{4,2},{5,3},{6,4},{7,5},{10,8},{11,9},{12,10},{13,11},... | collective-permute-start | bytes 1572872 | tf_op jit(solution)/shard_map/ppermute | solution.py:192
  61.0 23.8 %collective-permute-start.3 = (f32[256,512]{1,0:T(8,128)S(1)}, f32[256,512]{1,0:T(8,128)S(1)}, u32[]{:S(2)}, u32[]{:S(2)}) collective-permute-start(f32[256,512]{1,0:T(8,128)S(1)} %collective-permute-done.2), channel_id=1, source_target_pairs={{0,2},{1,3},{2,4},{3,5},{4,6},{5,7},{8,10},{9,11},{10,12},{11,13},... | collective-permute-start | bytes 1572872 | tf_op jit(solution)/shard_map/ppermute | solution.py:192
  75.0 41.4 %collective-permute-start.24 = (f32[3,312,512]{2,1,0:T(8,128)S(1)}, f32[3,312,512]{2,1,0:T(8,128)}, u32[]{:S(2)}, u32[]{:S(2)}) collective-permute-start(f32[3,312,512]{2,1,0:T(8,128)S(1)} %pad_maximum_fusion.others), channel_id=1, source_target_pairs={{0,1},{1,0},{2,3},{3,2},{4,5},{5,4},{6,7},{7,6},{8,9},{9,8},{10,11... | collective-permute-start | bytes 5750792 | tf_op jit(solution)/shard_map/ppermute | solution.py:192
  88.8 42.4 %collective-permute-start.7 = (f32[3,256,512]{2,1,0:T(8,128)}, f32[3,256,512]{2,1,0:T(8,128)}, u32[]{:S(2)}, u32[]{:S(2)}) collective-permute-start(f32[3,256,512]{2,1,0:T(8,128)} %pad_maximum_fusion.1.others), channel_id=1, source_target_pairs={{0,1},{1,0},{2,3},{3,2},{4,5},{5,4},{6,7},{7,6},{8,9},{9,8},{10,11... | collective-permute-start | bytes 4718600 | tf_op jit(solution)/shard_map/ppermute | solution.py:192
  88.8 27.5 %collective-permute-start.23 = (f32[312,512]{1,0:T(8,128)}, f32[312,512]{1,0:T(8,128)}, u32[]{:S(2)}, u32[]{:S(2)}) collective-permute-start(f32[312,512]{1,0:T(8,128)} %shard_map.89.own), channel_id=1, source_target_pairs={{0,1},{1,0},{2,3},{3,2},{4,5},{5,4},{6,7},{7,6},{8,9},{9,8},{10,11... | collective-permute-start | bytes 1916936 | tf_op jit(solution)/shard_map/ppermute | solution.py:192
  89.4 25.0 %collective-permute-start.20 = (f32[4,56,512]{2,1,0:T(8,128)S(1)}, f32[4,56,512]{2,1,0:T(8,128)}, u32[]{:S(2)}, u32[]{:S(2)}) collective-permute-start(f32[4,56,512]{2,1,0:T(8,128)S(1)} %pad_maximum_fusion.3.lines), channel_id=1, source_target_pairs={{0,16},{1,17},{2,18},{3,19},{4,20},{5,21},{6,22},{7,23},{8,24},{9,... | collective-permute-start | bytes 1376264 | tf_op jit(solution)/shard_map/ppermute | solution.py:192
  115.8 70.2 %collective-permute-start.22 = (f32[3,4,56,512]{3,2,1,0:T(8,128)S(1)}, f32[3,4,56,512]{3,2,1,0:T(8,128)S(1)}, u32[]{:S(2)}, u32[]{:S(2)}) collective-permute-start(f32[3,4,56,512]{3,2,1,0:T(8,128)S(1)} %pad_maximum_fusion.2.planes), channel_id=1, source_target_pairs={{0,1},{1,0},{2,3},{3,2},{4,5},{5,4},{6,7},{7,6},{8,9},{9,8},{10,11... | collective-permute-start | bytes 4128776 | tf_op jit(solution)/shard_map/ppermute | solution.py:192
  129.2 25.5 %collective-permute-start.25 = (f32[4,64,512]{2,1,0:T(8,128)S(1)}, f32[4,64,512]{2,1,0:T(8,128)S(1)}, u32[]{:S(2)}, u32[]{:S(2)}) collective-permute-start(f32[4,64,512]{2,1,0:T(8,128)S(1)} %get-tuple-element.31), channel_id=1, source_target_pairs={{0,8},{1,9},{2,10},{3,11},{4,12},{5,13},{6,14},{7,15},{8,0},{9,1},... | collective-permute-start | bytes 1572872 | tf_op jit(solution)/shard_map/ppermute | solution.py:192
  130.7 24.6 %collective-permute-start.26 = (f32[4,64,512]{2,1,0:T(8,128)S(1)}, f32[4,64,512]{2,1,0:T(8,128)S(1)}, u32[]{:S(2)}, u32[]{:S(2)}) collective-permute-start(f32[4,64,512]{2,1,0:T(8,128)S(1)} %get-tuple-element.32), channel_id=1, source_target_pairs={{0,16},{1,17},{2,18},{3,19},{4,20},{5,21},{6,22},{7,23},{8,24},{9,... | collective-permute-start | bytes 1572872 | tf_op jit(solution)/shard_map/ppermute | solution.py:192
  142.4 26.3 %collective-permute-start.10 = (f32[4,64,512]{2,1,0:T(8,128)S(1)}, f32[4,64,512]{2,1,0:T(8,128)S(1)}, u32[]{:S(2)}, u32[]{:S(2)}) collective-permute-start(f32[4,64,512]{2,1,0:T(8,128)S(1)} %get-tuple-element.27), channel_id=1, source_target_pairs={{0,24},{1,25},{2,26},{3,27},{4,28},{5,29},{6,30},{7,31},{8,16},{9,... | collective-permute-start | bytes 1572872 | tf_op jit(solution)/shard_map/ppermute | solution.py:192
  144.0 38.0 %collective-permute-start.8 = (f32[4,64,512]{2,1,0:T(8,128)S(1)}, f32[4,64,512]{2,1,0:T(8,128)S(1)}, u32[]{:S(2)}, u32[]{:S(2)}) collective-permute-start(f32[4,64,512]{2,1,0:T(8,128)S(1)} %get-tuple-element.25), channel_id=1, source_target_pairs={{0,8},{1,9},{2,10},{3,11},{4,12},{5,13},{6,14},{7,15},{8,0},{9,1},... | collective-permute-start | bytes 1572872 | tf_op jit(solution)/shard_map/ppermute | solution.py:192
  154.7 27.2 %collective-permute-start.9 = (f32[4,64,512]{2,1,0:T(8,128)S(1)}, f32[4,64,512]{2,1,0:T(8,128)S(1)}, u32[]{:S(2)}, u32[]{:S(2)}) collective-permute-start(f32[4,64,512]{2,1,0:T(8,128)S(1)} %get-tuple-element.26), channel_id=1, source_target_pairs={{0,16},{1,17},{2,18},{3,19},{4,20},{5,21},{6,22},{7,23},{8,24},{9,... | collective-permute-start | bytes 1572872 | tf_op jit(solution)/shard_map/ppermute | solution.py:192
  155.6 35.7 %collective-permute-start.28 = (f32[4,32,512]{2,1,0:T(8,128)S(1)}, f32[4,32,512]{2,1,0:T(8,128)S(1)}, u32[]{:S(2)}, u32[]{:S(2)}) collective-permute-start(f32[4,32,512]{2,1,0:T(8,128)S(1)} %get-tuple-element.46), channel_id=1, source_target_pairs={{0,0},{1,8},{2,20},{3,28},{4,3},{5,11},{6,23},{7,31},{8,2},{9,10},... | collective-permute-start | bytes 786440 | tf_op jit(solution)/shard_map/ppermute | solution.py:192
  201.6 24.2 %collective-permute-start.37 = (f32[7,4,32,256]{3,2,1,0:T(8,128)S(1)}, f32[7,4,32,256]{3,2,1,0:T(8,128)}, u32[]{:S(2)}, u32[]{:S(2)}) collective-permute-start(f32[7,4,32,256]{3,2,1,0:T(8,128)S(1)} %get-tuple-element.41), channel_id=1, source_target_pairs={{0,1},{1,0},{2,3},{3,2},{4,5},{5,4},{6,7},{7,6},{8,9},{9,8},{10,11... | collective-permute-start | bytes 2752520 | tf_op jit(solution)/shard_map/ppermute | solution.py:192
  230.2 23.3 %collective-permute-start.39 = (f32[7,32,256]{2,1,0:T(8,128)S(1)}, f32[7,32,256]{2,1,0:T(8,128)S(1)}, u32[]{:S(2)}, u32[]{:S(2)}) collective-permute-start(f32[7,32,256]{2,1,0:T(8,128)S(1)} %get-tuple-element.44), channel_id=1, source_target_pairs={{0,4},{1,5},{2,6},{3,7},{4,0},{5,1},{6,2},{7,3},{8,12},{9,13},{10,... | collective-permute-start | bytes 688136 | tf_op jit(solution)/shard_map/ppermute | solution.py:192
  230.7 22.8 %collective-permute-start.38 = (f32[7,32,256]{2,1,0:T(8,128)S(1)}, f32[7,32,256]{2,1,0:T(8,128)S(1)}, u32[]{:S(2)}, u32[]{:S(2)}) collective-permute-start(f32[7,32,256]{2,1,0:T(8,128)S(1)} %get-tuple-element.42), channel_id=1, source_target_pairs={{0,2},{1,3},{2,0},{3,1},{4,6},{5,7},{6,4},{7,5},{8,10},{9,11},{10,... | collective-permute-start | bytes 688136 | tf_op jit(solution)/shard_map/ppermute | solution.py:192
  (30 other events, 439.6 us)

commit v2 on v1

--- a/solution.py
+++ b/solution.py
@@ -187,6 +187,12 @@
     s: route(lambda p, z, c, s=s: ((z % 2) * 2 + c, HOLDS[p][z], (z // 2) ^ s)) for s in (0, 1)
 }
 
+BACK = {s: [(goal, source) for source, goal in HOME[s]] for s in (0, 1)}
+SUM_UP = {t: route(lambda p, z, c, t=t: (p, z + 1, c) if z < min(t, 3) else None) for t in (1, 2, 3)}
+SUM_DOWN = {
+    t: route(lambda p, z, c, t=t: (p, z - 1, c) if z >= max(NZ - t, 1) else None) for t in (1, 2, 3)
+}
+
 
 def move(array, pairs):
     return lax.ppermute(array, AXES, pairs)
@@ -257,6 +263,92 @@
         struct(rows + extra.shape[0], width),
         (0, 2 * view.size),
     )(view, extra)
+
+
+def take_parts_body(panels, core, view, same, cross, scratch):
+    steps, sub = same.shape[0], same.shape[1]
+    for at, panel in enumerate(panels):
+        scratch[:, at * NB : (at + 1) * NB] = panel_of(view, panel)
+    for k in range(steps):
+        for out, odd in ((same, core[0]), (cross, 1 - core[0])):
+            out[k] = scratch[pl.ds(pl.multiple_of((2 * k + odd) * sub, sub), sub), :]
+
+
+def take_parts(panels, core, view, sub):
+    rows, width = view.shape[0] // 8, len(panels) * NB
+    shape = struct(rows // sub // 2, sub, width)
+    return call(
+        lambda *refs: take_parts_body(panels, *refs),
+        [shape, shape],
+        (0, 2 * view.size),
+        in_specs=[smem(), vmem()],
+        out_specs=[vmem(), vmem()],
+        scratch_shapes=[pltpu.VMEM((rows, width), jnp.float32)],
+    )(core, view)
+
+
+def halve_body(order, block, high, low):
+    rows = block.shape[0] * block.shape[2] // 8
+    flat = block.reshape(rows * 8, LANES)
+    for part in range(8):
+        lanes = slice(part * LANES, (part + 1) * LANES)
+        high[0, :, lanes], low[0, :, lanes] = split(flat[pl.ds(part, rows, stride=8), :])
+
+
+def halve(trail, order):
+    cycles, slots, rows, _ = trail.shape
+    unit = cycles * rows // 8
+    spec = pl.BlockSpec((1, unit, 8 * LANES), lambda i, order: (i, 0, 0))
+    shape = struct(slots, unit, 8 * LANES, dtype=jnp.bfloat16)
+    return call(
+        halve_body,
+        (shape, shape),
+        (0, 2 * trail.size * 4),
+        grid_spec=pltpu.PrefetchScalarGridSpec(
+            num_scalar_prefetch=1,
+            grid=(slots,),
+            in_specs=[
+                pl.BlockSpec((cycles, 1, rows, LANES), lambda i, order: (0, order[i], 0, 0))
+            ],
+            out_specs=[spec, spec],
+        ),
+    )(order, trail)
+
+
+def column_body(where, high, low, *refs):
+    quarters, out, c_high, c_low = refs[:8], refs[8], refs[9], refs[10]
+
+    @pl.when(pl.program_id(0) == 0)
+    def _():
+        for d in range(4):
+            for side in range(2):
+                source = quarters[2 * d + side]
+                sub = source.shape[1]
+                for k in range(source.shape[0]):
+                    at = k * NB + (where[d] * 2 + (where[4] ^ side)) * sub
+                    at = pl.ds(pl.multiple_of(at, sub), sub)
+                    c_high[at, :], c_low[at, :] = split(source[k])
+
+    out[0] = dot3((high[0], low[0]), (c_high[...], c_low[...]))
+
+
+def column_product(halves, first, count, where, quarters):
+    unit, depth = halves[0].shape[1:]
+    width = quarters[0].shape[2]
+    spec = pl.BlockSpec((1, unit, depth), lambda i, where: (first + i, 0, 0))
+    whole = [pl.BlockSpec(q.shape, lambda i, where: (0, 0, 0)) for q in quarters]
+    return call(
+        column_body,
+        struct(count, unit, width),
+        (6 * count * unit * depth * width, count * unit * depth * 4 + depth * width * 4),
+        grid_spec=pltpu.PrefetchScalarGridSpec(
+            num_scalar_prefetch=1,
+            grid=(count,),
+            in_specs=[spec, spec] + whole,
+            out_specs=pl.BlockSpec((1, unit, width), lambda i, where: (i, 0, 0)),
+            scratch_shapes=[pltpu.VMEM((depth, width), jnp.bfloat16)] * 2,
+        ),
+    )(where, *halves, *quarters)
 
 
 def turn_body(order, block, high, low):
@@ -386,9 +478,11 @@
     )(where, lines, planes, planes_x, own_x, others_x)
 
 
-def panel_body(panels, done, *refs):
-    where, same, cross, adjoint, factor, top_high, top_low, adjoint_top = refs[:8]
-    refs = refs[8:]
+def panel_body(panels, done, parts_in, *refs):
+    where, refs = refs[0], refs[1:]
+    images, refs = refs[:parts_in], refs[parts_in:]
+    adjoint, factor, top_high, top_low, adjoint_top = refs[:5]
+    refs = refs[5:]
     lower_in, refs = refs[: len(done)], refs[len(done) :]
     blocks_in, refs = refs[: bool(done)], refs[bool(done) :]
     last = 0 in panels
@@ -399,11 +493,14 @@
         lower_out, refs = refs[: len(panels)], refs[len(panels) :]
         blocks_out, keep, send, image, scratch = refs
     prow, pcol, core = where[0], where[1], where[2]
-    steps = same.shape[0]
-    sub = same.shape[1]
-    for k in range(steps):
-        image[pl.ds(pl.multiple_of((2 * k + core) * sub, sub), sub), :] = same[k]
-        image[pl.ds(pl.multiple_of((2 * k + 1 - core) * sub, sub), sub), :] = cross[k]
+    if parts_in == 2:
+        same, cross = images
+        steps, sub = same.shape[0], same.shape[1]
+        for k in range(steps):
+            image[pl.ds(pl.multiple_of((2 * k + core) * sub, sub), sub), :] = same[k]
+            image[pl.ds(pl.multiple_of((2 * k + 1 - core) * sub, sub), sub), :] = cross[k]
+    else:
+        image[...] = images[0][...]
 
     def block(row, column):
         slot = block_slot(row, column)
@@ -494,7 +591,7 @@
                 target[at, z] = scratch[pl.ds(start, share), :]
 
 
-def panel_group(panels, done, where, same, cross, views, top, adjoint_top, lower, blocks):
+def panel_group(panels, done, where, images, views, top, adjoint_top, lower, blocks):
     local_rows = views[0].shape[0] // 8
     share = adjoint_top.shape[1]
     count = sum(panel + 1 for panel in panels)
@@ -503,10 +600,10 @@
         out = [struct(*views[0].shape)] + scattered
     else:
         out = [struct(local_rows, NB)] * len(panels) + [struct(count, NB, NB)] + scattered
-    arrays = (where, same, cross, *views, *top, adjoint_top, *lower, *blocks)
+    arrays = (where, *images, *views, *top, adjoint_top, *lower, *blocks)
     work = 40 * 6 * NB**3
     return call(
-        lambda *refs: panel_body(panels, done, *refs),
+        lambda *refs: panel_body(panels, done, len(images), *refs),
         out,
         (work, 10 * 1024 * 1024),
         in_specs=[smem()] + [vmem()] * (len(arrays) - 1),
@@ -546,46 +643,59 @@
     extra = extra.reshape(2, total_blocks // 2 * part, NB)
     extra = jnp.concatenate([extra[0], extra[1]], 1)
 
-    pieces = [
-        take(panels, views[1], extra if at == 0 else None) for at, panels in enumerate(GROUPS)
-    ]
-    gathered = [line_gather(piece) for piece in pieces]
+    rows = cycles * sub_rows
     trail = adjoint_trail.reshape(cycles, 2 * NZ, sub_rows * 8, LANES)
+    spot = jnp.stack([prow, layer, core]).astype(jnp.int32)
+    quarters = jnp.concatenate([quarter, (layer // 2)[None]]).astype(jnp.int32)
+    near = jnp.stack([((layer + t) % NZ) * 2 + (core ^ 1 ^ f) for f in range(2) for t in range(NZ)])
+
+    own = take(GROUPS[0], views[1], extra)
+    mine = take_parts(GROUPS[1], core[None].astype(jnp.int32), views[1], sub_rows)
+    mine = [move(mine[s], BACK[s]) for s in (0, 1)]
+    others = line_gather(own)
+    spread = list(mine)
+    for d in (1, 2, 3):
+        spread += [move(mine[s], PLANE[d]) for s in (0, 1)]
+    halves = halve(trail, near.astype(jnp.int32))
     turned = turn(trail, order.astype(jnp.int32))
-
-    rows = cycles * sub_rows
-    lower, lower_of, blocks, scattered, low_out = [], [], [], [], None
-    top = None
-    for at, panels in enumerate(GROUPS):
-        own, others = pieces[at], gathered[at]
-        own_x, others_x = move(own, CORE), move(others, CORE)
-        if at == 0:
-            lines = jnp.concatenate([own[None, rows:], others[:, rows:]])
-            planes = jnp.stack([move(lines, PLANE[d]) for d in (1, 2, 3)])
-            planes_x = move(planes, CORE)
-            spot = jnp.stack([prow, layer, core]).astype(jnp.int32)
-            top = lay_top(spot, total_blocks, lines, planes, planes_x, own_x, others_x)
-        outs = product(turned, quarter, own, others, own_x, others_x)
-        total = outs[0] + sum(move(outs[d], PLANE[d]) for d in (1, 2, 3))
-        total = total.reshape(col_cycles, 2, sub_rows, -1)
-        same = move(pick(total, layer // 2, 1), HOME[0])
-        cross = move(pick(total, 1 - layer // 2, 1), HOME[1])
-        results = panel_group(
-            panels, tuple(lower_of), where, same, cross, views, top, adjoint_top, lower, blocks
-        )
-        if 0 in panels:
-            low_out = results[0]
-        else:
-            lower.extend(results[: len(panels)])
-            lower_of.extend(panels)
-            blocks = [results[len(panels)]]
-        keep, send = results[-2:]
+    send = column_product(halves, 0, NZ, quarters, spread)
+    keep = column_product(halves, NZ, NZ, quarters, spread)
+    crossed = move(send, CORE)
+    partial = [keep[t] + crossed[t] for t in range(NZ)]
+    up = down = None
+    for t in (1, 2, 3):
+        up_term, down_term = partial[NZ - t], partial[t]
+        if t > 1:
+            up_term, down_term = up_term + up, down_term + down
+        up, down = move(up_term, SUM_UP[t]), move(down_term, SUM_DOWN[t])
+    second_image = partial[0] + up + down
+
+    own_x, others_x = move(own, CORE), move(others, CORE)
+    lines = jnp.concatenate([own[None, rows:], others[:, rows:]])
+    planes = jnp.stack([move(lines, PLANE[d]) for d in (1, 2, 3)])
+    planes_x = move(planes, CORE)
+    top = lay_top(spot, total_blocks, lines, planes, planes_x, own_x, others_x)
+    outs = product(turned, quarter, own, others, own_x, others_x)
+    total = outs[0] + sum(move(outs[d], PLANE[d]) for d in (1, 2, 3))
+    total = total.reshape(col_cycles, 2, sub_rows, -1)
+    same = move(pick(total, layer // 2, 1), HOME[0])
+    cross = move(pick(total, 1 - layer // 2, 1), HOME[1])
+
+    def scatter(keep, send):
         kept = keep + move(send, CORE)
         line = pick(kept, layer, 1)
         for d in (1, 2, 3):
             line = line + move(pick(kept, layer ^ d, 1), LINE[d])
-        scattered.append(line + sum(move(line, PLANE[d]) for d in (1, 2, 3)))
-    grad_top = jnp.concatenate(scattered[::-1])
+        return line + sum(move(line, PLANE[d]) for d in (1, 2, 3))
+
+    *lower, blocks, keep, send = panel_group(
+        GROUPS[0], (), where, (same, cross), views, top, adjoint_top, (), ()
+    )
+    low_rows = scatter(keep, send)
+    low_out, keep, send = panel_group(
+        GROUPS[1], GROUPS[0], where, (second_image,), views, top, adjoint_top, lower, (blocks,)
+    )
+    grad_top = jnp.concatenate([scatter(keep, send), low_rows])
     grad_low = low_out.reshape(rows, 2, K, LANES).transpose(0, 2, 1, 3).reshape(factor_low.shape)
     return (grad_low, grad_top)
 

time: 270 us -> 293 us (1.085)
  waiting for transfers between devices: 114 us -> 98.3 us
  Pallas kernels: 55.8 us -> 67.6 us
  starting transfers between devices: 82.3 us -> 92.8 us
  other arithmetic: 10.2 us -> 18.8 us
  local copies, waits for them, and re-layouts: 6.16 us -> 13.1 us
    pallas_call x3 -> x6, Pallas kernels: 19 us -> 40.1 us  [the longest x2 18.7 us: panel_group(): call(lambda *refs: panel_body(panels, done, len(images), *refs), out, (wo...]
    ppermute x44 -> x46, waiting for transfers between devices: 114 us -> 98.3 us  [move(): return lax.ppermute(array, AXES, pairs)]
    ppermute x44 -> x46, starting transfers between devices: 82.3 us -> 92.8 us  [move(): return lax.ppermute(array, AXES, pairs)]
    pallas_call x2 -> x1, Pallas kernels: 22.5 us -> 12.6 us  [product(): call(product_body, [struct(steps, span, width)] * 4, (6 * rows * depth *...]
    add x6 -> x12, other arithmetic: 1.54 us -> 8.04 us  [the longest x4 5.02 us: per_device(): up_term, down_term = (up_term + up, down_term + down)]
    unnamed x20 -> x50, local copies, waits for them, and re-layouts: 4.26 us -> 7.64 us
  transfers between devices with their start and end apart: 44 -> 46, of which waited for: 21 -> 18; matrix products, arithmetic and copies ran while one was open for 4% -> 8% of each run, Pallas kernels for 20% -> 23%
where the time goes in v2:
time: 293 us; the launch traced here: 292 us
  waiting for transfers between devices  98.3 us (34%)
  starting transfers between devices  92.8 us (32%)
  Pallas kernels  67.6 us (23%)
  other arithmetic  18.8 us (6%)
  local copies, waits for them, and re-layouts  13.1 us (4%)
    ppermute x46, waiting for transfers between devices, move(): return lax.ppermute(array, AXES, pairs)  98.3 us
    ppermute x46, starting transfers between devices, move(): return lax.ppermute(array, AXES, pairs)  92.8 us
    pallas_call x2, Pallas kernels, panel_group(): call(lambda *refs: panel_body(panels, done, len(images), *refs), out, (wo...  18.7 us
    pallas_call x1, Pallas kernels, product(): call(product_body, [struct(steps, span, width)] * 4, (6 * rows * depth *...  12.6 us
    pallas_call x2, Pallas kernels, column_product(): call(column_body, struct(count, unit, width), (6 * count * unit * depth *...  12.4 us
    pallas_call x1, Pallas kernels, turn(): call(turn_body, (shape, shape), (0, 2 * trail.size * 4), grid_spec=pltpu....  9.44 us
    pallas_call x1, Pallas kernels, halve(): call(halve_body, (shape, shape), (0, 2 * trail.size * 4), grid_spec=pltpu...  8.83 us
    unnamed x50, local copies, waits for them, and re-layouts  7.64 us
  transfers between devices with their start and end apart: 46, of which 18 were waited for; matrix products, arithmetic and copies ran while one was open for 8% of the time, Pallas kernels for 23%

profile of v2, /device:TPU:0, one launch (start us, length us, event | category | flops | bytes accessed | tf_op | source)
XLA Modules:
  0.0 292.0 jit_solution(12165672258667060990)
XLA Ops:
  2.8 8.8 %collective-permute-start.1 = (f32[4,32,512]{2,1,0:T(8,128)S(1)}, f32[4,32,512]{2,1,0:T(8,128)S(1)}, u32[]{:S(2)}, u32[]{:S(2)}) collective-permute-start(f32[4,32,512]{2,1,0:T(8,128)S(1)} %get-tuple-element.25), channel_id=1, source_target_pairs={{1,0},{9,1},{21,2},{29,3},{2,4},{10,5},{22,6},{30,7},{3,8},{11,9},... | collective-permute-start | bytes 786440 | tf_op jit(solution)/shard_map/ppermute | solution.py:198
  15.0 14.0 %collective-permute-start.2 = (f32[4,32,512]{2,1,0:T(8,128)S(1)}, f32[4,32,512]{2,1,0:T(8,128)S(1)}, u32[]{:S(2)}, u32[]{:S(2)}) collective-permute-start(f32[4,32,512]{2,1,0:T(8,128)S(1)} %collective-permute-done.refs_0_), channel_id=1, source_target_pairs={{0,8},{1,9},{2,10},{3,11},{4,12},{5,13},{6,14},{7,15},{8,0},{9,1},... | collective-permute-start | bytes 786440 | tf_op jit(solution)/shard_map/ppermute | solution.py:198
  36.1 5.6 %collective-permute-done.3.refs_3_ = f32[4,32,512]{2,1,0:T(8,128)S(1)} collective-permute-done((f32[4,32,512]{2,1,0:T(8,128)S(1)}, f32[4,32,512]{2,1,0:T(8,128)S(1)}, u32[]{:S(2)}, u32[]{:S(2)}) %collective-permute-start.3) | collective-permute-done | bytes 262176 | tf_op jit(solution)/shard_map/ppermute | solution.py:198
  41.7 9.3 %collective-permute-done.4.refs_4_ = f32[4,32,512]{2,1,0:T(8,128)S(1)} collective-permute-done((f32[4,32,512]{2,1,0:T(8,128)S(1)}, f32[4,32,512]{2,1,0:T(8,128)S(1)}, u32[]{:S(2)}, u32[]{:S(2)}) %collective-permute-start.4) | collective-permute-done | bytes 262176 | tf_op jit(solution)/shard_map/ppermute | solution.py:198
  52.6 8.8 %shard_map.86 = (bf16[8,256,1024]{2,1,0:T(8,128)(2,1)S(1)}, bf16[8,256,1024]{2,1,0:T(8,128)(2,1)}) custom-call(s32[8]{0:T(128)S(1)} %stack.105.order, f32[8,8,256,128]{3,2,1,0:T(8,128)} %bitcast.115), custom_call_target="tpu_custom_call" | custom-call | bytes 16777216 | tf_op jit(solution)/shard_map/pallas_call | solution.py:303
  68.0 6.2 %shard_map.89 = f32[4,256,512]{2,1,0:T(8,128)S(1)} custom-call(s32[5]{0:T(128)S(1)} %concatenate.16.where, bf16[8,256,1024]{2,1,0:T(8,128)(2,1)} %copy-done, bf16[8,256,1024]{2,1,0:T(8,128)(2,1)} %get-tuple-element.23.low, f32[4,32,512]{2,1,0:T(8,128)S(1)} %collective-permute-done.refs_0_, f32[4,32,512]{2,1,0:T(8,128)S(1)} %collective-permute-done.1.refs_1_, ...), custom_call_target="tpu_custom_call" | custom-call | flops 3221225472 | bytes 6291456 | tf_op jit(solution)/shard_map/pallas_call | solution.py:340
  74.4 4.6 %collective-permute-start.17 = (f32[312,512]{1,0:T(8,128)S(1)}, f32[312,512]{1,0:T(8,128)S(1)}, u32[]{:S(2)}, u32[]{:S(2)}) collective-permute-start(f32[312,512]{1,0:T(8,128)S(1)} %collective-permute-done.16), channel_id=1, source_target_pairs={{0,2},{1,3},{2,4},{3,5},{4,6},{5,7},{8,10},{9,11},{10,12},{11,13},... | collective-permute-start | bytes 1916936 | tf_op jit(solution)/shard_map/ppermute | solution.py:198
  79.0 4.9 %collective-permute-done.19 = f32[312,512]{1,0:T(8,128)S(1)} collective-permute-done((f32[312,512]{1,0:T(8,128)}, f32[312,512]{1,0:T(8,128)S(1)}, u32[]{:S(2)}, u32[]{:S(2)}) %collective-permute-start.19) | collective-permute-done | bytes 639008 | tf_op jit(solution)/shard_map/ppermute | solution.py:198
  85.1 8.0 %collective-permute-done.17 = f32[312,512]{1,0:T(8,128)S(1)} collective-permute-done((f32[312,512]{1,0:T(8,128)S(1)}, f32[312,512]{1,0:T(8,128)S(1)}, u32[]{:S(2)}, u32[]{:S(2)}) %collective-permute-start.17) | collective-permute-done | bytes 639008 | tf_op jit(solution)/shard_map/ppermute | solution.py:198
  93.2 7.3 %collective-permute-start.18 = (f32[312,512]{1,0:T(8,128)S(1)}, f32[312,512]{1,0:T(8,128)S(1)}, u32[]{:S(2)}, u32[]{:S(2)}) collective-permute-start(f32[312,512]{1,0:T(8,128)S(1)} %collective-permute-done.17), channel_id=1, source_target_pairs={{0,2},{1,3},{2,4},{3,5},{4,6},{5,7},{8,10},{9,11},{10,12},{11,13},... | collective-permute-start | bytes 1916936 | tf_op jit(solution)/shard_map/ppermute | solution.py:198
  101.1 12.9 %collective-permute-done.18 = f32[312,512]{1,0:T(8,128)S(1)} collective-permute-done((f32[312,512]{1,0:T(8,128)S(1)}, f32[312,512]{1,0:T(8,128)S(1)}, u32[]{:S(2)}, u32[]{:S(2)}) %collective-permute-start.18) | collective-permute-done | bytes 639008 | tf_op jit(solution)/shard_map/ppermute | solution.py:198
  116.6 6.2 %shard_map.88 = f32[4,256,512]{2,1,0:T(8,128)S(1)} custom-call(s32[5]{0:T(128)S(1)} %concatenate.16.where, bf16[8,256,1024]{2,1,0:T(8,128)(2,1)} %copy-done, bf16[8,256,1024]{2,1,0:T(8,128)(2,1)} %get-tuple-element.23.low, f32[4,32,512]{2,1,0:T(8,128)S(1)} %collective-permute-done.refs_0_, f32[4,32,512]{2,1,0:T(8,128)S(1)} %collective-permute-done.1.refs_1_, ...), custom_call_target="tpu_custom_call" | custom-call | flops 3221225472 | bytes 6291456 | tf_op jit(solution)/shard_map/pallas_call | solution.py:340
  132.9 6.3 %collective-permute-done.9 = f32[256,512]{1,0:T(8,128)S(1)} collective-permute-done((f32[256,512]{1,0:T(8,128)S(1)}, f32[256,512]{1,0:T(8,128)S(1)}, u32[]{:S(2)}, u32[]{:S(2)}) %collective-permute-start.9) | collective-permute-done | bytes 524320 | tf_op jit(solution)/shard_map/ppermute | solution.py:198
  140.2 5.2 %collective-permute-start.10 = (f32[256,512]{1,0:T(8,128)}, f32[256,512]{1,0:T(8,128)}, u32[]{:S(2)}, u32[]{:S(2)}) collective-permute-start(f32[256,512]{1,0:T(8,128)} %fusion.9), channel_id=1, source_target_pairs={{0,2},{1,3},{2,4},{3,5},{8,10},{9,11},{10,12},{11,13},{16,18},{17,... | collective-permute-start | bytes 1572872 | tf_op jit(solution)/shard_map/ppermute | solution.py:198
  145.5 9.4 %shard_map.92 = (bf16[1024,2048]{1,0:T(8,128)(2,1)S(1)}, bf16[1024,2048]{1,0:T(8,128)(2,1)}) custom-call(s32[8]{0:T(128)S(1)} %stack.121.order, f32[8,8,256,128]{3,2,1,0:T(8,128)} %bitcast.116), custom_call_target="tpu_custom_call" | custom-call | bytes 16777216 | tf_op jit(solution)/shard_map/pallas_call | solution.py:369
  164.3 12.6 %shard_map.93 = (f32[4,64,512]{2,1,0:T(8,128)S(1)}, f32[4,64,512]{2,1,0:T(8,128)}, f32[4,64,512]{2,1,0:T(8,128)}, f32[4,64,512]{2,1,0:T(8,128)}) custom-call(s32[4]{0:T(128)S(1)} %pad_add_fusion.order, bf16[1024,2048]{1,0:T(8,128)(2,1)} %copy-done.13, bf16[1024,2048]{1,0:T(8,128)(2,1)} %get-tuple-element.29.low, f32[312,512]{1,0:T(8,128)} %shard_map.90.own, ...), custom_call_target="tpu_custom_call" | custom-call | flops 6442450944 | bytes 12582912 | tf_op jit(solution)/shard_map/pallas_call | solution.py:414
  183.6 10.1 %collective-permute-done.29 = f32[4,64,512]{2,1,0:T(8,128)} collective-permute-done((f32[4,64,512]{2,1,0:T(8,128)}, f32[4,64,512]{2,1,0:T(8,128)}, u32[]{:S(2)}, u32[]{:S(2)}) %collective-permute-start.29) | collective-permute-done | bytes 524320 | tf_op jit(solution)/shard_map/ppermute | solution.py:198
  193.7 8.2 %collective-permute-done.27 = f32[4,64,512]{2,1,0:T(8,128)} collective-permute-done((f32[4,64,512]{2,1,0:T(8,128)}, f32[4,64,512]{2,1,0:T(8,128)}, u32[]{:S(2)}, u32[]{:S(2)}) %collective-permute-start.27) | collective-permute-done | bytes 524320 | tf_op jit(solution)/shard_map/ppermute | solution.py:198
  222.0 10.4 %shard_map.94 = (f32[256,256]{1,0:T(8,128)S(1)}, f32[256,256]{1,0:T(8,128)S(1)}, f32[7,256,256]{2,1,0:T(8,128)}, f32[7,4,32,256]{3,2,1,0:T(8,128)S(1)}, f32[7,4,32,256]{3,2,1,0:T(8,128)}) custom-call(s32[3]{0:T(128)S(1)} %add_add_fusion.3.refs_0_, f32[4,32,512]{2,1,0:T(8,128)S(1)} %collective-permute-done.30.refs_1_, ...), custom_call_target="tpu_custom_call" | custom-call | flops 4026531840 | bytes 10485760 | tf_op jit(solution)/shard_map/pallas_call | solution.py:605
  234.1 8.3 %shard_map.95 = (f32[2048,128]{1,0:T(8,128)}, f32[3,4,32,256]{3,2,1,0:T(8,128)S(1)}, f32[3,4,32,256]{3,2,1,0:T(8,128)S(1)}) custom-call(s32[3]{0:T(128)S(1)} %add_add_fusion.3.refs_0_, f32[256,512]{1,0:T(8,128)S(1)} %fusion.5.refs_1_, f32[2048,128]{1,0:T(8,128)S(1)} %bitcast.114, f32[2048,128]{1,0:T(8,128)S(1)} %bitcast.112, ...), custom_call_target="tpu_custom_call" | custom-call | flops 4026531840 | bytes 10485760 | tf_op jit(solution)/shard_map/pallas_call | solution.py:605
  244.1 6.1 %collective-permute-start.35 = (f32[3,32,256]{2,1,0:T(8,128)S(1)}, f32[3,32,256]{2,1,0:T(8,128)S(1)}, u32[]{:S(2)}, u32[]{:S(2)}) collective-permute-start(f32[3,32,256]{2,1,0:T(8,128)S(1)} %get-tuple-element.52), channel_id=1, source_target_pairs={{0,6},{1,7},{2,4},{3,5},{4,2},{5,3},{6,0},{7,1},{8,14},{9,15},{10,... | collective-permute-start | bytes 294920 | tf_op jit(solution)/shard_map/ppermute | solution.py:198
  257.5 11.4 %collective-permute-done.34 = f32[3,32,256]{2,1,0:T(8,128)S(1)} collective-permute-done((f32[3,32,256]{2,1,0:T(8,128)S(1)}, f32[3,32,256]{2,1,0:T(8,128)S(1)}, u32[]{:S(2)}, u32[]{:S(2)}) %collective-permute-start.34) | collective-permute-done | bytes 98336 | tf_op jit(solution)/shard_map/ppermute | solution.py:198
  272.5 5.7 %collective-permute-done.41 = f32[7,32,256]{2,1,0:T(8,128)S(1)} collective-permute-done((f32[7,32,256]{2,1,0:T(8,128)S(1)}, f32[7,32,256]{2,1,0:T(8,128)S(1)}, u32[]{:S(2)}, u32[]{:S(2)}) %collective-permute-start.41) | collective-permute-done | bytes 229408 | tf_op jit(solution)/shard_map/ppermute | solution.py:198
  281.8 5.9 %collective-permute-done.45 = f32[7,32,256]{2,1,0:T(8,128)S(1)} collective-permute-done((f32[7,32,256]{2,1,0:T(8,128)S(1)}, f32[7,32,256]{2,1,0:T(8,128)S(1)}, u32[]{:S(2)}, u32[]{:S(2)}) %collective-permute-start.45) | collective-permute-done | bytes 229408 | tf_op jit(solution)/shard_map/ppermute | solution.py:198
  (163 shorter events, 94.3 us)
Async XLA Ops:
  2.8 26.2 %collective-permute-start.1 = (f32[4,32,512]{2,1,0:T(8,128)S(1)}, f32[4,32,512]{2,1,0:T(8,128)S(1)}, u32[]{:S(2)}, u32[]{:S(2)}) collective-permute-start(f32[4,32,512]{2,1,0:T(8,128)S(1)} %get-tuple-element.25), channel_id=1, source_target_pairs={{1,0},{9,1},{21,2},{29,3},{2,4},{10,5},{22,6},{30,7},{3,8},{11,9},... | collective-permute-start | bytes 786440 | tf_op jit(solution)/shard_map/ppermute | solution.py:198
  13.7 52.9 %collective-permute-start.15 = (f32[312,512]{1,0:T(8,128)}, f32[312,512]{1,0:T(8,128)}, u32[]{:S(2)}, u32[]{:S(2)}) collective-permute-start(f32[312,512]{1,0:T(8,128)} %shard_map.90.own), channel_id=1, source_target_pairs={{2,0},{3,1},{4,2},{5,3},{6,4},{7,5},{10,8},{11,9},{12,10},{13,11},... | collective-permute-start | bytes 1916936 | tf_op jit(solution)/shard_map/ppermute | solution.py:198
  15.0 21.1 %collective-permute-start.2 = (f32[4,32,512]{2,1,0:T(8,128)S(1)}, f32[4,32,512]{2,1,0:T(8,128)S(1)}, u32[]{:S(2)}, u32[]{:S(2)}) collective-permute-start(f32[4,32,512]{2,1,0:T(8,128)S(1)} %collective-permute-done.refs_0_), channel_id=1, source_target_pairs={{0,8},{1,9},{2,10},{3,11},{4,12},{5,13},{6,14},{7,15},{8,0},{9,1},... | collective-permute-start | bytes 786440 | tf_op jit(solution)/shard_map/ppermute | solution.py:198
  31.1 19.9 %collective-permute-start.4 = (f32[4,32,512]{2,1,0:T(8,128)S(1)}, f32[4,32,512]{2,1,0:T(8,128)S(1)}, u32[]{:S(2)}, u32[]{:S(2)}) collective-permute-start(f32[4,32,512]{2,1,0:T(8,128)S(1)} %collective-permute-done.refs_0_), channel_id=1, source_target_pairs={{0,16},{1,17},{2,18},{3,19},{4,20},{5,21},{6,22},{7,23},{8,24},{9,... | collective-permute-start | bytes 786440 | tf_op jit(solution)/shard_map/ppermute | solution.py:198
  31.1 36.9 %collective-permute-start.5 = (f32[4,32,512]{2,1,0:T(8,128)S(1)}, f32[4,32,512]{2,1,0:T(8,128)S(1)}, u32[]{:S(2)}, u32[]{:S(2)}) collective-permute-start(f32[4,32,512]{2,1,0:T(8,128)S(1)} %collective-permute-done.1.refs_1_), channel_id=1, source_target_pairs={{0,16},{1,17},{2,18},{3,19},{4,20},{5,21},{6,22},{7,23},{8,24},{9,... | collective-permute-start | bytes 786440 | tf_op jit(solution)/shard_map/ppermute | solution.py:198
  36.1 31.9 %collective-permute-start.6 = (f32[4,32,512]{2,1,0:T(8,128)S(1)}, f32[4,32,512]{2,1,0:T(8,128)S(1)}, u32[]{:S(2)}, u32[]{:S(2)}) collective-permute-start(f32[4,32,512]{2,1,0:T(8,128)S(1)} %collective-permute-done.refs_0_), channel_id=1, source_target_pairs={{0,24},{1,25},{2,26},{3,27},{4,28},{5,29},{6,30},{7,31},{8,16},{9,... | collective-permute-start | bytes 786440 | tf_op jit(solution)/shard_map/ppermute | solution.py:198
  41.7 26.3 %collective-permute-start.7 = (f32[4,32,512]{2,1,0:T(8,128)S(1)}, f32[4,32,512]{2,1,0:T(8,128)S(1)}, u32[]{:S(2)}, u32[]{:S(2)}) collective-permute-start(f32[4,32,512]{2,1,0:T(8,128)S(1)} %collective-permute-done.1.refs_1_), channel_id=1, source_target_pairs={{0,24},{1,25},{2,26},{3,27},{4,28},{5,29},{6,30},{7,31},{8,16},{9,... | collective-permute-start | bytes 786440 | tf_op jit(solution)/shard_map/ppermute | solution.py:198
  51.0 23.3 %collective-permute-start.16 = (f32[312,512]{1,0:T(8,128)}, f32[312,512]{1,0:T(8,128)S(1)}, u32[]{:S(2)}, u32[]{:S(2)}) collective-permute-start(f32[312,512]{1,0:T(8,128)} %shard_map.90.own), channel_id=1, source_target_pairs={{0,2},{1,3},{2,4},{3,5},{4,6},{5,7},{8,10},{9,11},{10,12},{11,13},... | collective-permute-start | bytes 1916936 | tf_op jit(solution)/shard_map/ppermute | solution.py:198
  74.3 48.6 %collective-permute-start.8 = (f32[4,256,512]{2,1,0:T(8,128)S(1)}, f32[4,256,512]{2,1,0:T(8,128)S(1)}, u32[]{:S(2)}, u32[]{:S(2)}) collective-permute-start(f32[4,256,512]{2,1,0:T(8,128)S(1)} %shard_map.89), channel_id=1, source_target_pairs={{0,1},{1,0},{2,3},{3,2},{4,5},{5,4},{6,7},{7,6},{8,9},{9,8},{10,11... | collective-permute-start | bytes 6291464 | tf_op jit(solution)/shard_map/ppermute | solution.py:198
  74.4 18.8 %collective-permute-start.17 = (f32[312,512]{1,0:T(8,128)S(1)}, f32[312,512]{1,0:T(8,128)S(1)}, u32[]{:S(2)}, u32[]{:S(2)}) collective-permute-start(f32[312,512]{1,0:T(8,128)S(1)} %collective-permute-done.16), channel_id=1, source_target_pairs={{0,2},{1,3},{2,4},{3,5},{4,6},{5,7},{8,10},{9,11},{10,12},{11,13},... | collective-permute-start | bytes 1916936 | tf_op jit(solution)/shard_map/ppermute | solution.py:198
  93.2 20.8 %collective-permute-start.18 = (f32[312,512]{1,0:T(8,128)S(1)}, f32[312,512]{1,0:T(8,128)S(1)}, u32[]{:S(2)}, u32[]{:S(2)}) collective-permute-start(f32[312,512]{1,0:T(8,128)S(1)} %collective-permute-done.17), channel_id=1, source_target_pairs={{0,2},{1,3},{2,4},{3,5},{4,6},{5,7},{8,10},{9,11},{10,12},{11,13},... | collective-permute-start | bytes 1916936 | tf_op jit(solution)/shard_map/ppermute | solution.py:198
  116.6 47.7 %collective-permute-start.26 = (f32[3,312,512]{2,1,0:T(8,128)}, f32[3,312,512]{2,1,0:T(8,128)}, u32[]{:S(2)}, u32[]{:S(2)}) collective-permute-start(f32[3,312,512]{2,1,0:T(8,128)} %pad_maximum_fusion.others), channel_id=1, source_target_pairs={{0,1},{1,0},{2,3},{3,2},{4,5},{5,4},{6,7},{7,6},{8,9},{9,8},{10,11... | collective-permute-start | bytes 5750792 | tf_op jit(solution)/shard_map/ppermute | solution.py:198
  129.5 30.2 %collective-permute-start.22 = (f32[4,56,512]{2,1,0:T(8,128)S(1)}, f32[4,56,512]{2,1,0:T(8,128)}, u32[]{:S(2)}, u32[]{:S(2)}) collective-permute-start(f32[4,56,512]{2,1,0:T(8,128)S(1)} %pad_maximum_fusion.2.lines), channel_id=1, source_target_pairs={{0,16},{1,17},{2,18},{3,19},{4,20},{5,21},{6,22},{7,23},{8,24},{9,... | collective-permute-start | bytes 1376264 | tf_op jit(solution)/shard_map/ppermute | solution.py:198
  129.5 30.1 %collective-permute-start.21 = (f32[4,56,512]{2,1,0:T(8,128)S(1)}, f32[4,56,512]{2,1,0:T(8,128)}, u32[]{:S(2)}, u32[]{:S(2)}) collective-permute-start(f32[4,56,512]{2,1,0:T(8,128)S(1)} %pad_maximum_fusion.2.lines), channel_id=1, source_target_pairs={{0,8},{1,9},{2,10},{3,11},{4,12},{5,13},{6,14},{7,15},{8,0},{9,1},... | collective-permute-start | bytes 1376264 | tf_op jit(solution)/shard_map/ppermute | solution.py:198
  140.2 21.5 %collective-permute-start.10 = (f32[256,512]{1,0:T(8,128)}, f32[256,512]{1,0:T(8,128)}, u32[]{:S(2)}, u32[]{:S(2)}) collective-permute-start(f32[256,512]{1,0:T(8,128)} %fusion.9), channel_id=1, source_target_pairs={{0,2},{1,3},{2,4},{3,5},{8,10},{9,11},{10,12},{11,13},{16,18},{17,... | collective-permute-start | bytes 1572872 | tf_op jit(solution)/shard_map/ppermute | solution.py:198
  145.3 19.0 %collective-permute-start.25 = (f32[312,512]{1,0:T(8,128)}, f32[312,512]{1,0:T(8,128)}, u32[]{:S(2)}, u32[]{:S(2)}) collective-permute-start(f32[312,512]{1,0:T(8,128)} %shard_map.90.own), channel_id=1, source_target_pairs={{0,1},{1,0},{2,3},{3,2},{4,5},{5,4},{6,7},{7,6},{8,9},{9,8},{10,11... | collective-permute-start | bytes 1916936 | tf_op jit(solution)/shard_map/ppermute | solution.py:198
  161.1 54.2 %collective-permute-start.24 = (f32[3,4,56,512]{3,2,1,0:T(8,128)S(1)}, f32[3,4,56,512]{3,2,1,0:T(8,128)}, u32[]{:S(2)}, u32[]{:S(2)}) collective-permute-start(f32[3,4,56,512]{3,2,1,0:T(8,128)S(1)} %pad_maximum_fusion.1.planes), channel_id=1, source_target_pairs={{0,1},{1,0},{2,3},{3,2},{4,5},{5,4},{6,7},{7,6},{8,9},{9,8},{10,11... | collective-permute-start | bytes 4128776 | tf_op jit(solution)/shard_map/ppermute | solution.py:198
  177.7 24.3 %collective-permute-start.27 = (f32[4,64,512]{2,1,0:T(8,128)}, f32[4,64,512]{2,1,0:T(8,128)}, u32[]{:S(2)}, u32[]{:S(2)}) collective-permute-start(f32[4,64,512]{2,1,0:T(8,128)} %get-tuple-element.31), channel_id=1, source_target_pairs={{0,8},{1,9},{2,10},{3,11},{4,12},{5,13},{6,14},{7,15},{8,0},{9,1},... | collective-permute-start | bytes 1572872 | tf_op jit(solution)/shard_map/ppermute | solution.py:198
  178.6 25.4 %collective-permute-start.28 = (f32[4,64,512]{2,1,0:T(8,128)}, f32[4,64,512]{2,1,0:T(8,128)}, u32[]{:S(2)}, u32[]{:S(2)}) collective-permute-start(f32[4,64,512]{2,1,0:T(8,128)} %get-tuple-element.32), channel_id=1, source_target_pairs={{0,16},{1,17},{2,18},{3,19},{4,20},{5,21},{6,22},{7,23},{8,24},{9,... | collective-permute-start | bytes 1572872 | tf_op jit(solution)/shard_map/ppermute | solution.py:198
  182.1 30.3 %collective-permute-start.13 = (f32[256,512]{1,0:T(8,128)}, f32[256,512]{1,0:T(8,128)}, u32[]{:S(2)}, u32[]{:S(2)}) collective-permute-start(f32[256,512]{1,0:T(8,128)} %fusion.8), channel_id=1, source_target_pairs={{4,2},{5,3},{6,4},{7,5},{12,10},{13,11},{14,12},{15,13},{20,18},{2... | collective-permute-start | bytes 1572872 | tf_op jit(solution)/shard_map/ppermute | solution.py:198
  209.7 22.7 %collective-permute-start.11 = (f32[256,512]{1,0:T(8,128)S(1)}, f32[256,512]{1,0:T(8,128)S(1)}, u32[]{:S(2)}, u32[]{:S(2)}) collective-permute-start(f32[256,512]{1,0:T(8,128)S(1)} %copy-done.22), channel_id=1, source_target_pairs={{0,2},{1,3},{2,4},{3,5},{4,6},{5,7},{8,10},{9,11},{10,12},{11,13},... | collective-permute-start | bytes 1572872 | tf_op jit(solution)/shard_map/ppermute | solution.py:198
  250.9 19.9 %collective-permute-start.42 = (f32[7,32,256]{2,1,0:T(8,128)S(1)}, f32[7,32,256]{2,1,0:T(8,128)S(1)}, u32[]{:S(2)}, u32[]{:S(2)}) collective-permute-start(f32[7,32,256]{2,1,0:T(8,128)S(1)} %get-tuple-element.45), channel_id=1, source_target_pairs={{0,6},{1,7},{2,4},{3,5},{4,2},{5,3},{6,0},{7,1},{8,14},{9,15},{10,... | collective-permute-start | bytes 688136 | tf_op jit(solution)/shard_map/ppermute | solution.py:198
  254.7 23.4 %collective-permute-start.41 = (f32[7,32,256]{2,1,0:T(8,128)S(1)}, f32[7,32,256]{2,1,0:T(8,128)S(1)}, u32[]{:S(2)}, u32[]{:S(2)}) collective-permute-start(f32[7,32,256]{2,1,0:T(8,128)S(1)} %get-tuple-element.46), channel_id=1, source_target_pairs={{0,4},{1,5},{2,6},{3,7},{4,0},{5,1},{6,2},{7,3},{8,12},{9,13},{10,... | collective-permute-start | bytes 688136 | tf_op jit(solution)/shard_map/ppermute | solution.py:198
  254.8 23.4 %collective-permute-start.40 = (f32[7,32,256]{2,1,0:T(8,128)S(1)}, f32[7,32,256]{2,1,0:T(8,128)S(1)}, u32[]{:S(2)}, u32[]{:S(2)}) collective-permute-start(f32[7,32,256]{2,1,0:T(8,128)S(1)} %get-tuple-element.44), channel_id=1, source_target_pairs={{0,2},{1,3},{2,0},{3,1},{4,6},{5,7},{6,4},{7,5},{8,10},{9,11},{10,... | collective-permute-start | bytes 688136 | tf_op jit(solution)/shard_map/ppermute | solution.py:198
  (47 other events, 523.0 us)

commit v3 on v2

--- a/solution.py
+++ b/solution.py
@@ -179,19 +179,15 @@
 
 
 CORE = route(lambda p, z, c: (p, z, 1 - c))
-UP = route(lambda p, z, c: (p, z + 1, c) if z + 1 < NZ else None)
-DOWN = route(lambda p, z, c: (p, z - 1, c) if z > 0 else None)
 PLANE = {d: route(lambda p, z, c, d=d: (p ^ d, z, c)) for d in (1, 2, 3)}
 LINE = {d: route(lambda p, z, c, d=d: (p, z ^ d, c)) for d in (1, 2, 3)}
+MIDDLE_IN = route(lambda p, z, c: (p, z ^ 1, c) if z in (0, 3) else None)
+MIDDLE_OUT = {d: route(lambda p, z, c, d=d: (p, z ^ d, c) if z in (1, 2) else None) for d in (2, 3)}
 HOME = {
     s: route(lambda p, z, c, s=s: ((z % 2) * 2 + c, HOLDS[p][z], (z // 2) ^ s)) for s in (0, 1)
 }
 
 BACK = {s: [(goal, source) for source, goal in HOME[s]] for s in (0, 1)}
-SUM_UP = {t: route(lambda p, z, c, t=t: (p, z + 1, c) if z < min(t, 3) else None) for t in (1, 2, 3)}
-SUM_DOWN = {
-    t: route(lambda p, z, c, t=t: (p, z - 1, c) if z >= max(NZ - t, 1) else None) for t in (1, 2, 3)
-}
 
 
 def move(array, pairs):
@@ -287,7 +283,7 @@
     )(core, view)
 
 
-def halve_body(order, block, high, low):
+def halve_body(block, high, low):
     rows = block.shape[0] * block.shape[2] // 8
     flat = block.reshape(rows * 8, LANES)
     for part in range(8):
@@ -295,63 +291,61 @@
         high[0, :, lanes], low[0, :, lanes] = split(flat[pl.ds(part, rows, stride=8), :])
 
 
-def halve(trail, order):
+def halve(trail):
     cycles, slots, rows, _ = trail.shape
     unit = cycles * rows // 8
-    spec = pl.BlockSpec((1, unit, 8 * LANES), lambda i, order: (i, 0, 0))
+    spec = pl.BlockSpec((1, unit, 8 * LANES), lambda i: (i, 0, 0))
     shape = struct(slots, unit, 8 * LANES, dtype=jnp.bfloat16)
     return call(
         halve_body,
         (shape, shape),
         (0, 2 * trail.size * 4),
-        grid_spec=pltpu.PrefetchScalarGridSpec(
-            num_scalar_prefetch=1,
-            grid=(slots,),
-            in_specs=[
-                pl.BlockSpec((cycles, 1, rows, LANES), lambda i, order: (0, order[i], 0, 0))
-            ],
-            out_specs=[spec, spec],
-        ),
-    )(order, trail)
+        grid=(slots,),
+        in_specs=[pl.BlockSpec((cycles, 1, rows, LANES), lambda i: (0, i, 0, 0))],
+        out_specs=[spec, spec],
+    )(trail)
 
 
 def column_body(where, high, low, *refs):
-    quarters, out, c_high, c_low = refs[:8], refs[8], refs[9], refs[10]
+    quarters, out, c_high, c_low = refs[:4], refs[4], refs[5], refs[6]
 
     @pl.when(pl.program_id(0) == 0)
     def _():
         for d in range(4):
             for side in range(2):
-                source = quarters[2 * d + side]
-                sub = source.shape[1]
-                for k in range(source.shape[0]):
-                    at = k * NB + (where[d] * 2 + (where[4] ^ side)) * sub
+                source = quarters[d]
+                sub = source.shape[2]
+                for k in range(source.shape[1]):
+                    at = k * NB + (where[d] * 2 + ((where[4] // 2) ^ side)) * sub
                     at = pl.ds(pl.multiple_of(at, sub), sub)
-                    c_high[at, :], c_low[at, :] = split(source[k])
+                    c_high[at, :], c_low[at, :] = split(source[side, k])
 
     out[0] = dot3((high[0], low[0]), (c_high[...], c_low[...]))
 
 
-def column_product(halves, first, count, where, quarters):
+def column_product(halves, side, where, quarters):
     unit, depth = halves[0].shape[1:]
-    width = quarters[0].shape[2]
-    spec = pl.BlockSpec((1, unit, depth), lambda i, where: (first + i, 0, 0))
-    whole = [pl.BlockSpec(q.shape, lambda i, where: (0, 0, 0)) for q in quarters]
+    width = quarters[0].shape[3]
+
+    def slot(i, where):
+        return ((where[4] ^ i) * 2 + (where[5] ^ side), 0, 0)
+
+    whole = [pl.BlockSpec(q.shape, lambda i, where: (0, 0, 0, 0)) for q in quarters]
     return call(
         column_body,
-        struct(count, unit, width),
-        (6 * count * unit * depth * width, count * unit * depth * 4 + depth * width * 4),
+        struct(NZ, unit, width),
+        (6 * NZ * unit * depth * width, NZ * unit * depth * 4 + depth * width * 4),
         grid_spec=pltpu.PrefetchScalarGridSpec(
             num_scalar_prefetch=1,
-            grid=(count,),
-            in_specs=[spec, spec] + whole,
+            grid=(NZ,),
+            in_specs=[pl.BlockSpec((1, unit, depth), slot)] * 2 + whole,
             out_specs=pl.BlockSpec((1, unit, width), lambda i, where: (i, 0, 0)),
             scratch_shapes=[pltpu.VMEM((depth, width), jnp.bfloat16)] * 2,
         ),
     )(where, *halves, *quarters)
 
 
-def turn_body(order, block, high, low):
+def turn_body(block, high, low):
     rows = block.shape[0] * block.shape[2] // 8
     flat = block.reshape(rows * 8, LANES)
     for part in range(8):
@@ -361,56 +355,47 @@
         low[part * LANES : (part + 1) * LANES, :] = rest
 
 
-def turn(trail, order):
+def turn(trail):
     cycles, slots, rows, _ = trail.shape
     unit = cycles * rows // 8
-    spec = pl.BlockSpec((8 * LANES, unit), lambda i, order: (0, i))
+    spec = pl.BlockSpec((8 * LANES, unit), lambda i: (0, i))
     shape = struct(8 * LANES, slots * unit, dtype=jnp.bfloat16)
     return call(
         turn_body,
         (shape, shape),
         (0, 2 * trail.size * 4),
-        grid_spec=pltpu.PrefetchScalarGridSpec(
-            num_scalar_prefetch=1,
-            grid=(slots,),
-            in_specs=[
-                pl.BlockSpec((cycles, 1, rows, LANES), lambda i, order: (0, order[i], 0, 0))
-            ],
-            out_specs=[spec, spec],
-        ),
-    )(order, trail)
-
-
-def product_body(order, high, low, own, others, own_x, others_x, *rest):
+        grid=(slots,),
+        in_specs=[pl.BlockSpec((cycles, 1, rows, LANES), lambda i: (0, i, 0, 0))],
+        out_specs=[spec, spec],
+    )(trail)
+
+
+def product_body(where, high, low, near, far, *rest):
     outs, (c_high, c_low, total) = rest[:4], rest[4:]
-    unit = high.shape[1] // 8
+    unit = high.shape[1] // (2 * NZ)
 
     @pl.when(pl.program_id(0) == 0)
     def _():
-        for half, (first, later) in enumerate(((own, others), (own_x, others_x))):
-            for slot in range(NZ):
-                value = first[:unit, :] if slot == 0 else later[slot - 1, :unit, :]
-                at = pl.ds((half * NZ + slot) * unit, unit)
-                c_high[at, :], c_low[at, :] = split(value)
+        for side, source in enumerate((near, far)):
+            for d in range(NZ):
+                at = ((where[4] ^ d) * 2 + (where[5] ^ side)) * unit
+                at = pl.ds(pl.multiple_of(at, unit), unit)
+                c_high[at, :], c_low[at, :] = split(source[d, :unit, :])
 
     total[...] = dot3((high[...], low[...]), (c_high[...], c_low[...]))
     span = total.shape[0] // NZ
     for d in range(4):
-        outs[d][0] = total[pl.ds(pl.multiple_of(order[d] * span, span), span), :]
-
-
-def product(turned, order, own, others, own_x, others_x):
+        outs[d][0] = total[pl.ds(pl.multiple_of(where[d] * span, span), span), :]
+
+
+def product(turned, where, near, far):
     high, low = turned
     rows, depth = high.shape
-    width = own.shape[1]
+    width = near.shape[2]
     steps = rows // NB
-    spec = pl.BlockSpec((NB, depth), lambda i, order: (i, 0))
-
-    def whole(array):
-        return pl.BlockSpec(array.shape, lambda i, order: (0,) * array.ndim)
-
-    arrays = (own, others, own_x, others_x)
     span = NB // NZ
+    spec = pl.BlockSpec((NB, depth), lambda i, where: (i, 0))
+    whole = pl.BlockSpec(near.shape, lambda i, where: (0, 0, 0))
     return call(
         product_body,
         [struct(steps, span, width)] * 4,
@@ -418,15 +403,15 @@
         grid_spec=pltpu.PrefetchScalarGridSpec(
             num_scalar_prefetch=1,
             grid=(steps,),
-            in_specs=[spec, spec] + [whole(a) for a in arrays],
-            out_specs=[pl.BlockSpec((1, span, width), lambda i, order: (i, 0, 0))] * 4,
+            in_specs=[spec, spec, whole, whole],
+            out_specs=[pl.BlockSpec((1, span, width), lambda i, where: (i, 0, 0))] * 4,
             scratch_shapes=[
                 pltpu.VMEM((depth, width), jnp.bfloat16),
                 pltpu.VMEM((depth, width), jnp.bfloat16),
                 pltpu.VMEM((NB, width), jnp.float32),
             ],
         ),
-    )(order, high, low, *arrays)
+    )(where, high, low, near, far)
 
 
 def smem():
@@ -437,45 +422,41 @@
     return pl.BlockSpec(memory_space=pltpu.VMEM)
 
 
-def lay_top_body(where, lines, planes, planes_x, own_x, others_x, high, low, scratch):
+def lay_top_body(where, near, planes, far, planes_x, high, low, scratch):
     prow, layer, core = where[0], where[1], where[2]
     blocks = scratch.shape[0]
-    rows = lines.shape[1]
-    skip = own_x.shape[0] - rows
+    rows = planes.shape[2]
+    skip = near.shape[1] - rows
     share = rows // (blocks // 2)
     sub = 4 * share
-    for far in range(2):
+    for side, (same, other) in enumerate(((near, planes), (far, planes_x))):
         for slot in range(NZ):
             for d in range(4):
-                column = ((layer + slot) % NZ) * 2 + (core ^ far)
-                at = pl.multiple_of(column * sub + (prow ^ d) * share, share)
+                at = ((layer ^ slot) * 2 + (core ^ side)) * sub + (prow ^ d) * share
+                at = pl.multiple_of(at, share)
                 for block in range(blocks):
                     start = (block % (blocks // 2)) * share
                     lanes = slice(block // (blocks // 2) * NB, (block // (blocks // 2) + 1) * NB)
-                    if d > 0:
-                        source = planes_x if far else planes
-                        value = source[d - 1, slot, start : start + share, lanes]
-                    elif not far:
-                        value = lines[slot, start : start + share, lanes]
-                    elif slot == 0:
-                        value = own_x[skip + start : skip + start + share, lanes]
+                    if d == 0:
+                        first = skip + start
+                        value = same[slot, first : first + share, lanes]
                     else:
-                        value = others_x[slot - 1, skip + start : skip + start + share, lanes]
+                        value = other[d - 1, slot, start : start + share, lanes]
                     scratch[block, pl.ds(at, share), :] = value
     for block in range(blocks):
         high[block], low[block] = split(scratch[block])
 
 
-def lay_top(where, blocks, lines, planes, planes_x, own_x, others_x):
+def lay_top(where, blocks, *arrays):
     shape = struct(blocks, NB, NB, dtype=jnp.bfloat16)
     return call(
         lay_top_body,
         (shape, shape),
         (0, 3 * blocks * NB * NB * 4),
-        in_specs=[smem()] + [vmem()] * 5,
+        in_specs=[smem()] + [vmem()] * 4,
         out_specs=[vmem()] * 2,
         scratch_shapes=[pltpu.VMEM((blocks, NB, NB), jnp.float32)],
-    )(where, lines, planes, planes_x, own_x, others_x)
+    )(where, *arrays)
 
 
 def panel_body(panels, done, parts_in, *refs):
@@ -615,14 +596,6 @@
     )(*arrays)
 
 
-def line_gather(piece):
-    up, down = [piece], [piece]
-    for _ in range(NZ - 1):
-        up.append(move(up[-1], UP))
-        down.append(move(down[-1], DOWN))
-    return jnp.stack([down[t] + up[NZ - t] for t in range(1, NZ)])
-
-
 def per_device(adjoint_trail, factor_low, adjoint_low, factor_top, adjoint_top, diag_inverse):
     cycles, sub_rows = factor_low.shape[0], factor_low.shape[3]
     col_cycles = adjoint_trail.shape[3]
@@ -632,8 +605,9 @@
     shares = factor_top.shape[1]
     count = factor_top.shape[0]
     where = jnp.stack([prow, pcol, core]).astype(jnp.int32)
-    order = jnp.stack([((layer + t) % NZ) * 2 + (core ^ f) for f in range(2) for t in range(NZ)])
-    quarter = jnp.stack([holds[prow ^ d, layer] for d in range(4)])
+    quarters = [holds[prow ^ d, layer] for d in range(4)]
+    quarters = jnp.stack(quarters + [layer, core]).astype(jnp.int32)
+    spot = jnp.stack([prow, layer, core]).astype(jnp.int32)
 
     views = (eighths(adjoint_low), eighths(factor_low))
     part = shares // 4
@@ -645,57 +619,75 @@
 
     rows = cycles * sub_rows
     trail = adjoint_trail.reshape(cycles, 2 * NZ, sub_rows * 8, LANES)
-    spot = jnp.stack([prow, layer, core]).astype(jnp.int32)
-    quarters = jnp.concatenate([quarter, (layer // 2)[None]]).astype(jnp.int32)
-    near = jnp.stack([((layer + t) % NZ) * 2 + (core ^ 1 ^ f) for f in range(2) for t in range(NZ)])
-
-    own = take(GROUPS[0], views[1], extra)
+
+    barrier = lax.optimization_barrier
     mine = take_parts(GROUPS[1], core[None].astype(jnp.int32), views[1], sub_rows)
     mine = [move(mine[s], BACK[s]) for s in (0, 1)]
-    others = line_gather(own)
-    spread = list(mine)
-    for d in (1, 2, 3):
-        spread += [move(mine[s], PLANE[d]) for s in (0, 1)]
-    halves = halve(trail, near.astype(jnp.int32))
-    turned = turn(trail, order.astype(jnp.int32))
-    send = column_product(halves, 0, NZ, quarters, spread)
-    keep = column_product(halves, NZ, NZ, quarters, spread)
-    crossed = move(send, CORE)
-    partial = [keep[t] + crossed[t] for t in range(NZ)]
-    up = down = None
-    for t in (1, 2, 3):
-        up_term, down_term = partial[NZ - t], partial[t]
-        if t > 1:
-            up_term, down_term = up_term + up, down_term + down
-        up, down = move(up_term, SUM_UP[t]), move(down_term, SUM_DOWN[t])
-    second_image = partial[0] + up + down
-
-    own_x, others_x = move(own, CORE), move(others, CORE)
-    lines = jnp.concatenate([own[None, rows:], others[:, rows:]])
-    planes = jnp.stack([move(lines, PLANE[d]) for d in (1, 2, 3)])
-    planes_x = move(planes, CORE)
-    top = lay_top(spot, total_blocks, lines, planes, planes_x, own_x, others_x)
-    outs = product(turned, quarter, own, others, own_x, others_x)
-    total = outs[0] + sum(move(outs[d], PLANE[d]) for d in (1, 2, 3))
-    total = total.reshape(col_cycles, 2, sub_rows, -1)
+    own = take(GROUPS[0], views[1], extra)
+    line = [own, move(own, LINE[1])]
+    halves = halve(trail)
+    mine, halves, line = barrier((jnp.stack(mine), halves, line))
+
+    line += [move(own, LINE[2]), move(own, LINE[3])]
+    spread = [mine] + [move(mine, PLANE[d]) for d in (1, 2, 3)]
+    turned = turn(trail)
+    spread, turned, line = barrier((spread, turned, line))
+
+    near = jnp.stack(line)
+    leaving = column_product(halves, 1, quarters, spread)
+    arriving = move(leaving, CORE)
+    far = move(near, CORE)
+    staying = column_product(halves, 0, quarters, spread)
+    staying, arriving = barrier((staying, arriving))
+
+    term = [staying[d] + arriving[d] for d in range(NZ)]
+    came = move(jnp.stack([term[2], term[3]]), MIDDLE_IN)
+    extras = near[:, rows:]
+    planes = [move(extras, PLANE[d]) for d in (1, 2, 3)]
+    outs = product(turned, quarters, near, far)
+    outs, planes, came = barrier((outs, planes, came))
+
+    folded = [
+        move(term[3] + came[0], MIDDLE_OUT[3]),
+        move(term[2] + came[1], MIDDLE_OUT[2]),
+        move(term[1], LINE[1]),
+    ]
+    parts = [move(outs[d], PLANE[d]) for d in (1, 2, 3)]
+    planes = jnp.stack(planes)
+    top = lay_top(spot, total_blocks, near, planes, far, move(planes, CORE))
+    parts, top = barrier((parts, top))
+
+    total = (outs[0] + sum(parts)).reshape(col_cycles, 2, sub_rows, -1)
     same = move(pick(total, layer // 2, 1), HOME[0])
     cross = move(pick(total, 1 - layer // 2, 1), HOME[1])
-
-    def scatter(keep, send):
-        kept = keep + move(send, CORE)
-        line = pick(kept, layer, 1)
+    same, cross, folded = barrier((same, cross, folded))
+
+    def strips(kept):
+        kept = kept.reshape(kept.shape[0], NZ, 4, part, NB)
+        strip = pick(kept, prow, 2)
         for d in (1, 2, 3):
-            line = line + move(pick(kept, layer ^ d, 1), LINE[d])
-        return line + sum(move(line, PLANE[d]) for d in (1, 2, 3))
+            strip = strip + move(pick(kept, prow ^ d, 2), PLANE[d])
+        return strip
 
     *lower, blocks, keep, send = panel_group(
         GROUPS[0], (), where, (same, cross), views, top, adjoint_top, (), ()
     )
-    low_rows = scatter(keep, send)
+    kept = keep + move(send, CORE)
+    kept, folded = barrier((kept, folded))
+    second_image = term[0] + sum(folded)
+    strip = strips(kept)
     low_out, keep, send = panel_group(
         GROUPS[1], GROUPS[0], where, (second_image,), views, top, adjoint_top, lower, (blocks,)
     )
-    grad_top = jnp.concatenate([scatter(keep, send), low_rows])
+    keep, send, strip = barrier((keep, send, strip))
+    strip = jnp.concatenate([strips(keep + move(send, CORE)), strip])
+    own_strip = pick(strip, layer, 1)
+    for d in (1, 2, 3):
+        own_strip = own_strip + move(pick(strip, layer ^ d, 1), LINE[d])
+    pieces = [own_strip] + [move(own_strip, PLANE[d]) for d in (1, 2, 3)]
+    for bit in (1, 2):
+        pieces = [jnp.where(prow & bit, pieces[d ^ bit], pieces[d]) for d in range(4)]
+    grad_top = jnp.stack(pieces, 1).reshape(count, 4 * part, NB)
     grad_low = low_out.reshape(rows, 2, K, LANES).transpose(0, 2, 1, 3).reshape(factor_low.shape)
     return (grad_low, grad_top)
 

time: 293 us -> 229 us (0.78)
  starting transfers between devices: 92.8 us -> 59.1 us
  waiting for transfers between devices: 98.3 us -> 81 us
  other arithmetic: 18.8 us -> 10.5 us
    ppermute x46 -> x37, starting transfers between devices: 92.8 us -> 59.1 us  [move(): return lax.ppermute(array, AXES, pairs)]
    ppermute x46 -> x37, waiting for transfers between devices: 98.3 us -> 81 us  [move(): return lax.ppermute(array, AXES, pairs)]
    another operation x6 -> x5, other arithmetic: 6.96 us -> 1.89 us  [the longest x1 1.62 us: per_device(): near = jnp.stack(line)]
    add x13 -> x8, other arithmetic: 9.82 us -> 6.48 us  [the longest x1 1.72 us: per_device(): term[2] + came[1]]
    unnamed x50 -> x48, local copies, waits for them, and re-layouts: 7.64 us -> 7.38 us
  transfers between devices with their start and end apart: 46 -> 37, of which waited for: 18 -> 17; matrix products, arithmetic and copies ran while one was open for 8% -> 5% of each run, Pallas kernels for 23% -> 21%
where the time goes in v3:
time: 229 us; the launch traced here: 228 us
  waiting for transfers between devices  81 us (35%)
  Pallas kernels  65.3 us (29%)
  starting transfers between devices  59.1 us (26%)
  local copies, waits for them, and re-layouts  10.8 us (5%)
  other arithmetic  10.5 us (5%)
    ppermute x37, waiting for transfers between devices, move(): return lax.ppermute(array, AXES, pairs)  81 us
    ppermute x37, starting transfers between devices, move(): return lax.ppermute(array, AXES, pairs)  59.1 us
    pallas_call x2, Pallas kernels, panel_group(): call(lambda *refs: panel_body(panels, done, len(images), *refs), out, (wo...  18.4 us
    pallas_call x2, Pallas kernels, column_product(): call(column_body, struct(NZ, unit, width), (6 * NZ * unit * depth * width...  12.8 us
    pallas_call x1, Pallas kernels, product(): call(product_body, [struct(steps, span, width)] * 4, (6 * rows * depth *...  11.8 us
    pallas_call x1, Pallas kernels, turn(): call(turn_body, (shape, shape), (0, 2 * trail.size * 4), grid=(slots,), i...  8.93 us
    pallas_call x1, Pallas kernels, halve(): call(halve_body, (shape, shape), (0, 2 * trail.size * 4), grid=(slots,),...  8.31 us
    unnamed x48, local copies, waits for them, and re-layouts  7.38 us
  transfers between devices with their start and end apart: 37, of which 17 were waited for; matrix products, arithmetic and copies ran while one was open for 5% of the time, Pallas kernels for 21%

profile of v3, /device:TPU:0, one launch (start us, length us, event | category | flops | bytes accessed | tf_op | source)
XLA Modules:
  0.0 227.9 jit_solution(15654112311054534776)
XLA Ops:
  2.1 3.1 %collective-permute-start.2 = (f32[312,512]{1,0:T(8,128)S(1)}, f32[312,512]{1,0:T(8,128)S(1)}, u32[]{:S(2)}, u32[]{:S(2)}) collective-permute-start(f32[312,512]{1,0:T(8,128)S(1)} %shard_map.88), channel_id=1, source_target_pairs={{0,2},{1,3},{2,0},{3,1},{4,6},{5,7},{6,4},{7,5},{8,10},{9,11},{10,... | collective-permute-start | bytes 1916936 | tf_op jit(solution)/shard_map/ppermute | solution.py:194
  6.1 7.1 %collective-permute-start.1 = (f32[4,32,512]{2,1,0:T(8,128)S(1)}, f32[4,32,512]{2,1,0:T(8,128)S(1)}, u32[]{:S(2)}, u32[]{:S(2)}) collective-permute-start(f32[4,32,512]{2,1,0:T(8,128)S(1)} %get-tuple-element.65), channel_id=1, source_target_pairs={{1,0},{9,1},{21,2},{29,3},{2,4},{10,5},{22,6},{30,7},{3,8},{11,9},... | collective-permute-start | bytes 786440 | tf_op jit(solution)/shard_map/ppermute | solution.py:194
  15.2 8.3 %shard_map.87 = (bf16[8,256,1024]{2,1,0:T(8,128)(2,1)S(1)}, bf16[8,256,1024]{2,1,0:T(8,128)(2,1)}) custom-call(f32[8,8,256,128]{3,2,1,0:T(8,128)} %bitcast.125), custom_call_target="tpu_custom_call" | custom-call | bytes 16777216 | tf_op jit(solution)/shard_map/pallas_call | solution.py:299
  25.7 20.8 %collective-permute-done.2 = f32[312,512]{1,0:T(8,128)S(1)} collective-permute-done((f32[312,512]{1,0:T(8,128)S(1)}, f32[312,512]{1,0:T(8,128)S(1)}, u32[]{:S(2)}, u32[]{:S(2)}) %collective-permute-start.2) | collective-permute-done | bytes 639008 | tf_op jit(solution)/shard_map/ppermute | solution.py:194
  46.5 8.7 %collective-permute-start.4 = (f32[2,4,32,512]{3,2,1,0:T(8,128)S(1)}, f32[2,4,32,512]{3,2,1,0:T(8,128)S(1)}, u32[]{:S(2)}, u32[]{:S(2)}) collective-permute-start(f32[2,4,32,512]{3,2,1,0:T(8,128)S(1)} %pad_maximum_fusion.3.refs_0_), channel_id=1, source_target_pairs={{0,16},{1,17},{2,18},{3,19},{4,20},{5,21},{6,22},{7,23},{8,24},{9,... | collective-permute-start | bytes 1572872 | tf_op jit(solution)/shard_map/ppermute | solution.py:194
  55.2 8.9 %shard_map.89 = (bf16[1024,2048]{1,0:T(8,128)(2,1)S(1)}, bf16[1024,2048]{1,0:T(8,128)(2,1)}) custom-call(f32[8,8,256,128]{3,2,1,0:T(8,128)} %bitcast.126), custom_call_target="tpu_custom_call" | custom-call | bytes 16777216 | tf_op jit(solution)/shard_map/pallas_call | solution.py:363
  66.8 2.6 %stack.86.where = s32[6]{0:T(128)S(1)} concatenate(s32[1]{0:T(128)} %bitcast.3, s32[1]{0:T(128)} %bitcast.4, s32[1]{0:T(128)} %bitcast.5, s32[1]{0:T(128)} %bitcast.6, s32[1]{0:T(128)} %bitcast.7, s32[1]{0:T(128)} %bitcast.2.refs_0_), dimensions={0} | concatenate | bytes 48 | tf_op jit(solution)/shard_map/stack | solution.py:609
  69.4 8.5 %collective-permute-done.6 = f32[312,512]{1,0:T(8,128)} collective-permute-done((f32[312,512]{1,0:T(8,128)S(1)}, f32[312,512]{1,0:T(8,128)}, u32[]{:S(2)}, u32[]{:S(2)}) %collective-permute-start.6) | collective-permute-done | bytes 639008 | tf_op jit(solution)/shard_map/ppermute | solution.py:194
  78.0 6.4 %shard_map.91 = f32[4,256,512]{2,1,0:T(8,128)S(1)} custom-call(s32[6]{0:T(128)S(1)} %stack.86.where, bf16[8,256,1024]{2,1,0:T(8,128)(2,1)} %copy-done, bf16[8,256,1024]{2,1,0:T(8,128)(2,1)} %get-tuple-element.69.low, f32[2,4,32,512]{3,2,1,0:T(8,128)S(1)} %pad_maximum_fusion.3.refs_0_, f32[2,4,32,512]{3,2,1,0:T(8,128)S(1)} %collective-permute-done.3.refs_1_, ...), custom_call_target="tpu_custom_call" | custom-call | flops 3221225472 | bytes 6291456 | tf_op jit(solution)/shard_map/pallas_call | solution.py:334
  84.5 2.2 collective-permute-start.8
  88.4 6.4 %shard_map.90 = f32[4,256,512]{2,1,0:T(8,128)S(1)} custom-call(s32[6]{0:T(128)S(1)} %stack.86.where, bf16[8,256,1024]{2,1,0:T(8,128)(2,1)} %copy-done, bf16[8,256,1024]{2,1,0:T(8,128)(2,1)} %get-tuple-element.69.low, f32[2,4,32,512]{3,2,1,0:T(8,128)S(1)} %pad_maximum_fusion.3.refs_0_, f32[2,4,32,512]{3,2,1,0:T(8,128)S(1)} %copy-done.12, ...), custom_call_target="tpu_custom_call" | custom-call | flops 3221225472 | bytes 6291456 | tf_op jit(solution)/shard_map/pallas_call | solution.py:334
  99.3 2.4 %collective-permute-start.11 = (f32[4,56,512]{2,1,0:T(8,128)S(1)}, f32[4,56,512]{2,1,0:T(8,128)S(1)}, u32[]{:S(2)}, u32[]{:S(2)}) collective-permute-start(f32[4,56,512]{2,1,0:T(8,128)S(1)} %slice.54), channel_id=1, source_target_pairs={{0,16},{1,17},{2,18},{3,19},{4,20},{5,21},{6,22},{7,23},{8,24},{9,... | collective-permute-start | bytes 1376264 | tf_op jit(solution)/shard_map/ppermute | solution.py:194
  103.6 11.8 %shard_map.92 = (f32[4,64,512]{2,1,0:T(8,128)S(1)}, f32[4,64,512]{2,1,0:T(8,128)}, f32[4,64,512]{2,1,0:T(8,128)}, f32[4,64,512]{2,1,0:T(8,128)}) custom-call(s32[6]{0:T(128)S(1)} %stack.86.where, bf16[1024,2048]{1,0:T(8,128)(2,1)} %copy-done.13, bf16[1024,2048]{1,0:T(8,128)(2,1)} %get-tuple-element.82.low, f32[4,312,512]{2,1,0:T(8,128)S(1)} %pad_maximum_fusion.near, ...), custom_call_target="tpu_custom_call" | custom-call | flops 6442450944 | bytes 12582912 | tf_op jit(solution)/shard_map/pallas_call | solution.py:399
  115.4 6.6 %collective-permute-done.11 = f32[4,56,512]{2,1,0:T(8,128)S(1)} collective-permute-done((f32[4,56,512]{2,1,0:T(8,128)S(1)}, f32[4,56,512]{2,1,0:T(8,128)S(1)}, u32[]{:S(2)}, u32[]{:S(2)}) %collective-permute-start.11) | collective-permute-done | bytes 458784 | tf_op jit(solution)/shard_map/ppermute | solution.py:194
  131.9 4.7 %shard_map.93 = (bf16[14,256,256]{2,1,0:T(8,128)(2,1)S(1)}, bf16[14,256,256]{2,1,0:T(8,128)(2,1)}) custom-call(s32[3]{0:T(128)S(1)} %add_add_fusion.2.where, f32[4,312,512]{2,1,0:T(8,128)} %copy-done.1, f32[3,4,56,512]{3,2,1,0:T(8,128)S(1)} %pad_maximum_fusion.1.planes, f32[4,312,512]{2,1,0:T(8,128)} %copy-done.20, ...), custom_call_target="tpu_custom_call" | custom-call | bytes 11010048 | tf_op jit(solution)/shard_map/pallas_call | solution.py:452
  139.0 11.0 %collective-permute-done.15 = f32[4,64,512]{2,1,0:T(8,128)} collective-permute-done((f32[4,64,512]{2,1,0:T(8,128)}, f32[4,64,512]{2,1,0:T(8,128)}, u32[]{:S(2)}, u32[]{:S(2)}) %collective-permute-start.15) | collective-permute-done | bytes 524320 | tf_op jit(solution)/shard_map/ppermute | solution.py:194
  154.5 11.9 %collective-permute-done.19.refs_2_ = f32[4,32,512]{2,1,0:T(8,128)S(1)} collective-permute-done((f32[4,32,512]{2,1,0:T(8,128)S(1)}, f32[4,32,512]{2,1,0:T(8,128)S(1)}, u32[]{:S(2)}, u32[]{:S(2)}) %collective-permute-start.19) | collective-permute-done | bytes 262176 | tf_op jit(solution)/shard_map/ppermute | solution.py:194
  166.5 10.1 %shard_map.94 = (f32[256,256]{1,0:T(8,128)S(1)}, f32[256,256]{1,0:T(8,128)S(1)}, f32[7,256,256]{2,1,0:T(8,128)}, f32[7,4,32,256]{3,2,1,0:T(8,128)S(1)}, f32[7,4,32,256]{3,2,1,0:T(8,128)S(1)}) custom-call(s32[3]{0:T(128)S(1)} %add_add_fusion.1.refs_0_, f32[4,32,512]{2,1,0:T(8,128)S(1)} %collective-permute-done.18.refs_1_, ...), custom_call_target="tpu_custom_call" | custom-call | flops 4026531840 | bytes 10485760 | tf_op jit(solution)/shard_map/pallas_call | solution.py:586
  176.6 4.4 %collective-permute-start.23 = (f32[7,4,32,256]{3,2,1,0:T(8,128)S(1)}, f32[7,4,32,256]{3,2,1,0:T(8,128)S(1)}, u32[]{:S(2)}, u32[]{:S(2)}) collective-permute-start(f32[7,4,32,256]{3,2,1,0:T(8,128)S(1)} %get-tuple-element.109), channel_id=1, source_target_pairs={{0,1},{1,0},{2,3},{3,2},{4,5},{5,4},{6,7},{7,6},{8,9},{9,8},{10,11... | collective-permute-start | bytes 2752520 | tf_op jit(solution)/shard_map/ppermute | solution.py:194
  188.4 8.3 %shard_map.95 = (f32[2048,128]{1,0:T(8,128)}, f32[3,4,32,256]{3,2,1,0:T(8,128)S(1)}, f32[3,4,32,256]{3,2,1,0:T(8,128)S(1)}) custom-call(s32[3]{0:T(128)S(1)} %add_add_fusion.1.refs_0_, f32[256,512]{1,0:T(8,128)S(1)} %bitcast_add_fusion.refs_1_, f32[2048,128]{1,0:T(8,128)S(1)} %bitcast.124, f32[2048,128]{1,0:T(8,128)S(1)} %bitcast.121, ...), custom_call_target="tpu_custom_call" | custom-call | flops 4026531840 | bytes 10485760 | tf_op jit(solution)/shard_map/pallas_call | solution.py:586
  200.0 2.6 %collective-permute-start.30 = (f32[3,4,8,256]{3,2,1,0:T(8,128)S(1)}, f32[3,4,8,256]{3,2,1,0:T(8,128)S(1)}, u32[]{:S(2)}, u32[]{:S(2)}) collective-permute-start(f32[3,4,8,256]{3,2,1,0:T(8,128)S(1)} %get-tuple-element.139), channel_id=1, source_target_pairs={{0,24},{1,25},{2,26},{3,27},{4,28},{5,29},{6,30},{7,31},{8,16},{9,... | collective-permute-start | bytes 294920 | tf_op jit(solution)/shard_map/ppermute | solution.py:194
  205.2 2.4 %collective-permute-done.30 = f32[3,4,8,256]{3,2,1,0:T(8,128)S(1)} collective-permute-done((f32[3,4,8,256]{3,2,1,0:T(8,128)S(1)}, f32[3,4,8,256]{3,2,1,0:T(8,128)S(1)}, u32[]{:S(2)}, u32[]{:S(2)}) %collective-permute-start.30) | collective-permute-done | bytes 98336 | tf_op jit(solution)/shard_map/ppermute | solution.py:194
  209.3 4.1 %collective-permute-start.32 = (f32[10,8,256]{2,1,0:T(8,128)S(1)}, f32[10,8,256]{2,1,0:T(8,128)S(1)}, u32[]{:S(2)}, u32[]{:S(2)}) collective-permute-start(f32[10,8,256]{2,1,0:T(8,128)S(1)} %get-tuple-element.146), channel_id=1, source_target_pairs={{0,4},{1,5},{2,6},{3,7},{4,0},{5,1},{6,2},{7,3},{8,12},{9,13},{10,... | collective-permute-start | bytes 245768 | tf_op jit(solution)/shard_map/ppermute | solution.py:194
  213.8 6.0 %collective-permute-done.32 = f32[10,8,256]{2,1,0:T(8,128)S(1)} collective-permute-done((f32[10,8,256]{2,1,0:T(8,128)S(1)}, f32[10,8,256]{2,1,0:T(8,128)S(1)}, u32[]{:S(2)}, u32[]{:S(2)}) %collective-permute-start.32) | collective-permute-done | bytes 81952 | tf_op jit(solution)/shard_map/ppermute | solution.py:194
  (135 shorter events, 57.2 us)
Async XLA Ops:
  2.1 44.4 %collective-permute-start.2 = (f32[312,512]{1,0:T(8,128)S(1)}, f32[312,512]{1,0:T(8,128)S(1)}, u32[]{:S(2)}, u32[]{:S(2)}) collective-permute-start(f32[312,512]{1,0:T(8,128)S(1)} %shard_map.88), channel_id=1, source_target_pairs={{0,2},{1,3},{2,0},{3,1},{4,6},{5,7},{6,4},{7,5},{8,10},{9,11},{10,... | collective-permute-start | bytes 1916936 | tf_op jit(solution)/shard_map/ppermute | solution.py:194
  5.4 20.1 %collective-permute-start = (f32[4,32,512]{2,1,0:T(8,128)S(1)}, f32[4,32,512]{2,1,0:T(8,128)S(1)}, u32[]{:S(2)}, u32[]{:S(2)}) collective-permute-start(f32[4,32,512]{2,1,0:T(8,128)S(1)} %get-tuple-element.64), channel_id=1, source_target_pairs={{0,0},{8,1},{20,2},{28,3},{3,4},{11,5},{23,6},{31,7},{2,8},{10,9},... | collective-permute-start | bytes 786440 | tf_op jit(solution)/shard_map/ppermute | solution.py:194
  6.1 19.6 %collective-permute-start.1 = (f32[4,32,512]{2,1,0:T(8,128)S(1)}, f32[4,32,512]{2,1,0:T(8,128)S(1)}, u32[]{:S(2)}, u32[]{:S(2)}) collective-permute-start(f32[4,32,512]{2,1,0:T(8,128)S(1)} %get-tuple-element.65), channel_id=1, source_target_pairs={{1,0},{9,1},{21,2},{29,3},{2,4},{10,5},{22,6},{30,7},{3,8},{11,9},... | collective-permute-start | bytes 786440 | tf_op jit(solution)/shard_map/ppermute | solution.py:194
  13.1 56.3 %collective-permute-start.7 = (f32[312,512]{1,0:T(8,128)S(1)}, f32[312,512]{1,0:T(8,128)}, u32[]{:S(2)}, u32[]{:S(2)}) collective-permute-start(f32[312,512]{1,0:T(8,128)S(1)} %shard_map.88), channel_id=1, source_target_pairs={{0,6},{1,7},{2,4},{3,5},{4,2},{5,3},{6,0},{7,1},{8,14},{9,15},{10,... | collective-permute-start | bytes 1916936 | tf_op jit(solution)/shard_map/ppermute | solution.py:194
  15.0 63.0 %collective-permute-start.6 = (f32[312,512]{1,0:T(8,128)S(1)}, f32[312,512]{1,0:T(8,128)}, u32[]{:S(2)}, u32[]{:S(2)}) collective-permute-start(f32[312,512]{1,0:T(8,128)S(1)} %shard_map.88), channel_id=1, source_target_pairs={{0,4},{1,5},{2,6},{3,7},{4,0},{5,1},{6,2},{7,3},{8,12},{9,13},{10,... | collective-permute-start | bytes 1916936 | tf_op jit(solution)/shard_map/ppermute | solution.py:194
  46.5 31.4 %collective-permute-start.5 = (f32[2,4,32,512]{3,2,1,0:T(8,128)S(1)}, f32[2,4,32,512]{3,2,1,0:T(8,128)S(1)}, u32[]{:S(2)}, u32[]{:S(2)}) collective-permute-start(f32[2,4,32,512]{3,2,1,0:T(8,128)S(1)} %pad_maximum_fusion.3.refs_0_), channel_id=1, source_target_pairs={{0,24},{1,25},{2,26},{3,27},{4,28},{5,29},{6,30},{7,31},{8,16},{9,... | collective-permute-start | bytes 1572872 | tf_op jit(solution)/shard_map/ppermute | solution.py:194
  46.5 31.4 %collective-permute-start.4 = (f32[2,4,32,512]{3,2,1,0:T(8,128)S(1)}, f32[2,4,32,512]{3,2,1,0:T(8,128)S(1)}, u32[]{:S(2)}, u32[]{:S(2)}) collective-permute-start(f32[2,4,32,512]{3,2,1,0:T(8,128)S(1)} %pad_maximum_fusion.3.refs_0_), channel_id=1, source_target_pairs={{0,16},{1,17},{2,18},{3,19},{4,20},{5,21},{6,22},{7,23},{8,24},{9,... | collective-permute-start | bytes 1572872 | tf_op jit(solution)/shard_map/ppermute | solution.py:194
  55.2 22.8 %collective-permute-start.3 = (f32[2,4,32,512]{3,2,1,0:T(8,128)S(1)}, f32[2,4,32,512]{3,2,1,0:T(8,128)S(1)}, u32[]{:S(2)}, u32[]{:S(2)}) collective-permute-start(f32[2,4,32,512]{3,2,1,0:T(8,128)S(1)} %pad_maximum_fusion.3.refs_0_), channel_id=1, source_target_pairs={{0,8},{1,9},{2,10},{3,11},{4,12},{5,13},{6,14},{7,15},{8,0},{9,1},... | collective-permute-start | bytes 1572872 | tf_op jit(solution)/shard_map/ppermute | solution.py:194
  88.3 13.8 %collective-permute-start.9 = (f32[4,312,512]{2,1,0:T(8,128)S(1)}, f32[4,312,512]{2,1,0:T(8,128)S(1)}, u32[]{:S(2)}, u32[]{:S(2)}) collective-permute-start(f32[4,312,512]{2,1,0:T(8,128)S(1)} %pad_maximum_fusion.near), channel_id=1, source_target_pairs={{0,1},{1,0},{2,3},{3,2},{4,5},{5,4},{6,7},{7,6},{8,9},{9,8},{10,11... | collective-permute-start | bytes 7667720 | tf_op jit(solution)/shard_map/ppermute | solution.py:194
  97.1 24.9 %collective-permute-start.13 = (f32[2,256,512]{2,1,0:T(8,128)S(1)}, f32[2,256,512]{2,1,0:T(8,128)S(1)}, u32[]{:S(2)}, u32[]{:S(2)}) collective-permute-start(f32[2,256,512]{2,1,0:T(8,128)S(1)} %pad_maximum_fusion.2), channel_id=1, source_target_pairs={{0,2},{1,3},{6,4},{7,5},{8,10},{9,11},{14,12},{15,13},{16,18},{17,... | collective-permute-start | bytes 3145736 | tf_op jit(solution)/shard_map/ppermute | solution.py:194
  98.5 16.8 %collective-permute-start.12 = (f32[4,56,512]{2,1,0:T(8,128)S(1)}, f32[4,56,512]{2,1,0:T(8,128)S(1)}, u32[]{:S(2)}, u32[]{:S(2)}) collective-permute-start(f32[4,56,512]{2,1,0:T(8,128)S(1)} %slice.54), channel_id=1, source_target_pairs={{0,24},{1,25},{2,26},{3,27},{4,28},{5,29},{6,30},{7,31},{8,16},{9,... | collective-permute-start | bytes 1376264 | tf_op jit(solution)/shard_map/ppermute | solution.py:194
  99.3 22.7 %collective-permute-start.11 = (f32[4,56,512]{2,1,0:T(8,128)S(1)}, f32[4,56,512]{2,1,0:T(8,128)S(1)}, u32[]{:S(2)}, u32[]{:S(2)}) collective-permute-start(f32[4,56,512]{2,1,0:T(8,128)S(1)} %slice.54), channel_id=1, source_target_pairs={{0,16},{1,17},{2,18},{3,19},{4,20},{5,21},{6,22},{7,23},{8,24},{9,... | collective-permute-start | bytes 1376264 | tf_op jit(solution)/shard_map/ppermute | solution.py:194
  101.7 20.3 %collective-permute-start.10 = (f32[4,56,512]{2,1,0:T(8,128)S(1)}, f32[4,56,512]{2,1,0:T(8,128)S(1)}, u32[]{:S(2)}, u32[]{:S(2)}) collective-permute-start(f32[4,56,512]{2,1,0:T(8,128)S(1)} %slice.54), channel_id=1, source_target_pairs={{0,8},{1,9},{2,10},{3,11},{4,12},{5,13},{6,14},{7,15},{8,0},{9,1},... | collective-permute-start | bytes 1376264 | tf_op jit(solution)/shard_map/ppermute | solution.py:194
  123.2 15.1 %collective-permute-start.14 = (f32[4,64,512]{2,1,0:T(8,128)}, f32[4,64,512]{2,1,0:T(8,128)}, u32[]{:S(2)}, u32[]{:S(2)}) collective-permute-start(f32[4,64,512]{2,1,0:T(8,128)} %get-tuple-element.92), channel_id=1, source_target_pairs={{0,8},{1,9},{2,10},{3,11},{4,12},{5,13},{6,14},{7,15},{8,0},{9,1},... | collective-permute-start | bytes 1572872 | tf_op jit(solution)/shard_map/ppermute | solution.py:194
  124.4 25.5 %collective-permute-start.15 = (f32[4,64,512]{2,1,0:T(8,128)}, f32[4,64,512]{2,1,0:T(8,128)}, u32[]{:S(2)}, u32[]{:S(2)}) collective-permute-start(f32[4,64,512]{2,1,0:T(8,128)} %get-tuple-element.93), channel_id=1, source_target_pairs={{0,16},{1,17},{2,18},{3,19},{4,20},{5,21},{6,22},{7,23},{8,24},{9,... | collective-permute-start | bytes 1572872 | tf_op jit(solution)/shard_map/ppermute | solution.py:194
  125.5 24.5 %collective-permute-start.16 = (f32[4,64,512]{2,1,0:T(8,128)}, f32[4,64,512]{2,1,0:T(8,128)}, u32[]{:S(2)}, u32[]{:S(2)}) collective-permute-start(f32[4,64,512]{2,1,0:T(8,128)} %get-tuple-element.94), channel_id=1, source_target_pairs={{0,24},{1,25},{2,26},{3,27},{4,28},{5,29},{6,30},{7,31},{8,16},{9,... | collective-permute-start | bytes 1572872 | tf_op jit(solution)/shard_map/ppermute | solution.py:194
  126.8 27.6 %collective-permute-start.22 = (f32[256,512]{1,0:T(8,128)}, f32[256,512]{1,0:T(8,128)S(1)}, u32[]{:S(2)}, u32[]{:S(2)}) collective-permute-start(f32[256,512]{1,0:T(8,128)} %get-tuple-element.126), channel_id=1, source_target_pairs={{0,2},{1,3},{2,0},{3,1},{4,6},{5,7},{6,4},{7,5},{8,10},{9,11},{10,... | collective-permute-start | bytes 1572872 | tf_op jit(solution)/shard_map/ppermute | solution.py:194
  130.6 23.9 %collective-permute-start.21 = (f32[256,512]{1,0:T(8,128)S(1)}, f32[256,512]{1,0:T(8,128)S(1)}, u32[]{:S(2)}, u32[]{:S(2)}) collective-permute-start(f32[256,512]{1,0:T(8,128)S(1)} %get-tuple-element.129), channel_id=1, source_target_pairs={{2,6},{3,7},{4,0},{5,1},{10,14},{11,15},{12,8},{13,9},{18,22},{19,... | collective-permute-start | bytes 1572872 | tf_op jit(solution)/shard_map/ppermute | solution.py:194
  138.3 16.2 %collective-permute-start.20 = (f32[256,512]{1,0:T(8,128)S(1)}, f32[256,512]{1,0:T(8,128)S(1)}, u32[]{:S(2)}, u32[]{:S(2)}) collective-permute-start(f32[256,512]{1,0:T(8,128)S(1)} %get-tuple-element.130), channel_id=1, source_target_pairs={{2,4},{3,5},{4,2},{5,3},{10,12},{11,13},{12,10},{13,11},{18,20},{1... | collective-permute-start | bytes 1572872 | tf_op jit(solution)/shard_map/ppermute | solution.py:194
  151.6 14.8 %collective-permute-start.19 = (f32[4,32,512]{2,1,0:T(8,128)S(1)}, f32[4,32,512]{2,1,0:T(8,128)S(1)}, u32[]{:S(2)}, u32[]{:S(2)}) collective-permute-start(f32[4,32,512]{2,1,0:T(8,128)S(1)} %get-tuple-element.134), channel_id=1, source_target_pairs={{0,1},{1,9},{2,21},{3,29},{4,2},{5,10},{6,22},{7,30},{8,3},{9,11},... | collective-permute-start | bytes 786440 | tf_op jit(solution)/shard_map/ppermute | solution.py:194
  153.5 12.9 %collective-permute-start.18 = (f32[4,32,512]{2,1,0:T(8,128)S(1)}, f32[4,32,512]{2,1,0:T(8,128)S(1)}, u32[]{:S(2)}, u32[]{:S(2)}) collective-permute-start(f32[4,32,512]{2,1,0:T(8,128)S(1)} %get-tuple-element.135), channel_id=1, source_target_pairs={{0,0},{1,8},{2,20},{3,28},{4,3},{5,11},{6,23},{7,31},{8,2},{9,10},... | collective-permute-start | bytes 786440 | tf_op jit(solution)/shard_map/ppermute | solution.py:194
  183.3 13.4 %collective-permute-start.24 = (f32[7,4,8,256]{3,2,1,0:T(8,128)S(1)}, f32[7,4,8,256]{3,2,1,0:T(8,128)S(1)}, u32[]{:S(2)}, u32[]{:S(2)}) collective-permute-start(f32[7,4,8,256]{3,2,1,0:T(8,128)S(1)} %get-tuple-element.131), channel_id=1, source_target_pairs={{0,8},{1,9},{2,10},{3,11},{4,12},{5,13},{6,14},{7,15},{8,0},{9,1},... | collective-permute-start | bytes 688136 | tf_op jit(solution)/shard_map/ppermute | solution.py:194
  183.4 13.3 %collective-permute-start.26 = (f32[7,4,8,256]{3,2,1,0:T(8,128)S(1)}, f32[7,4,8,256]{3,2,1,0:T(8,128)S(1)}, u32[]{:S(2)}, u32[]{:S(2)}) collective-permute-start(f32[7,4,8,256]{3,2,1,0:T(8,128)S(1)} %get-tuple-element.132), channel_id=1, source_target_pairs={{0,24},{1,25},{2,26},{3,27},{4,28},{5,29},{6,30},{7,31},{8,16},{9,... | collective-permute-start | bytes 688136 | tf_op jit(solution)/shard_map/ppermute | solution.py:194
  185.3 12.2 %collective-permute-start.25 = (f32[7,4,8,256]{3,2,1,0:T(8,128)S(1)}, f32[7,4,8,256]{3,2,1,0:T(8,128)S(1)}, u32[]{:S(2)}, u32[]{:S(2)}) collective-permute-start(f32[7,4,8,256]{3,2,1,0:T(8,128)S(1)} %get-tuple-element.133), channel_id=1, source_target_pairs={{0,16},{1,17},{2,18},{3,19},{4,20},{5,21},{6,22},{7,23},{8,24},{9,... | collective-permute-start | bytes 688136 | tf_op jit(solution)/shard_map/ppermute | solution.py:194
  (37 other events, 320.4 us)

commit v4 on v3

--- a/solution.py
+++ b/solution.py
@@ -323,26 +323,39 @@
     out[0] = dot3((high[0], low[0]), (c_high[...], c_low[...]))
 
 
-def column_product(halves, side, where, quarters):
+def column_again_body(where, high, low, c_high, c_low, out):
+    out[0] = dot3((high[0], low[0]), (c_high[...], c_low[...]))
+
+
+def column_product(halves, side, where, quarters, split_rows=None):
     unit, depth = halves[0].shape[1:]
     width = quarters[0].shape[3]
 
     def slot(i, where):
         return ((where[4] ^ i) * 2 + (where[5] ^ side), 0, 0)
 
-    whole = [pl.BlockSpec(q.shape, lambda i, where: (0, 0, 0, 0)) for q in quarters]
+    rows_spec = pl.BlockSpec((depth, width), lambda i, where: (0, 0))
+    out_spec = pl.BlockSpec((1, unit, width), lambda i, where: (i, 0, 0))
+    out_shape = struct(NZ, unit, width)
+    cost = (6 * NZ * unit * depth * width, NZ * unit * depth * 4 + depth * width * 4)
+    given = quarters if split_rows is None else split_rows
+    if split_rows is None:
+        specs = [pl.BlockSpec(q.shape, lambda i, where: (0, 0, 0, 0)) for q in quarters]
+        out_spec = [out_spec, rows_spec, rows_spec]
+        out_shape = [out_shape] + [struct(depth, width, dtype=jnp.bfloat16)] * 2
+    else:
+        specs = [rows_spec, rows_spec]
     return call(
-        column_body,
-        struct(NZ, unit, width),
-        (6 * NZ * unit * depth * width, NZ * unit * depth * 4 + depth * width * 4),
+        column_body if split_rows is None else column_again_body,
+        out_shape,
+        cost,
         grid_spec=pltpu.PrefetchScalarGridSpec(
             num_scalar_prefetch=1,
             grid=(NZ,),
-            in_specs=[pl.BlockSpec((1, unit, depth), slot)] * 2 + whole,
-            out_specs=pl.BlockSpec((1, unit, width), lambda i, where: (i, 0, 0)),
-            scratch_shapes=[pltpu.VMEM((depth, width), jnp.bfloat16)] * 2,
+            in_specs=[pl.BlockSpec((1, unit, depth), slot)] * 2 + specs,
+            out_specs=out_spec,
         ),
-    )(where, *halves, *quarters)
+    )(where, *halves, *given)
 
 
 def turn_body(block, high, low):
@@ -634,10 +647,10 @@
     spread, turned, line = barrier((spread, turned, line))
 
     near = jnp.stack(line)
-    leaving = column_product(halves, 1, quarters, spread)
+    leaving, *split_rows = column_product(halves, 1, quarters, spread)
     arriving = move(leaving, CORE)
     far = move(near, CORE)
-    staying = column_product(halves, 0, quarters, spread)
+    staying = column_product(halves, 0, quarters, spread, split_rows)
     staying, arriving = barrier((staying, arriving))
 
     term = [staying[d] + arriving[d] for d in range(NZ)]
@@ -673,7 +686,6 @@
         GROUPS[0], (), where, (same, cross), views, top, adjoint_top, (), ()
     )
     kept = keep + move(send, CORE)
-    kept, folded = barrier((kept, folded))
     second_image = term[0] + sum(folded)
     strip = strips(kept)
     low_out, keep, send = panel_group(

time: 229 us -> 229 us (level)
    unnamed x48 -> x32, local copies, waits for them, and re-layouts: 7.38 us -> 7.19 us
  transfers between devices with their start and end apart: 37 -> 37, of which waited for: 17 -> 18; matrix products, arithmetic and copies ran while one was open for 5% -> 5% of each run, Pallas kernels for 21% -> 21%
where the time goes in v4:
time: 229 us; the launch traced here: 228 us
  waiting for transfers between devices  81.4 us (36%)
  Pallas kernels  65.9 us (29%)
  starting transfers between devices  59 us (26%)
  local copies, waits for them, and re-layouts  10.7 us (5%)
  other arithmetic  10.4 us (5%)
    ppermute x37, waiting for transfers between devices, move(): return lax.ppermute(array, AXES, pairs)  81.4 us
    ppermute x37, starting transfers between devices, move(): return lax.ppermute(array, AXES, pairs)  59 us
    pallas_call x2, Pallas kernels, panel_group(): call(lambda *refs: panel_body(panels, done, len(images), *refs), out, (wo...  18.4 us
    pallas_call x2, Pallas kernels, column_product(): call(column_body if split_rows is None else column_again_body, out_shape,...  13.5 us
    pallas_call x1, Pallas kernels, product(): call(product_body, [struct(steps, span, width)] * 4, (6 * rows * depth *...  11.8 us
    pallas_call x1, Pallas kernels, turn(): call(turn_body, (shape, shape), (0, 2 * trail.size * 4), grid=(slots,), i...  8.87 us
    pallas_call x1, Pallas kernels, halve(): call(halve_body, (shape, shape), (0, 2 * trail.size * 4), grid=(slots,),...  8.31 us
    unnamed x32, local copies, waits for them, and re-layouts  7.19 us
  transfers between devices with their start and end apart: 37, of which 18 were waited for; matrix products, arithmetic and copies ran while one was open for 5% of the time, Pallas kernels for 21%

profile of v4, /device:TPU:0, one launch (start us, length us, event | category | flops | bytes accessed | tf_op | source)
XLA Modules:
  0.0 228.3 jit_solution(2936437496671592203)
XLA Ops:
  2.1 3.1 %collective-permute-start.2 = (f32[312,512]{1,0:T(8,128)S(1)}, f32[312,512]{1,0:T(8,128)S(1)}, u32[]{:S(2)}, u32[]{:S(2)}) collective-permute-start(f32[312,512]{1,0:T(8,128)S(1)} %shard_map.88), channel_id=1, source_target_pairs={{0,2},{1,3},{2,0},{3,1},{4,6},{5,7},{6,4},{7,5},{8,10},{9,11},{10,... | collective-permute-start | bytes 1916936 | tf_op jit(solution)/shard_map/ppermute | solution.py:194
  6.0 7.1 %collective-permute-start.1 = (f32[4,32,512]{2,1,0:T(8,128)S(1)}, f32[4,32,512]{2,1,0:T(8,128)S(1)}, u32[]{:S(2)}, u32[]{:S(2)}) collective-permute-start(f32[4,32,512]{2,1,0:T(8,128)S(1)} %get-tuple-element.64), channel_id=1, source_target_pairs={{1,0},{9,1},{21,2},{29,3},{2,4},{10,5},{22,6},{30,7},{3,8},{11,9},... | collective-permute-start | bytes 786440 | tf_op jit(solution)/shard_map/ppermute | solution.py:194
  15.2 8.3 %shard_map.87 = (bf16[8,256,1024]{2,1,0:T(8,128)(2,1)S(1)}, bf16[8,256,1024]{2,1,0:T(8,128)(2,1)}) custom-call(f32[8,8,256,128]{3,2,1,0:T(8,128)} %bitcast.126), custom_call_target="tpu_custom_call" | custom-call | bytes 16777216 | tf_op jit(solution)/shard_map/pallas_call | solution.py:299
  25.7 20.8 %collective-permute-done.2 = f32[312,512]{1,0:T(8,128)S(1)} collective-permute-done((f32[312,512]{1,0:T(8,128)S(1)}, f32[312,512]{1,0:T(8,128)S(1)}, u32[]{:S(2)}, u32[]{:S(2)}) %collective-permute-start.2) | collective-permute-done | bytes 639008 | tf_op jit(solution)/shard_map/ppermute | solution.py:194
  46.5 8.7 %collective-permute-start.4 = (f32[2,4,32,512]{3,2,1,0:T(8,128)S(1)}, f32[2,4,32,512]{3,2,1,0:T(8,128)S(1)}, u32[]{:S(2)}, u32[]{:S(2)}) collective-permute-start(f32[2,4,32,512]{3,2,1,0:T(8,128)S(1)} %pad_maximum_fusion.3.refs_0_), channel_id=1, source_target_pairs={{0,16},{1,17},{2,18},{3,19},{4,20},{5,21},{6,22},{7,23},{8,24},{9,... | collective-permute-start | bytes 1572872 | tf_op jit(solution)/shard_map/ppermute | solution.py:194
  55.2 8.9 %shard_map.89 = (bf16[1024,2048]{1,0:T(8,128)(2,1)S(1)}, bf16[1024,2048]{1,0:T(8,128)(2,1)}) custom-call(f32[8,8,256,128]{3,2,1,0:T(8,128)} %bitcast.127), custom_call_target="tpu_custom_call" | custom-call | bytes 16777216 | tf_op jit(solution)/shard_map/pallas_call | solution.py:376
  66.7 2.6 %stack.86.where = s32[6]{0:T(128)S(1)} concatenate(s32[1]{0:T(128)} %bitcast.3, s32[1]{0:T(128)} %bitcast.4, s32[1]{0:T(128)} %bitcast.5, s32[1]{0:T(128)} %bitcast.6, s32[1]{0:T(128)} %bitcast.7, s32[1]{0:T(128)} %bitcast.2.refs_0_), dimensions={0} | concatenate | bytes 48 | tf_op jit(solution)/shard_map/stack | solution.py:622
  69.4 8.6 %collective-permute-done.6 = f32[312,512]{1,0:T(8,128)} collective-permute-done((f32[312,512]{1,0:T(8,128)S(1)}, f32[312,512]{1,0:T(8,128)}, u32[]{:S(2)}, u32[]{:S(2)}) %collective-permute-start.6) | collective-permute-done | bytes 639008 | tf_op jit(solution)/shard_map/ppermute | solution.py:194
  78.0 7.3 %shard_map.90 = (f32[4,256,512]{2,1,0:T(8,128)}, bf16[1024,512]{1,0:T(8,128)(2,1)S(1)}, bf16[1024,512]{1,0:T(8,128)(2,1)S(1)}) custom-call(s32[6]{0:T(128)S(1)} %stack.86.where, bf16[8,256,1024]{2,1,0:T(8,128)(2,1)} %copy-done.4, bf16[8,256,1024]{2,1,0:T(8,128)(2,1)} %get-tuple-element.68.low, f32[2,4,32,512]{3,2,1,0:T(8,128)S(1)} %pad_maximum_fusion.3.refs_0_, ...), custom_call_target="tpu_custom_call" | custom-call | flops 3221225472 | bytes 6291456 | tf_op jit(solution)/shard_map/pallas_call | solution.py:348
  89.0 6.2 %shard_map.91 = f32[4,256,512]{2,1,0:T(8,128)S(1)} custom-call(s32[6]{0:T(128)S(1)} %stack.86.where, bf16[8,256,1024]{2,1,0:T(8,128)(2,1)} %copy-done.4, bf16[8,256,1024]{2,1,0:T(8,128)(2,1)} %get-tuple-element.68.low, bf16[1024,512]{1,0:T(8,128)(2,1)S(1)} %get-tuple-element.78.c_high, bf16[1024,512]{1,0:T(8,128)(2,1)S(1)} %get-tuple-element.79.c_low), custom_call_target="tpu_custom_call" | custom-call | flops 3221225472 | bytes 6291456 | tf_op jit(solution)/shard_map/pallas_call | solution.py:348
  99.5 2.4 %collective-permute-start.11 = (f32[4,56,512]{2,1,0:T(8,128)S(1)}, f32[4,56,512]{2,1,0:T(8,128)S(1)}, u32[]{:S(2)}, u32[]{:S(2)}) collective-permute-start(f32[4,56,512]{2,1,0:T(8,128)S(1)} %slice.54), channel_id=1, source_target_pairs={{0,16},{1,17},{2,18},{3,19},{4,20},{5,21},{6,22},{7,23},{8,24},{9,... | collective-permute-start | bytes 1376264 | tf_op jit(solution)/shard_map/ppermute | solution.py:194
  103.8 11.8 %shard_map.92 = (f32[4,64,512]{2,1,0:T(8,128)S(1)}, f32[4,64,512]{2,1,0:T(8,128)}, f32[4,64,512]{2,1,0:T(8,128)}, f32[4,64,512]{2,1,0:T(8,128)}) custom-call(s32[6]{0:T(128)S(1)} %stack.86.where, bf16[1024,2048]{1,0:T(8,128)(2,1)} %copy-done.5, bf16[1024,2048]{1,0:T(8,128)(2,1)} %get-tuple-element.84.low, f32[4,312,512]{2,1,0:T(8,128)S(1)} %pad_maximum_fusion.near, ...), custom_call_target="tpu_custom_call" | custom-call | flops 6442450944 | bytes 12582912 | tf_op jit(solution)/shard_map/pallas_call | solution.py:412
  115.6 6.7 %collective-permute-done.11 = f32[4,56,512]{2,1,0:T(8,128)S(1)} collective-permute-done((f32[4,56,512]{2,1,0:T(8,128)S(1)}, f32[4,56,512]{2,1,0:T(8,128)S(1)}, u32[]{:S(2)}, u32[]{:S(2)}) %collective-permute-start.11) | collective-permute-done | bytes 458784 | tf_op jit(solution)/shard_map/ppermute | solution.py:194
  132.1 4.7 %shard_map.93 = (bf16[14,256,256]{2,1,0:T(8,128)(2,1)S(1)}, bf16[14,256,256]{2,1,0:T(8,128)(2,1)}) custom-call(s32[3]{0:T(128)S(1)} %add_add_fusion.2.where, f32[4,312,512]{2,1,0:T(8,128)} %copy-done, f32[3,4,56,512]{3,2,1,0:T(8,128)S(1)} %pad_maximum_fusion.1.planes, f32[4,312,512]{2,1,0:T(8,128)} %copy-done.12, ...), custom_call_target="tpu_custom_call" | custom-call | bytes 11010048 | tf_op jit(solution)/shard_map/pallas_call | solution.py:465
  139.3 11.0 %collective-permute-done.15 = f32[4,64,512]{2,1,0:T(8,128)} collective-permute-done((f32[4,64,512]{2,1,0:T(8,128)}, f32[4,64,512]{2,1,0:T(8,128)}, u32[]{:S(2)}, u32[]{:S(2)}) %collective-permute-start.15) | collective-permute-done | bytes 524320 | tf_op jit(solution)/shard_map/ppermute | solution.py:194
  154.7 12.2 %collective-permute-done.19.refs_2_ = f32[4,32,512]{2,1,0:T(8,128)S(1)} collective-permute-done((f32[4,32,512]{2,1,0:T(8,128)S(1)}, f32[4,32,512]{2,1,0:T(8,128)S(1)}, u32[]{:S(2)}, u32[]{:S(2)}) %collective-permute-start.19) | collective-permute-done | bytes 262176 | tf_op jit(solution)/shard_map/ppermute | solution.py:194
  166.9 10.1 %shard_map.94 = (f32[256,256]{1,0:T(8,128)S(1)}, f32[256,256]{1,0:T(8,128)S(1)}, f32[7,256,256]{2,1,0:T(8,128)}, f32[7,4,32,256]{3,2,1,0:T(8,128)S(1)}, f32[7,4,32,256]{3,2,1,0:T(8,128)S(1)}) custom-call(s32[3]{0:T(128)S(1)} %add_add_fusion.1.refs_0_, f32[4,32,512]{2,1,0:T(8,128)S(1)} %collective-permute-done.18.refs_1_, ...), custom_call_target="tpu_custom_call" | custom-call | flops 4026531840 | bytes 10485760 | tf_op jit(solution)/shard_map/pallas_call | solution.py:599
  177.1 4.4 %collective-permute-start.23 = (f32[7,4,32,256]{3,2,1,0:T(8,128)S(1)}, f32[7,4,32,256]{3,2,1,0:T(8,128)S(1)}, u32[]{:S(2)}, u32[]{:S(2)}) collective-permute-start(f32[7,4,32,256]{3,2,1,0:T(8,128)S(1)} %get-tuple-element.120), channel_id=1, source_target_pairs={{0,1},{1,0},{2,3},{3,2},{4,5},{5,4},{6,7},{7,6},{8,9},{9,8},{10,11... | collective-permute-start | bytes 2752520 | tf_op jit(solution)/shard_map/ppermute | solution.py:194
  187.3 8.3 %shard_map.95 = (f32[2048,128]{1,0:T(8,128)}, f32[3,4,32,256]{3,2,1,0:T(8,128)S(1)}, f32[3,4,32,256]{3,2,1,0:T(8,128)S(1)}) custom-call(s32[3]{0:T(128)S(1)} %add_add_fusion.1.refs_0_, f32[256,512]{1,0:T(8,128)S(1)} %bitcast_add_fusion.refs_1_, f32[2048,128]{1,0:T(8,128)S(1)} %bitcast.125, f32[2048,128]{1,0:T(8,128)S(1)} %bitcast.122, ...), custom_call_target="tpu_custom_call" | custom-call | flops 4026531840 | bytes 10485760 | tf_op jit(solution)/shard_map/pallas_call | solution.py:599
  200.4 2.6 %collective-permute-start.30 = (f32[3,4,8,256]{3,2,1,0:T(8,128)S(1)}, f32[3,4,8,256]{3,2,1,0:T(8,128)S(1)}, u32[]{:S(2)}, u32[]{:S(2)}) collective-permute-start(f32[3,4,8,256]{3,2,1,0:T(8,128)S(1)} %get-tuple-element.137), channel_id=1, source_target_pairs={{0,24},{1,25},{2,26},{3,27},{4,28},{5,29},{6,30},{7,31},{8,16},{9,... | collective-permute-start | bytes 294920 | tf_op jit(solution)/shard_map/ppermute | solution.py:194
  203.5 2.1 collective-permute-done.28
  205.7 2.4 %collective-permute-done.30 = f32[3,4,8,256]{3,2,1,0:T(8,128)S(1)} collective-permute-done((f32[3,4,8,256]{3,2,1,0:T(8,128)S(1)}, f32[3,4,8,256]{3,2,1,0:T(8,128)S(1)}, u32[]{:S(2)}, u32[]{:S(2)}) %collective-permute-start.30) | collective-permute-done | bytes 98336 | tf_op jit(solution)/shard_map/ppermute | solution.py:194
  209.7 4.2 %collective-permute-start.32 = (f32[10,8,256]{2,1,0:T(8,128)S(1)}, f32[10,8,256]{2,1,0:T(8,128)S(1)}, u32[]{:S(2)}, u32[]{:S(2)}) collective-permute-start(f32[10,8,256]{2,1,0:T(8,128)S(1)} %get-tuple-element.144), channel_id=1, source_target_pairs={{0,4},{1,5},{2,6},{3,7},{4,0},{5,1},{6,2},{7,3},{8,12},{9,13},{10,... | collective-permute-start | bytes 245768 | tf_op jit(solution)/shard_map/ppermute | solution.py:194
  214.2 6.0 %collective-permute-done.32 = f32[10,8,256]{2,1,0:T(8,128)S(1)} collective-permute-done((f32[10,8,256]{2,1,0:T(8,128)S(1)}, f32[10,8,256]{2,1,0:T(8,128)S(1)}, u32[]{:S(2)}, u32[]{:S(2)}) %collective-permute-start.32) | collective-permute-done | bytes 81952 | tf_op jit(solution)/shard_map/ppermute | solution.py:194
  (119 shorter events, 56.9 us)
Async XLA Ops:
  2.1 44.4 %collective-permute-start.2 = (f32[312,512]{1,0:T(8,128)S(1)}, f32[312,512]{1,0:T(8,128)S(1)}, u32[]{:S(2)}, u32[]{:S(2)}) collective-permute-start(f32[312,512]{1,0:T(8,128)S(1)} %shard_map.88), channel_id=1, source_target_pairs={{0,2},{1,3},{2,0},{3,1},{4,6},{5,7},{6,4},{7,5},{8,10},{9,11},{10,... | collective-permute-start | bytes 1916936 | tf_op jit(solution)/shard_map/ppermute | solution.py:194
  5.4 20.1 %collective-permute-start = (f32[4,32,512]{2,1,0:T(8,128)S(1)}, f32[4,32,512]{2,1,0:T(8,128)S(1)}, u32[]{:S(2)}, u32[]{:S(2)}) collective-permute-start(f32[4,32,512]{2,1,0:T(8,128)S(1)} %get-tuple-element.63), channel_id=1, source_target_pairs={{0,0},{8,1},{20,2},{28,3},{3,4},{11,5},{23,6},{31,7},{2,8},{10,9},... | collective-permute-start | bytes 786440 | tf_op jit(solution)/shard_map/ppermute | solution.py:194
  6.0 19.6 %collective-permute-start.1 = (f32[4,32,512]{2,1,0:T(8,128)S(1)}, f32[4,32,512]{2,1,0:T(8,128)S(1)}, u32[]{:S(2)}, u32[]{:S(2)}) collective-permute-start(f32[4,32,512]{2,1,0:T(8,128)S(1)} %get-tuple-element.64), channel_id=1, source_target_pairs={{1,0},{9,1},{21,2},{29,3},{2,4},{10,5},{22,6},{30,7},{3,8},{11,9},... | collective-permute-start | bytes 786440 | tf_op jit(solution)/shard_map/ppermute | solution.py:194
  13.1 56.2 %collective-permute-start.7 = (f32[312,512]{1,0:T(8,128)S(1)}, f32[312,512]{1,0:T(8,128)}, u32[]{:S(2)}, u32[]{:S(2)}) collective-permute-start(f32[312,512]{1,0:T(8,128)S(1)} %shard_map.88), channel_id=1, source_target_pairs={{0,6},{1,7},{2,4},{3,5},{4,2},{5,3},{6,0},{7,1},{8,14},{9,15},{10,... | collective-permute-start | bytes 1916936 | tf_op jit(solution)/shard_map/ppermute | solution.py:194
  15.0 63.0 %collective-permute-start.6 = (f32[312,512]{1,0:T(8,128)S(1)}, f32[312,512]{1,0:T(8,128)}, u32[]{:S(2)}, u32[]{:S(2)}) collective-permute-start(f32[312,512]{1,0:T(8,128)S(1)} %shard_map.88), channel_id=1, source_target_pairs={{0,4},{1,5},{2,6},{3,7},{4,0},{5,1},{6,2},{7,3},{8,12},{9,13},{10,... | collective-permute-start | bytes 1916936 | tf_op jit(solution)/shard_map/ppermute | solution.py:194
  46.5 31.4 %collective-permute-start.5 = (f32[2,4,32,512]{3,2,1,0:T(8,128)S(1)}, f32[2,4,32,512]{3,2,1,0:T(8,128)S(1)}, u32[]{:S(2)}, u32[]{:S(2)}) collective-permute-start(f32[2,4,32,512]{3,2,1,0:T(8,128)S(1)} %pad_maximum_fusion.3.refs_0_), channel_id=1, source_target_pairs={{0,24},{1,25},{2,26},{3,27},{4,28},{5,29},{6,30},{7,31},{8,16},{9,... | collective-permute-start | bytes 1572872 | tf_op jit(solution)/shard_map/ppermute | solution.py:194
  46.5 31.4 %collective-permute-start.4 = (f32[2,4,32,512]{3,2,1,0:T(8,128)S(1)}, f32[2,4,32,512]{3,2,1,0:T(8,128)S(1)}, u32[]{:S(2)}, u32[]{:S(2)}) collective-permute-start(f32[2,4,32,512]{3,2,1,0:T(8,128)S(1)} %pad_maximum_fusion.3.refs_0_), channel_id=1, source_target_pairs={{0,16},{1,17},{2,18},{3,19},{4,20},{5,21},{6,22},{7,23},{8,24},{9,... | collective-permute-start | bytes 1572872 | tf_op jit(solution)/shard_map/ppermute | solution.py:194
  55.2 22.8 %collective-permute-start.3 = (f32[2,4,32,512]{3,2,1,0:T(8,128)S(1)}, f32[2,4,32,512]{3,2,1,0:T(8,128)S(1)}, u32[]{:S(2)}, u32[]{:S(2)}) collective-permute-start(f32[2,4,32,512]{3,2,1,0:T(8,128)S(1)} %pad_maximum_fusion.3.refs_0_), channel_id=1, source_target_pairs={{0,8},{1,9},{2,10},{3,11},{4,12},{5,13},{6,14},{7,15},{8,0},{9,1},... | collective-permute-start | bytes 1572872 | tf_op jit(solution)/shard_map/ppermute | solution.py:194
  88.9 13.4 %collective-permute-start.9 = (f32[4,312,512]{2,1,0:T(8,128)S(1)}, f32[4,312,512]{2,1,0:T(8,128)S(1)}, u32[]{:S(2)}, u32[]{:S(2)}) collective-permute-start(f32[4,312,512]{2,1,0:T(8,128)S(1)} %pad_maximum_fusion.near), channel_id=1, source_target_pairs={{0,1},{1,0},{2,3},{3,2},{4,5},{5,4},{6,7},{7,6},{8,9},{9,8},{10,11... | collective-permute-start | bytes 7667720 | tf_op jit(solution)/shard_map/ppermute | solution.py:194
  97.4 24.9 %collective-permute-start.13 = (f32[2,256,512]{2,1,0:T(8,128)S(1)}, f32[2,256,512]{2,1,0:T(8,128)S(1)}, u32[]{:S(2)}, u32[]{:S(2)}) collective-permute-start(f32[2,256,512]{2,1,0:T(8,128)S(1)} %pad_maximum_fusion.2), channel_id=1, source_target_pairs={{0,2},{1,3},{6,4},{7,5},{8,10},{9,11},{14,12},{15,13},{16,18},{17,... | collective-permute-start | bytes 3145736 | tf_op jit(solution)/shard_map/ppermute | solution.py:194
  98.8 16.8 %collective-permute-start.12 = (f32[4,56,512]{2,1,0:T(8,128)S(1)}, f32[4,56,512]{2,1,0:T(8,128)S(1)}, u32[]{:S(2)}, u32[]{:S(2)}) collective-permute-start(f32[4,56,512]{2,1,0:T(8,128)S(1)} %slice.54), channel_id=1, source_target_pairs={{0,24},{1,25},{2,26},{3,27},{4,28},{5,29},{6,30},{7,31},{8,16},{9,... | collective-permute-start | bytes 1376264 | tf_op jit(solution)/shard_map/ppermute | solution.py:194
  99.5 22.7 %collective-permute-start.11 = (f32[4,56,512]{2,1,0:T(8,128)S(1)}, f32[4,56,512]{2,1,0:T(8,128)S(1)}, u32[]{:S(2)}, u32[]{:S(2)}) collective-permute-start(f32[4,56,512]{2,1,0:T(8,128)S(1)} %slice.54), channel_id=1, source_target_pairs={{0,16},{1,17},{2,18},{3,19},{4,20},{5,21},{6,22},{7,23},{8,24},{9,... | collective-permute-start | bytes 1376264 | tf_op jit(solution)/shard_map/ppermute | solution.py:194
  101.9 20.3 %collective-permute-start.10 = (f32[4,56,512]{2,1,0:T(8,128)S(1)}, f32[4,56,512]{2,1,0:T(8,128)S(1)}, u32[]{:S(2)}, u32[]{:S(2)}) collective-permute-start(f32[4,56,512]{2,1,0:T(8,128)S(1)} %slice.54), channel_id=1, source_target_pairs={{0,8},{1,9},{2,10},{3,11},{4,12},{5,13},{6,14},{7,15},{8,0},{9,1},... | collective-permute-start | bytes 1376264 | tf_op jit(solution)/shard_map/ppermute | solution.py:194
  123.5 15.1 %collective-permute-start.14 = (f32[4,64,512]{2,1,0:T(8,128)}, f32[4,64,512]{2,1,0:T(8,128)}, u32[]{:S(2)}, u32[]{:S(2)}) collective-permute-start(f32[4,64,512]{2,1,0:T(8,128)} %get-tuple-element.94), channel_id=1, source_target_pairs={{0,8},{1,9},{2,10},{3,11},{4,12},{5,13},{6,14},{7,15},{8,0},{9,1},... | collective-permute-start | bytes 1572872 | tf_op jit(solution)/shard_map/ppermute | solution.py:194
  124.7 25.5 %collective-permute-start.15 = (f32[4,64,512]{2,1,0:T(8,128)}, f32[4,64,512]{2,1,0:T(8,128)}, u32[]{:S(2)}, u32[]{:S(2)}) collective-permute-start(f32[4,64,512]{2,1,0:T(8,128)} %get-tuple-element.95), channel_id=1, source_target_pairs={{0,16},{1,17},{2,18},{3,19},{4,20},{5,21},{6,22},{7,23},{8,24},{9,... | collective-permute-start | bytes 1572872 | tf_op jit(solution)/shard_map/ppermute | solution.py:194
  125.7 24.5 %collective-permute-start.16 = (f32[4,64,512]{2,1,0:T(8,128)}, f32[4,64,512]{2,1,0:T(8,128)}, u32[]{:S(2)}, u32[]{:S(2)}) collective-permute-start(f32[4,64,512]{2,1,0:T(8,128)} %get-tuple-element.96), channel_id=1, source_target_pairs={{0,24},{1,25},{2,26},{3,27},{4,28},{5,29},{6,30},{7,31},{8,16},{9,... | collective-permute-start | bytes 1572872 | tf_op jit(solution)/shard_map/ppermute | solution.py:194
  127.1 27.6 %collective-permute-start.22 = (f32[256,512]{1,0:T(8,128)}, f32[256,512]{1,0:T(8,128)S(1)}, u32[]{:S(2)}, u32[]{:S(2)}) collective-permute-start(f32[256,512]{1,0:T(8,128)} %get-tuple-element.124), channel_id=1, source_target_pairs={{0,2},{1,3},{2,0},{3,1},{4,6},{5,7},{6,4},{7,5},{8,10},{9,11},{10,... | collective-permute-start | bytes 1572872 | tf_op jit(solution)/shard_map/ppermute | solution.py:194
  130.8 23.9 %collective-permute-start.21 = (f32[256,512]{1,0:T(8,128)S(1)}, f32[256,512]{1,0:T(8,128)S(1)}, u32[]{:S(2)}, u32[]{:S(2)}) collective-permute-start(f32[256,512]{1,0:T(8,128)S(1)} %get-tuple-element.127), channel_id=1, source_target_pairs={{2,6},{3,7},{4,0},{5,1},{10,14},{11,15},{12,8},{13,9},{18,22},{19,... | collective-permute-start | bytes 1572872 | tf_op jit(solution)/shard_map/ppermute | solution.py:194
  138.6 16.2 %collective-permute-start.20 = (f32[256,512]{1,0:T(8,128)S(1)}, f32[256,512]{1,0:T(8,128)S(1)}, u32[]{:S(2)}, u32[]{:S(2)}) collective-permute-start(f32[256,512]{1,0:T(8,128)S(1)} %get-tuple-element.128), channel_id=1, source_target_pairs={{2,4},{3,5},{4,2},{5,3},{10,12},{11,13},{12,10},{13,11},{18,20},{1... | collective-permute-start | bytes 1572872 | tf_op jit(solution)/shard_map/ppermute | solution.py:194
  151.8 15.1 %collective-permute-start.19 = (f32[4,32,512]{2,1,0:T(8,128)S(1)}, f32[4,32,512]{2,1,0:T(8,128)S(1)}, u32[]{:S(2)}, u32[]{:S(2)}) collective-permute-start(f32[4,32,512]{2,1,0:T(8,128)S(1)} %get-tuple-element.132), channel_id=1, source_target_pairs={{0,1},{1,9},{2,21},{3,29},{4,2},{5,10},{6,22},{7,30},{8,3},{9,11},... | collective-permute-start | bytes 786440 | tf_op jit(solution)/shard_map/ppermute | solution.py:194
  153.8 13.1 %collective-permute-start.18 = (f32[4,32,512]{2,1,0:T(8,128)S(1)}, f32[4,32,512]{2,1,0:T(8,128)S(1)}, u32[]{:S(2)}, u32[]{:S(2)}) collective-permute-start(f32[4,32,512]{2,1,0:T(8,128)S(1)} %get-tuple-element.133), channel_id=1, source_target_pairs={{0,0},{1,8},{2,20},{3,28},{4,3},{5,11},{6,23},{7,31},{8,2},{9,10},... | collective-permute-start | bytes 786440 | tf_op jit(solution)/shard_map/ppermute | solution.py:194
  183.8 11.9 %collective-permute-start.24 = (f32[7,4,8,256]{3,2,1,0:T(8,128)S(1)}, f32[7,4,8,256]{3,2,1,0:T(8,128)S(1)}, u32[]{:S(2)}, u32[]{:S(2)}) collective-permute-start(f32[7,4,8,256]{3,2,1,0:T(8,128)S(1)} %get-tuple-element.129), channel_id=1, source_target_pairs={{0,8},{1,9},{2,10},{3,11},{4,12},{5,13},{6,14},{7,15},{8,0},{9,1},... | collective-permute-start | bytes 688136 | tf_op jit(solution)/shard_map/ppermute | solution.py:194
  183.8 12.8 %collective-permute-start.26 = (f32[7,4,8,256]{3,2,1,0:T(8,128)S(1)}, f32[7,4,8,256]{3,2,1,0:T(8,128)S(1)}, u32[]{:S(2)}, u32[]{:S(2)}) collective-permute-start(f32[7,4,8,256]{3,2,1,0:T(8,128)S(1)} %get-tuple-element.130), channel_id=1, source_target_pairs={{0,24},{1,25},{2,26},{3,27},{4,28},{5,29},{6,30},{7,31},{8,16},{9,... | collective-permute-start | bytes 688136 | tf_op jit(solution)/shard_map/ppermute | solution.py:194
  185.8 12.2 %collective-permute-start.25 = (f32[7,4,8,256]{3,2,1,0:T(8,128)S(1)}, f32[7,4,8,256]{3,2,1,0:T(8,128)S(1)}, u32[]{:S(2)}, u32[]{:S(2)}) collective-permute-start(f32[7,4,8,256]{3,2,1,0:T(8,128)S(1)} %get-tuple-element.131), channel_id=1, source_target_pairs={{0,16},{1,17},{2,18},{3,19},{4,20},{5,21},{6,22},{7,23},{8,24},{9,... | collective-permute-start | bytes 688136 | tf_op jit(solution)/shard_map/ppermute | solution.py:194
  (29 other events, 265.1 us)
